TPU v7x, 128 devices: a whole 4x4x4 slice. The times are simulated.
128 devices in a mesh: row: 8 (over x, y_hi), col: 16 (over y_lo, z, core).
Axes of the slice: x: 4, y: 4 (y_hi: 2, y_lo: 2; y = y_hi * 2 + y_lo), z: 4, core: 2. Of those that a mesh axis runs over, the one named last changes fastest.
Arguments:
- feat_rows: float32 [8192, 512], P(('row', 'col')), may hold values from -0.6 to 0.6
- feat_cols: float32 [8192, 512], P(('col', 'row')), may hold values from -0.6 to 0.6
- panel_rows: float32 [8192, 1024], P(('row', 'col')), may hold values from -0.6 to 0.6
- panel_cols: float32 [8192, 1024], P(('col', 'row')), may hold values from -0.6 to 0.6
- accumulator: float32 [8192, 8192], P('row', 'col'), may hold values from -1.8 to 1.8
Outputs:
- acc_new: float32 [8192, 8192], P('row', 'col')
- grad_rows: float32 [8192, 512], P(('row', 'col'))
- grad_cols: float32 [8192, 512], P(('col', 'row'))
All inputs are finite; a program needn't handle non-finite values.
Results may differ from a plain program's by a relative error of at most 0.00011.
Values sent between devices are 32-bit elements; how exact they have to be, the bound alone decides.
No kernel may reach another device: no remote copies, remote signals or barrier semaphores. Data moves between devices by JAX's collectives and lax.ppermute only.
A program may use at most 64 MiB of HBM per device.

v0:
```python
import jax
import jax.numpy as jnp
from jax import lax
from jax.sharding import PartitionSpec as P

decay_rate = 0.125
grad_scale = 0.25


def local_tile(rows_feat, rows_panel, acc_tile, cols_feat, cols_panel):
    grams_tile = acc_tile + jnp.dot(rows_panel, cols_panel.T, precision=lax.Precision.HIGHEST)
    cross_term = jnp.dot(rows_feat, cols_feat.T, precision=lax.Precision.HIGHEST)
    norm_rows = jnp.sum(rows_feat * rows_feat, axis=1)
    norm_cols = jnp.sum(cols_feat * cols_feat, axis=1)
    dist_sq = norm_rows[:, None] + norm_cols[None, :] - 2.0 * cross_term
    kernel = jnp.exp(-decay_rate * dist_sq)
    weights = grams_tile * kernel
    row_term = grad_scale * (
        jnp.dot(weights, cols_feat, precision=lax.Precision.HIGHEST)
        - jnp.sum(weights, axis=1)[:, None] * rows_feat
    )
    col_term = grad_scale * (
        jnp.dot(weights.T, rows_feat, precision=lax.Precision.HIGHEST)
        - jnp.sum(weights, axis=0)[:, None] * cols_feat
    )
    return (grams_tile, row_term, col_term)


def local(feat_rows, feat_cols, panel_rows, panel_cols, accumulator):
    cols_feat, cols_panel = (
        lax.all_gather(feat_cols, "row", axis=0, tiled=True),
        lax.all_gather(panel_cols, "row", axis=0, tiled=True),
    )
    rows_feat, rows_panel = (
        lax.all_gather(feat_rows, "col", axis=0, tiled=True),
        lax.all_gather(panel_rows, "col", axis=0, tiled=True),
    )
    acc_new, row_term, col_term = local_tile(
        rows_feat, rows_panel, accumulator, cols_feat, cols_panel
    )
    grad_rows = lax.psum_scatter(row_term, "col", scatter_dimension=0, tiled=True)
    grad_cols = lax.psum_scatter(col_term, "row", scatter_dimension=0, tiled=True)
    return (acc_new, grad_rows, grad_cols)


def solution(mesh):
    in_specs = (
        P(("row", "col"), None),
        P(("col", "row"), None),
        P(("row", "col"), None),
        P(("col", "row"), None),
        P("row", "col"),
    )
    out_specs = (P("row", "col"), P(("row", "col"), None), P(("col", "row"), None))
    return jax.shard_map(local, mesh=mesh, in_specs=in_specs, out_specs=out_specs, check_vma=False)
```

profile of v0, /device:TPU:0, one launch (start us, length us, event | category | flops | bytes accessed | tf_op | source)
XLA Modules:
  0.0 354.2 jit_solution(9655624925160414229)
XLA Ops:
  7.2 0.0 all-gather.11.cloned.1.call-start
  7.2 0.7 all-gather.11.cloned.1.call-update
  7.9 0.0 all-gather.9.cloned.1.call-start
  7.9 0.7 all-gather.9.cloned.1.call-update
  8.6 0.0 all-gather.7.cloned.1.call-start
  8.7 0.7 all-gather.7.cloned.1.call-update
  9.4 0.0 all-gather.5.cloned.1.call-start
  9.4 0.5 all-gather.5.cloned.1.call-update
  10.0 0.0 reduce-scatter.5.cloned.1.call-start
  10.0 50.1 %all-gather.11.cloned.1.call-done = f32[512,512]{1,0:T(8,128)} async-done(((f32[64,512]{1,0:T(8,128)}), f32[512,512]{1,0:T(8,128)}) %all-gather.11.cloned.1.call-update) | async-done | bytes 1048592 | tf_op jit(solution)/shard_map/all_gather | solution.py:31
  60.1 1.4 multiply_reduce_fusion.1
  61.5 33.6 %all-gather.9.cloned.1.call-done = f32[1024,512]{1,0:T(8,128)} async-done(((f32[64,512]{1,0:T(8,128)}), f32[1024,512]{1,0:T(8,128)}) %all-gather.9.cloned.1.call-update) | async-done | bytes 2097168 | tf_op jit(solution)/shard_map/all_gather | solution.py:35
  95.1 1.8 multiply_reduce_fusion
  96.9 0.0 copy-start
  97.0 0.0 copy-start.2
  97.0 55.1 %all-gather.7.cloned.1.call-done = f32[512,1024]{1,0:T(8,128)} async-done(((f32[64,1024]{1,0:T(8,128)}), f32[512,1024]{1,0:T(8,128)}) %all-gather.7.cloned.1.call-update) | async-done | bytes 2097168 | tf_op jit(solution)/shard_map/all_gather | solution.py:32
  152.1 37.9 %all-gather.5.cloned.1.call-done = f32[1024,1024]{1,0:T(8,128)} async-done(((f32[64,1024]{1,0:T(8,128)}), f32[1024,1024]{1,0:T(8,128)}) %all-gather.5.cloned.1.call-update) | async-done | bytes 4194320 | tf_op jit(solution)/shard_map/all_gather | solution.py:36
  190.0 9.6 %convolution_add_fusion = f32[1024,512]{1,0:T(8,128)S(1)} fusion(f32[1024,512]{1,0:T(8,128)} %param.9, f32[1024,1024]{1,0:T(8,128)} %all-gather.5.cloned.1.call-done, f32[512,1024]{1,0:T(8,128)} %all-gather.7.cloned.1.call-done), kind=kOutput, calls=%fused_computation.3 | convolution fusion | flops 6442975232 | bytes 10485760 | tf_op jit(solution)/shard_map/dot_general | solution.py:11
  199.6 0.0 copy-done
  199.6 0.0 copy-done.2
  199.6 0.0 copy-start.3
  199.6 4.1 %fusion.1 = (f32[512]{0:T(512)S(1)}, f32[1024]{0:T(1024)S(1)}, f32[1024,512]{1,0:T(8,128)S(1)}) fusion(f32[1024,512]{1,0:T(8,128)S(1)} %convolution_add_fusion, f32[1024,512]{1,0:T(8,128)S(1)} %copy-done, f32[512,512]{1,0:T(8,128)S(1)} %copy-done.2, f32[512]{0:T(512)S(1)} %multiply_reduce_fusion.1, f32[1024]{0:T(1024)S(1)} %multiply_reduce_fusion), kind=kOutput, calls=%fused_computation.7 | convolution fusion | flops 3224893952 | bytes 7352320 | tf_op jit(solution)/shard_map/dot_general | solution.py:12
  203.7 0.0 copy-done.3
  203.7 0.0 copy-start.1
  203.7 1.3 copy-done.1
  205.0 4.6 %fusion = f32[512,512]{1,0:T(8,128)} fusion(f32[1024,512]{1,0:T(8,128)S(1)} %get-tuple-element.5, f32[1024,512]{1,0:T(8,128)S(1)} %copy-done, f32[512,512]{1,0:T(8,128)S(1)} %copy-done.2, f32[512]{0:T(512)S(1)} %get-tuple-element.3), kind=kOutput, calls=%fused_computation.5 | convolution fusion | flops 3222011904 | bytes 6293504 | tf_op jit(solution)/shard_map/dot_general | solution.py:23
  209.7 0.0 reduce-scatter.5.cloned.1.call-update
  209.7 0.2 reduce-scatter.3.cloned.1.call-start
  209.9 6.4 %subtract_multiply_fusion = f32[1024,512]{1,0:T(8,128)} fusion(f32[1024,512]{1,0:T(8,128)S(1)} %copy-done, f32[1024,512]{1,0:T(8,128)} %copy-done.1, f32[512,512]{1,0:T(8,128)S(1)} %copy-done.2, f32[1024]{0:T(1024)S(1)} %get-tuple-element.4), kind=kOutput, calls=%fused_computation | convolution fusion | flops 3222798336 | bytes 7344128 | tf_op jit(solution)/shard_map/dot_general | solution.py:19
  216.3 0.0 reduce-scatter.3.cloned.1.call-update
  216.3 65.4 %reduce-scatter.5.cloned.1.call-done = f32[64,512]{1,0:T(8,128)} async-done(((f32[512,512]{1,0:T(8,128)}), f32[64,512]{1,0:T(8,128)}) %reduce-scatter.5.cloned.1.call-update) | async-done | bytes 131088 | tf_op jit(solution)/shard_map/reduce_scatter | solution.py:42
  281.8 65.6 %reduce-scatter.3.cloned.1.call-done = f32[64,512]{1,0:T(8,128)} async-done(((f32[1024,512]{1,0:T(8,128)}), f32[64,512]{1,0:T(8,128)}) %reduce-scatter.3.cloned.1.call-update) | async-done | bytes 131088 | tf_op jit(solution)/shard_map/reduce_scatter | solution.py:41
Async XLA Ops:
  7.2 53.0 %all-gather.11.cloned.1.call-start = ((), (), s32[]{:S(2)}) async-start(), calls=%async_computation.5 | async-start | bytes 1179648 | tf_op jit(solution)/shard_map/all_gather | solution.py:31
  7.9 87.2 %all-gather.9.cloned.1.call-start = ((), (), s32[]{:S(2)}) async-start(), calls=%async_computation.4 | async-start | bytes 2228224 | tf_op jit(solution)/shard_map/all_gather | solution.py:35
  8.6 143.4 %all-gather.7.cloned.1.call-start = ((), (), s32[]{:S(2)}) async-start(), calls=%async_computation.3 | async-start | bytes 2359296 | tf_op jit(solution)/shard_map/all_gather | solution.py:32
  9.4 180.6 %all-gather.5.cloned.1.call-start = ((), (), s32[]{:S(2)}) async-start(), calls=%async_computation.2 | async-start | bytes 4456448 | tf_op jit(solution)/shard_map/all_gather | solution.py:36
  10.0 271.8 %reduce-scatter.5.cloned.1.call-start = ((), (), s32[]{:S(2)}) async-start(), calls=%async_computation.7 | async-start | bytes 1179648 | tf_op jit(solution)/shard_map/reduce_scatter | solution.py:42
  96.9 102.6 %copy-start = (f32[1024,512]{1,0:T(8,128)S(1)}, f32[1024,512]{1,0:T(8,128)}, u32[]{:S(2)}) copy-start(f32[1024,512]{1,0:T(8,128)} %all-gather.9.cloned.1.call-done) | copy-start | bytes 6291460
  97.0 102.6 %copy-start.2 = (f32[512,512]{1,0:T(8,128)S(1)}, f32[512,512]{1,0:T(8,128)}, u32[]{:S(2)}) copy-start(f32[512,512]{1,0:T(8,128)} %all-gather.11.cloned.1.call-done) | copy-start | bytes 3145732
  199.6 4.1 %copy-start.3 = (f32[1024,512]{1,0:T(8,128)}, f32[1024,512]{1,0:T(8,128)S(1)}, u32[]{:S(2)}) copy-start(f32[1024,512]{1,0:T(8,128)S(1)} %convolution_add_fusion) | copy-start | bytes 6291460
  203.7 1.3 copy-start.1
  209.7 137.7 %reduce-scatter.3.cloned.1.call-start = ((), (), s32[]{:S(2)}) async-start(), calls=%async_computation.6 | async-start | bytes 2228224 | tf_op jit(solution)/shard_map/reduce_scatter | solution.py:41
Sparse Core Ops, SparseCore 0:
  10.3 49.7 all-gather.10
  61.8 33.2 all-gather.8
  97.5 54.5 all-gather.6
  153.6 36.2 all-gather.4
  209.8 71.9 reduce-scatter.4
  284.7 62.6 reduce-scatter.2
where the time goes:
time: 354 us
  waiting for transfers between devices  310 us (88%)
  matrix products  24.7 us (7%)
  between operations  14.2 us (4%)
    reduce_scatter x1, waiting for transfers between devices, local(): lax.psum_scatter(row_term, 'col', scatter_dimension=0, tiled=True)  65.6 us
    reduce_scatter x1, waiting for transfers between devices, local(): lax.psum_scatter(col_term, 'row', scatter_dimension=0, tiled=True)  65.4 us
    all_gather x1, waiting for transfers between devices, local(): lax.all_gather(panel_cols, 'row', axis=0, tiled=True)  55.1 us
    all_gather x1, waiting for transfers between devices, local(): lax.all_gather(feat_cols, 'row', axis=0, tiled=True)  50.1 us
    all_gather x1, waiting for transfers between devices, local(): lax.all_gather(panel_rows, 'col', axis=0, tiled=True)  37.9 us
    all_gather x1, waiting for transfers between devices, local(): lax.all_gather(feat_rows, 'col', axis=0, tiled=True)  33.6 us
    dot_general x1, matrix products, local_tile(): jnp.dot(rows_panel, cols_panel.T, precision=lax.Precision.HIGHEST)  9.63 us
  transfers between devices with their start and end apart: 6, of which 6 were waited for; matrix products, arithmetic and copies ran while one was open for 3% of the time, Pallas kernels for 0%

commit v1 on v0

v1 whole, which is shorter than its diff:
```python
import jax
import jax.numpy as jnp
from jax import lax
from jax.experimental import pallas as pl
from jax.experimental.pallas import tpu as pltpu
from jax.sharding import PartitionSpec as P

decay_rate = 0.125
grad_scale = 0.25

B = 64
F = 512
K = 1024
STEPS = 4
ROWS = 1024
COLS = 512
CHUNK = ROWS // STEPS
SHIFTS = (0, 1, 3, 2)


def col_perm(dy, dz, dc):
    return [(q, (((q // 8) ^ dy) * 8) + (((q // 2 + dz) % 4) * 2) + ((q % 2) ^ dc)) for q in range(16)]


def row_perm(dx, dh):
    return [(r, ((r // 2 + dx) % 4) * 2 + ((r % 2) ^ dh)) for r in range(8)]


def over_col(a, dy=0, dz=0, dc=0):
    return lax.ppermute(a, "col", col_perm(dy, dz, dc))


def over_row(a, dx=0, dh=0):
    return lax.ppermute(a, "row", row_perm(dx, dh))


def split(a):
    hi = a.astype(jnp.bfloat16)
    return hi, (a - hi.astype(jnp.float32)).astype(jnp.bfloat16)


def dot3(ah, al, bh, bl, dims):
    def one(p, q):
        return lax.dot_general(p, q, (dims, ((), ())), preferred_element_type=jnp.float32)

    return one(ah, bh) + (one(ah, bl) + one(al, bh))


NT = ((1,), (1,))
NN = ((1,), (0,))
TN = ((0,), (0,))


def tile_kernel(place, *refs):
    rows = refs[:16]
    cols = refs[16:24]
    acc = refs[24]
    acc_new = refs[25]
    own_out = refs[26:30]
    sib_out = refs[30]
    col_out = refs[31:35]
    rh, rl, rf, ch, cl, cf, nr, nc, row_term, col_term, tsum = refs[35:]
    step = pl.program_id(0)

    @pl.when(step == 0)
    def _():
        for n in range(16):
            at = pl.ds(pl.multiple_of(place[n] * B, B), B)
            piece = rows[n][...]
            hi, lo = split(piece)
            rh[at, :] = hi
            rl[at, :] = lo
            feat = piece[:, :F]
            rf[at, :] = feat
            nr[at, :] = jnp.broadcast_to(jnp.sum(feat * feat, axis=1, keepdims=True), (B, 128))
        for n in range(8):
            at = pl.ds(pl.multiple_of(place[16 + n] * B, B), B)
            piece = cols[n][...]
            hi, lo = split(piece)
            ch[at, :] = hi
            cl[at, :] = lo
            feat = piece[:, :F]
            cf[at, :] = feat
            nc[at, :] = jnp.broadcast_to(jnp.sum(feat * feat, axis=1, keepdims=True), (B, 128))
        col_term[...] = jnp.zeros_like(col_term)
        tsum[...] = jnp.zeros_like(tsum)

    at = pl.ds(pl.multiple_of(step * CHUNK, CHUNK), CHUNK)
    rhc, rlc = rh[at, :], rl[at, :]
    chh, cll = ch[...], cl[...]
    grams = acc[...] + dot3(rhc[:, F:], rlc[:, F:], chh[:, F:], cll[:, F:], NT)
    acc_new[...] = grams
    cross = dot3(rhc[:, :F], rlc[:, :F], chh[:, :F], cll[:, :F], NT)
    nc_row = nc[...].T[0:1, :]
    dist_sq = nr[at, :][:, 0:1] + nc_row - 2.0 * cross
    weights = grams * jnp.exp(-decay_rate * dist_sq)
    wh, wl = split(weights)
    s = jnp.sum(weights, axis=1, keepdims=True)
    row_term[at, :] = grad_scale * (dot3(wh, wl, chh[:, :F], cll[:, :F], NN) - s * rf[at, :])
    col_term[...] += dot3(wh, wl, rhc[:, :F], rlc[:, :F], TN)
    tsum[...] += jnp.broadcast_to(jnp.sum(weights, axis=0, keepdims=True), (8, COLS))

    @pl.when(step == STEPS - 1)
    def _():
        for n in range(4):
            for d in range(2):
                own_out[n][d] = row_term[pl.ds(pl.multiple_of(place[24 + n * 2 + d] * B, B), B), :]
                sib_out[n * 2 + d] = row_term[pl.ds(pl.multiple_of(place[32 + n * 2 + d] * B, B), B), :]
        t = jnp.broadcast_to(tsum[0:1, :], (128, COLS)).T[:, 0:1]
        col_term[...] = grad_scale * (col_term[...] - t * cf[...])
        for n in range(4):
            for d in range(2):
                col_out[n][d] = col_term[pl.ds(pl.multiple_of(place[40 + n * 2 + d] * B, B), B), :]


def tile(place, rows, cols, accumulator):
    f32, bf16 = jnp.float32, jnp.bfloat16
    whole = pl.BlockSpec(memory_space=pltpu.VMEM)
    block = pl.BlockSpec((CHUNK, COLS), lambda i, place: (i, 0))
    pair = jax.ShapeDtypeStruct((2, B, F), f32)
    return pl.pallas_call(
        tile_kernel,
        out_shape=[jax.ShapeDtypeStruct((ROWS, COLS), f32)]
        + [pair] * 4
        + [jax.ShapeDtypeStruct((8, B, F), f32)]
        + [pair] * 4,
        grid_spec=pltpu.PrefetchScalarGridSpec(
            num_scalar_prefetch=1,
            grid=(STEPS,),
            in_specs=[whole] * 24 + [block],
            out_specs=[block] + [whole] * 9,
            scratch_shapes=[
                pltpu.VMEM((ROWS, F + K), bf16),
                pltpu.VMEM((ROWS, F + K), bf16),
                pltpu.VMEM((ROWS, F), f32),
                pltpu.VMEM((COLS, F + K), bf16),
                pltpu.VMEM((COLS, F + K), bf16),
                pltpu.VMEM((COLS, F), f32),
                pltpu.VMEM((ROWS, 128), f32),
                pltpu.VMEM((COLS, 128), f32),
                pltpu.VMEM((ROWS, F), f32),
                pltpu.VMEM((COLS, F), f32),
                pltpu.VMEM((8, COLS), f32),
            ],
        ),
        compiler_params=pltpu.CompilerParams(vmem_limit_bytes=46 * 1024 * 1024),
        cost_estimate=pl.CostEstimate(flops=8_000_000_000, bytes_accessed=20_000_000, transcendentals=524288),
        name="tile",
    )(place, *rows, *cols, accumulator)


def local(feat_rows, feat_cols, panel_rows, panel_cols, accumulator):
    q, r = lax.axis_index("col"), lax.axis_index("row")
    y, z, c = q // 8, (q // 2) % 4, q % 2
    x, h = r // 2, r % 2

    def row_at(dy, dz, dc):
        return (y ^ dy) * 8 + ((z + dz) % 4) * 2 + (c ^ dc)

    def col_at(dx, dh):
        return ((x + dx) % 4) * 2 + (h ^ dh)

    own_r = jnp.concatenate([feat_rows, panel_rows], axis=1)
    own_c = jnp.concatenate([feat_cols, panel_cols], axis=1)
    far_r = over_col(own_r, dy=1)
    far_c = over_row(own_c, dh=1)
    rows, cols = [], []
    for a_r, a_c in ((own_r, own_c), (far_r, far_c)):
        rows += [a_r] + [over_col(a_r, dz=-d) for d in SHIFTS[1:]]
        cols += [a_c] + [over_row(a_c, dx=-d) for d in SHIFTS[1:]]
    rows += [over_col(a, dc=1) for a in rows]
    place = jnp.stack(
        [row_at(dy, d, dc) for dc in range(2) for dy in range(2) for d in SHIFTS]
        + [col_at(d, dh) for dh in range(2) for d in SHIFTS]
        + [row_at(dy, d, dc) for dc in range(2) for d in SHIFTS for dy in range(2)]
        + [col_at(d, dh) for d in SHIFTS for dh in range(2)]
    ).astype(jnp.int32)
    out = tile(place, rows, cols, accumulator)
    acc_new, own, sib, col = out[0], out[1:5], out[5], out[6:10]
    sib = over_col(sib, dc=1)
    own = [a + sib[2 * n : 2 * n + 2] for n, a in enumerate(own)]
    row_sum, col_sum = own[0], col[0]
    for n in range(1, 4):
        row_sum = row_sum + over_col(own[n], dz=SHIFTS[n])
        col_sum = col_sum + over_row(col[n], dx=SHIFTS[n])
    grad_rows = row_sum[0] + over_col(row_sum[1], dy=1)
    grad_cols = col_sum[0] + over_row(col_sum[1], dh=1)
    return (acc_new, grad_rows, grad_cols)


def solution(mesh):
    in_specs = (
        P(("row", "col"), None),
        P(("col", "row"), None),
        P(("row", "col"), None),
        P(("col", "row"), None),
        P("row", "col"),
    )
    out_specs = (P("row", "col"), P(("row", "col"), None), P(("col", "row"), None))
    return jax.shard_map(local, mesh=mesh, in_specs=in_specs, out_specs=out_specs, check_vma=False)
```

time: 354 us -> 113 us (0.32)
  waiting for transfers between devices: 310 us -> 45 us
  starting transfers between devices: 0.41 us -> 42.4 us
  matrix products: 24.7 us -> 0 us
  Pallas kernels: 0 us -> 17.2 us
  between operations: 14.2 us -> 1 us
  local copies, waits for them, and re-layouts: 1.35 us -> 5.68 us
    all_gather x4 -> x0, waiting for transfers between devices: 177 us -> none  [the longest x1 55.1 us: local(): lax.all_gather(panel_cols, 'row', axis=0, tiled=True)]
    reduce_scatter x2 -> x0, waiting for transfers between devices: 131 us -> none  [the longest x1 65.6 us: local(): lax.psum_scatter(row_term, 'col', scatter_dimension=0, tiled=True)]
    ppermute x0 -> x31, waiting for transfers between devices: none -> 45 us  [the longest x11 23.4 us: over_row(): return lax.ppermute(a, 'row', row_perm(dx, dh))]
    ppermute x0 -> x31, starting transfers between devices: none -> 42.4 us  [the longest x20 24.1 us: over_col(): return lax.ppermute(a, 'col', col_perm(dy, dz, dc))]
    dot_general x4 -> x0, matrix products: 24.7 us -> none  [the longest x1 9.63 us: local_tile(): jnp.dot(rows_panel, cols_panel.T, precision=lax.Precision.HIGHEST)]
    pallas_call x0 -> x1, Pallas kernels: none -> 17.2 us  [tile(): pl.pallas_call(tile_kernel, out_shape=[jax.ShapeDtypeStruct((ROWS, COLS),...]
  transfers between devices with their start and end apart: 6 -> 31, of which waited for: 6 -> 15; matrix products, arithmetic and copies ran while one was open for 3% -> 3% of each run, Pallas kernels for 0% -> 0%
where the time goes in v1:
time: 113 us
  waiting for transfers between devices  45 us (40%)
  starting transfers between devices  42.4 us (38%)
  Pallas kernels  17.2 us (15%)
  local copies, waits for them, and re-layouts  5.68 us (5%)
  other arithmetic  1.68 us (1%)
    ppermute x20, starting transfers between devices, over_col(): return lax.ppermute(a, 'col', col_perm(dy, dz, dc))  24.1 us
    ppermute x11, waiting for transfers between devices, over_row(): return lax.ppermute(a, 'row', row_perm(dx, dh))  23.4 us
    ppermute x20, waiting for transfers between devices, over_col(): return lax.ppermute(a, 'col', col_perm(dy, dz, dc))  21.6 us
    ppermute x11, starting transfers between devices, over_row(): return lax.ppermute(a, 'row', row_perm(dx, dh))  18.3 us
    pallas_call x1, Pallas kernels, tile(): pl.pallas_call(tile_kernel, out_shape=[jax.ShapeDtypeStruct((ROWS, COLS),...  17.2 us
    unnamed x22, local copies, waits for them, and re-layouts  3.59 us
  transfers between devices with their start and end apart: 31, of which 15 were waited for; matrix products, arithmetic and copies ran while one was open for 3% of the time, Pallas kernels for 0%

profile of v1, /device:TPU:0, one launch (start us, length us, event | category | flops | bytes accessed | tf_op | source)
XLA Modules:
  0.0 112.9 jit_solution(15606711011452399554)
XLA Ops:
  0.6 0.9 constant_dynamic-update-slice_fusion.3
  1.5 1.0 constant_dynamic-update-slice_fusion.2.refs_16_
  2.5 3.4 %collective-permute-start.18 = (f32[64,1536]{1,0:T(8,128)S(1)}, f32[64,1536]{1,0:T(8,128)S(1)}, u32[]{:S(2)}, u32[]{:S(2)}) collective-permute-start(f32[64,1536]{1,0:T(8,128)S(1)} %constant_dynamic-update-slice_fusion.2.refs_16_), channel_id=1, source_target_pairs={{0,16},{16,0},{32,48},{48,32},{64,80},{80,64},{96,112},{112,96},{1... | collective-permute-start | bytes 1179656 | tf_op jit(solution)/shard_map/ppermute | solution.py:34
  5.9 3.0 %collective-permute-start.17 = (f32[64,1536]{1,0:T(8,128)S(1)}, f32[64,1536]{1,0:T(8,128)S(1)}, u32[]{:S(2)}, u32[]{:S(2)}) collective-permute-start(f32[64,1536]{1,0:T(8,128)S(1)} %constant_dynamic-update-slice_fusion.2.refs_16_), channel_id=1, source_target_pairs={{0,64},{16,80},{32,96},{48,112},{64,0},{80,16},{96,32},{112,48},{1... | collective-permute-start | bytes 1179656 | tf_op jit(solution)/shard_map/ppermute | solution.py:34
  8.9 0.6 collective-permute-start.16
  9.5 2.6 %collective-permute-start.15 = (f32[64,1536]{1,0:T(8,128)S(1)}, f32[64,1536]{1,0:T(8,128)S(1)}, u32[]{:S(2)}, u32[]{:S(2)}) collective-permute-start(f32[64,1536]{1,0:T(8,128)S(1)} %constant_dynamic-update-slice_fusion.2.refs_16_), channel_id=1, source_target_pairs={{0,96},{16,112},{32,0},{48,16},{64,32},{80,48},{96,64},{112,80},{1... | collective-permute-start | bytes 1179656 | tf_op jit(solution)/shard_map/ppermute | solution.py:34
  12.1 0.9 constant_dynamic-update-slice_fusion.1
  13.1 1.0 constant_dynamic-update-slice_fusion.refs_0_
  14.0 0.1 collective-permute-start.7
  14.1 0.9 collective-permute-done.18.refs_20_
  15.0 1.6 %collective-permute-start.3 = (f32[64,1536]{1,0:T(8,128)S(1)}, f32[64,1536]{1,0:T(8,128)S(1)}, u32[]{:S(2)}, u32[]{:S(2)}) collective-permute-start(f32[64,1536]{1,0:T(8,128)S(1)} %constant_dynamic-update-slice_fusion.refs_0_), channel_id=1, source_target_pairs={{0,8},{1,9},{2,10},{3,11},{4,12},{5,13},{6,14},{7,15},{8,0},{9,1},... | collective-permute-start | bytes 1179656 | tf_op jit(solution)/shard_map/ppermute | solution.py:30
  16.6 2.8 %collective-permute-done.17.refs_19_ = f32[64,1536]{1,0:T(8,128)S(1)} collective-permute-done((f32[64,1536]{1,0:T(8,128)S(1)}, f32[64,1536]{1,0:T(8,128)S(1)}, u32[]{:S(2)}, u32[]{:S(2)}) %collective-permute-start.17) | collective-permute-done | bytes 393248 | tf_op jit(solution)/shard_map/ppermute | solution.py:34
  19.5 3.9 %collective-permute-start.2 = (f32[64,1536]{1,0:T(8,128)S(1)}, f32[64,1536]{1,0:T(8,128)S(1)}, u32[]{:S(2)}, u32[]{:S(2)}) collective-permute-start(f32[64,1536]{1,0:T(8,128)S(1)} %constant_dynamic-update-slice_fusion.refs_0_), channel_id=1, source_target_pairs={{0,4},{1,5},{2,6},{3,7},{4,0},{5,1},{6,2},{7,3},{8,12},{9,13},{10,... | collective-permute-start | bytes 1179656 | tf_op jit(solution)/shard_map/ppermute | solution.py:30
  23.4 3.0 %collective-permute-done.16.refs_18_ = f32[64,1536]{1,0:T(8,128)S(1)} collective-permute-done((f32[64,1536]{1,0:T(8,128)S(1)}, f32[64,1536]{1,0:T(8,128)S(1)}, u32[]{:S(2)}, u32[]{:S(2)}) %collective-permute-start.16) | collective-permute-done | bytes 393248 | tf_op jit(solution)/shard_map/ppermute | solution.py:34
  26.4 1.9 %collective-permute-start.1 = (f32[64,1536]{1,0:T(8,128)S(1)}, f32[64,1536]{1,0:T(8,128)S(1)}, u32[]{:S(2)}, u32[]{:S(2)}) collective-permute-start(f32[64,1536]{1,0:T(8,128)S(1)} %constant_dynamic-update-slice_fusion.refs_0_), channel_id=1, source_target_pairs={{0,2},{1,3},{2,4},{3,5},{4,6},{5,7},{6,0},{7,1},{8,10},{9,11},{10,... | collective-permute-start | bytes 1179656 | tf_op jit(solution)/shard_map/ppermute | solution.py:30
  28.3 0.0 collective-permute-done.15.refs_17_
  28.3 2.2 %collective-permute-start = (f32[64,1536]{1,0:T(8,128)S(1)}, f32[64,1536]{1,0:T(8,128)S(1)}, u32[]{:S(2)}, u32[]{:S(2)}) collective-permute-start(f32[64,1536]{1,0:T(8,128)S(1)} %constant_dynamic-update-slice_fusion.refs_0_), channel_id=1, source_target_pairs={{0,6},{1,7},{2,0},{3,1},{4,2},{5,3},{6,4},{7,5},{8,14},{9,15},{10,... | collective-permute-start | bytes 1179656 | tf_op jit(solution)/shard_map/ppermute | solution.py:30
  30.6 2.1 %collective-permute-start.21 = (f32[64,1536]{1,0:T(8,128)S(1)}, f32[64,1536]{1,0:T(8,128)S(1)}, u32[]{:S(2)}, u32[]{:S(2)}) collective-permute-start(f32[64,1536]{1,0:T(8,128)S(1)} %collective-permute-done.18.refs_20_), channel_id=1, source_target_pairs={{0,64},{16,80},{32,96},{48,112},{64,0},{80,16},{96,32},{112,48},{1... | collective-permute-start | bytes 1179656 | tf_op jit(solution)/shard_map/ppermute | solution.py:34
  32.7 0.0 collective-permute-done.3.refs_4_
  32.7 1.4 %collective-permute-start.20 = (f32[64,1536]{1,0:T(8,128)S(1)}, f32[64,1536]{1,0:T(8,128)S(1)}, u32[]{:S(2)}, u32[]{:S(2)}) collective-permute-start(f32[64,1536]{1,0:T(8,128)S(1)} %collective-permute-done.18.refs_20_), channel_id=1, source_target_pairs={{0,32},{16,48},{32,64},{48,80},{64,96},{80,112},{96,0},{112,16},{1... | collective-permute-start | bytes 1179656 | tf_op jit(solution)/shard_map/ppermute | solution.py:34
  34.1 1.9 %collective-permute-start.19 = (f32[64,1536]{1,0:T(8,128)S(1)}, f32[64,1536]{1,0:T(8,128)S(1)}, u32[]{:S(2)}, u32[]{:S(2)}) collective-permute-start(f32[64,1536]{1,0:T(8,128)S(1)} %collective-permute-done.18.refs_20_), channel_id=1, source_target_pairs={{0,96},{16,112},{32,0},{48,16},{64,32},{80,48},{96,64},{112,80},{1... | collective-permute-start | bytes 1179656 | tf_op jit(solution)/shard_map/ppermute | solution.py:34
  35.9 3.8 %collective-permute-done.1.refs_2_ = f32[64,1536]{1,0:T(8,128)S(1)} collective-permute-done((f32[64,1536]{1,0:T(8,128)S(1)}, f32[64,1536]{1,0:T(8,128)S(1)}, u32[]{:S(2)}, u32[]{:S(2)}) %collective-permute-start.1) | collective-permute-done | bytes 393248 | tf_op jit(solution)/shard_map/ppermute | solution.py:30
  39.7 2.9 %collective-permute-start.6 = (f32[64,1536]{1,0:T(8,128)S(1)}, f32[64,1536]{1,0:T(8,128)S(1)}, u32[]{:S(2)}, u32[]{:S(2)}) collective-permute-start(f32[64,1536]{1,0:T(8,128)S(1)} %collective-permute-done.3.refs_4_), channel_id=1, source_target_pairs={{0,4},{1,5},{2,6},{3,7},{4,0},{5,1},{6,2},{7,3},{8,12},{9,13},{10,... | collective-permute-start | bytes 1179656 | tf_op jit(solution)/shard_map/ppermute | solution.py:30
  42.7 1.5 %collective-permute-done.21.refs_23_ = f32[64,1536]{1,0:T(8,128)S(1)} collective-permute-done((f32[64,1536]{1,0:T(8,128)S(1)}, f32[64,1536]{1,0:T(8,128)S(1)}, u32[]{:S(2)}, u32[]{:S(2)}) %collective-permute-start.21) | collective-permute-done | bytes 393248 | tf_op jit(solution)/shard_map/ppermute | solution.py:34
  44.1 0.0 collective-permute-start.5
  44.1 7.1 %collective-permute-done.20.refs_22_ = f32[64,1536]{1,0:T(8,128)S(1)} collective-permute-done((f32[64,1536]{1,0:T(8,128)S(1)}, f32[64,1536]{1,0:T(8,128)S(1)}, u32[]{:S(2)}, u32[]{:S(2)}) %collective-permute-start.20) | collective-permute-done | bytes 393248 | tf_op jit(solution)/shard_map/ppermute | solution.py:34
  51.2 1.7 %collective-permute-start.4 = (f32[64,1536]{1,0:T(8,128)S(1)}, f32[64,1536]{1,0:T(8,128)}, u32[]{:S(2)}, u32[]{:S(2)}) collective-permute-start(f32[64,1536]{1,0:T(8,128)S(1)} %collective-permute-done.3.refs_4_), channel_id=1, source_target_pairs={{0,6},{1,7},{2,0},{3,1},{4,2},{5,3},{6,4},{7,5},{8,14},{9,15},{10,... | collective-permute-start | bytes 1179656 | tf_op jit(solution)/shard_map/ppermute | solution.py:30
  52.9 0.1 collective-permute-start.10
  53.0 0.5 collective-permute-start.9
  53.5 0.0 collective-permute-done.6.refs_7_
  53.5 0.1 collective-permute-start.8
  53.6 7.6 %collective-permute-done.5.refs_6_ = f32[64,1536]{1,0:T(8,128)S(1)} collective-permute-done((f32[64,1536]{1,0:T(8,128)S(1)}, f32[64,1536]{1,0:T(8,128)S(1)}, u32[]{:S(2)}, u32[]{:S(2)}) %collective-permute-start.5) | collective-permute-done | bytes 393248 | tf_op jit(solution)/shard_map/ppermute | solution.py:30
  61.2 0.0 collective-permute-start.14
  61.2 1.1 %collective-permute-done.4.refs_5_ = f32[64,1536]{1,0:T(8,128)} collective-permute-done((f32[64,1536]{1,0:T(8,128)S(1)}, f32[64,1536]{1,0:T(8,128)}, u32[]{:S(2)}, u32[]{:S(2)}) %collective-permute-start.4) | collective-permute-done | bytes 393248 | tf_op jit(solution)/shard_map/ppermute | solution.py:30
  62.4 0.0 collective-permute-start.13
  62.4 0.0 collective-permute-done.10.refs_11_
  62.4 0.0 copy-start
  62.4 0.7 copy-done
  63.1 0.5 collective-permute-start.12
  63.8 0.1 stack.123.place
  64.0 0.0 collective-permute-done.9.refs_10_
  64.0 0.0 collective-permute-done.14.refs_15_
  64.0 0.2 collective-permute-done.13.refs_14_
  64.2 1.1 collective-permute-done.12.refs_13_
  65.3 1.0 copy-done.1
  66.3 17.2 %tile.1 = (f32[1024,512]{1,0:T(8,128)}, f32[2,64,512]{2,1,0:T(8,128)S(1)}, f32[2,64,512]{2,1,0:T(8,128)S(1)}, f32[2,64,512]{2,1,0:T(8,128)S(1)}, f32[2,64,512]{2...) custom-call(s32[48]{0:T(128)S(1)} %stack.123.place, ...), custom_call_target="tpu_custom_call" | custom-call | flops 8000000000 | bytes 20000000 | tf_op jit(solution)/shard_map/tile/pallas_call | solution.py:121
  83.5 0.5 collective-permute-start.22
  84.0 3.2 %collective-permute-start.28 = (f32[2,64,512]{2,1,0:T(8,128)S(1)}, f32[2,64,512]{2,1,0:T(8,128)S(1)}, u32[]{:S(2)}, u32[]{:S(2)}) collective-permute-start(f32[2,64,512]{2,1,0:T(8,128)S(1)} %get-tuple-element.21), channel_id=1, source_target_pairs={{0,96},{16,112},{32,0},{48,16},{64,32},{80,48},{96,64},{112,80},{1... | collective-permute-start | bytes 786440 | tf_op jit(solution)/shard_map/ppermute | solution.py:34
  87.2 0.0 collective-permute-start.29
  87.2 0.1 slice_add_fusion.2
  87.4 1.4 %collective-permute-start.23 = (f32[2,64,512]{2,1,0:T(8,128)S(1)}, f32[2,64,512]{2,1,0:T(8,128)S(1)}, u32[]{:S(2)}, u32[]{:S(2)}) collective-permute-start(f32[2,64,512]{2,1,0:T(8,128)S(1)} %get-tuple-element.23), channel_id=1, source_target_pairs={{0,2},{1,3},{2,4},{3,5},{4,6},{5,7},{6,0},{7,1},{8,10},{9,11},{10,... | collective-permute-start | bytes 786440 | tf_op jit(solution)/shard_map/ppermute | solution.py:30
  88.8 3.0 %collective-permute-start.25 = (f32[2,64,512]{2,1,0:T(8,128)S(1)}, f32[2,64,512]{2,1,0:T(8,128)S(1)}, u32[]{:S(2)}, u32[]{:S(2)}) collective-permute-start(f32[2,64,512]{2,1,0:T(8,128)S(1)} %get-tuple-element.24), channel_id=1, source_target_pairs={{0,4},{1,5},{2,6},{3,7},{4,0},{5,1},{6,2},{7,3},{8,12},{9,13},{10,... | collective-permute-start | bytes 786440 | tf_op jit(solution)/shard_map/ppermute | solution.py:30
  91.8 7.4 %collective-permute-done.27 = f32[2,64,512]{2,1,0:T(8,128)S(1)} collective-permute-done((f32[2,64,512]{2,1,0:T(8,128)S(1)}, f32[2,64,512]{2,1,0:T(8,128)S(1)}, u32[]{:S(2)}, u32[]{:S(2)}) %collective-permute-start.27) | collective-permute-done | bytes 262176 | tf_op jit(solution)/shard_map/ppermute | solution.py:34
  99.2 2.9 %collective-permute-start.24 = (f32[2,64,512]{2,1,0:T(8,128)S(1)}, f32[2,64,512]{2,1,0:T(8,128)S(1)}, u32[]{:S(2)}, u32[]{:S(2)}) collective-permute-start(f32[2,64,512]{2,1,0:T(8,128)S(1)} %get-tuple-element.25), channel_id=1, source_target_pairs={{0,6},{1,7},{2,0},{3,1},{4,2},{5,3},{6,4},{7,5},{8,14},{9,15},{10,... | collective-permute-start | bytes 786440 | tf_op jit(solution)/shard_map/ppermute | solution.py:30
  102.0 0.1 add_add_fusion
  102.1 0.1 collective-permute-start.30
  102.3 1.0 collective-permute-done.25
  103.2 3.9 %collective-permute-done.24 = f32[2,64,512]{2,1,0:T(8,128)S(1)} collective-permute-done((f32[2,64,512]{2,1,0:T(8,128)S(1)}, f32[2,64,512]{2,1,0:T(8,128)S(1)}, u32[]{:S(2)}, u32[]{:S(2)}) %collective-permute-start.24) | collective-permute-done | bytes 262176 | tf_op jit(solution)/shard_map/ppermute | solution.py:30
  107.1 0.1 fusion.2
  107.2 0.8 collective-permute-start.26
  108.0 0.7 collective-permute-done.30
  108.7 0.7 fusion.3
  109.4 2.9 %collective-permute-done.26 = f32[64,512]{1,0:T(8,128)S(1)} collective-permute-done((f32[64,512]{1,0:T(8,128)S(1)}, f32[64,512]{1,0:T(8,128)S(1)}, u32[]{:S(2)}, u32[]{:S(2)}) %collective-permute-start.26) | collective-permute-done | bytes 131104 | tf_op jit(solution)/shard_map/ppermute | solution.py:30
  112.3 0.7 fusion.4
  (31 shorter events, 0.1 us)
Async XLA Ops:
  2.5 59.8 %copy-start.2 = (f32[64,1536]{1,0:T(8,128)}, f32[64,1536]{1,0:T(8,128)S(1)}, u32[]{:S(2)}) copy-start(f32[64,1536]{1,0:T(8,128)S(1)} %constant_dynamic-update-slice_fusion.2.refs_16_) | copy-start | bytes 1179652
  2.5 12.5 %collective-permute-start.18 = (f32[64,1536]{1,0:T(8,128)S(1)}, f32[64,1536]{1,0:T(8,128)S(1)}, u32[]{:S(2)}, u32[]{:S(2)}) collective-permute-start(f32[64,1536]{1,0:T(8,128)S(1)} %constant_dynamic-update-slice_fusion.2.refs_16_), channel_id=1, source_target_pairs={{0,16},{16,0},{32,48},{48,32},{64,80},{80,64},{96,112},{112,96},{1... | collective-permute-start | bytes 1179656 | tf_op jit(solution)/shard_map/ppermute | solution.py:34
  5.9 13.6 %collective-permute-start.17 = (f32[64,1536]{1,0:T(8,128)S(1)}, f32[64,1536]{1,0:T(8,128)S(1)}, u32[]{:S(2)}, u32[]{:S(2)}) collective-permute-start(f32[64,1536]{1,0:T(8,128)S(1)} %constant_dynamic-update-slice_fusion.2.refs_16_), channel_id=1, source_target_pairs={{0,64},{16,80},{32,96},{48,112},{64,0},{80,16},{96,32},{112,48},{1... | collective-permute-start | bytes 1179656 | tf_op jit(solution)/shard_map/ppermute | solution.py:34
  8.9 17.5 %collective-permute-start.16 = (f32[64,1536]{1,0:T(8,128)S(1)}, f32[64,1536]{1,0:T(8,128)S(1)}, u32[]{:S(2)}, u32[]{:S(2)}) collective-permute-start(f32[64,1536]{1,0:T(8,128)S(1)} %constant_dynamic-update-slice_fusion.2.refs_16_), channel_id=1, source_target_pairs={{0,32},{16,48},{32,64},{48,80},{64,96},{80,112},{96,0},{112,16},{1... | collective-permute-start | bytes 1179656 | tf_op jit(solution)/shard_map/ppermute | solution.py:34
  9.5 18.8 %collective-permute-start.15 = (f32[64,1536]{1,0:T(8,128)S(1)}, f32[64,1536]{1,0:T(8,128)S(1)}, u32[]{:S(2)}, u32[]{:S(2)}) collective-permute-start(f32[64,1536]{1,0:T(8,128)S(1)} %constant_dynamic-update-slice_fusion.2.refs_16_), channel_id=1, source_target_pairs={{0,96},{16,112},{32,0},{48,16},{64,32},{80,48},{96,64},{112,80},{1... | collective-permute-start | bytes 1179656 | tf_op jit(solution)/shard_map/ppermute | solution.py:34
  14.0 16.5 %collective-permute-start.7 = (f32[64,1536]{1,0:T(8,128)S(1)}, f32[64,1536]{1,0:T(8,128)S(1)}, u32[]{:S(2)}, u32[]{:S(2)}) collective-permute-start(f32[64,1536]{1,0:T(8,128)S(1)} %constant_dynamic-update-slice_fusion.refs_0_), channel_id=1, source_target_pairs={{0,1},{1,0},{2,3},{3,2},{4,5},{5,4},{6,7},{7,6},{8,9},{9,8},{10,11... | collective-permute-start | bytes 1179656 | tf_op jit(solution)/shard_map/ppermute | solution.py:30
  15.0 48.6 %copy-start.3 = (f32[64,1536]{1,0:T(8,128)}, f32[64,1536]{1,0:T(8,128)S(1)}, u32[]{:S(2)}) copy-start(f32[64,1536]{1,0:T(8,128)S(1)} %collective-permute-done.18.refs_20_) | copy-start | bytes 1179652
  15.0 17.7 %collective-permute-start.3 = (f32[64,1536]{1,0:T(8,128)S(1)}, f32[64,1536]{1,0:T(8,128)S(1)}, u32[]{:S(2)}, u32[]{:S(2)}) collective-permute-start(f32[64,1536]{1,0:T(8,128)S(1)} %constant_dynamic-update-slice_fusion.refs_0_), channel_id=1, source_target_pairs={{0,8},{1,9},{2,10},{3,11},{4,12},{5,13},{6,14},{7,15},{8,0},{9,1},... | collective-permute-start | bytes 1179656 | tf_op jit(solution)/shard_map/ppermute | solution.py:30
  19.5 44.2 %copy-start.4 = (f32[64,1536]{1,0:T(8,128)}, f32[64,1536]{1,0:T(8,128)S(1)}, u32[]{:S(2)}) copy-start(f32[64,1536]{1,0:T(8,128)S(1)} %collective-permute-done.17.refs_19_) | copy-start | bytes 1179652
  19.5 14.6 %collective-permute-start.2 = (f32[64,1536]{1,0:T(8,128)S(1)}, f32[64,1536]{1,0:T(8,128)S(1)}, u32[]{:S(2)}, u32[]{:S(2)}) collective-permute-start(f32[64,1536]{1,0:T(8,128)S(1)} %constant_dynamic-update-slice_fusion.refs_0_), channel_id=1, source_target_pairs={{0,4},{1,5},{2,6},{3,7},{4,0},{5,1},{6,2},{7,3},{8,12},{9,13},{10,... | collective-permute-start | bytes 1179656 | tf_op jit(solution)/shard_map/ppermute | solution.py:30
  26.4 37.2 %copy-start.5 = (f32[64,1536]{1,0:T(8,128)}, f32[64,1536]{1,0:T(8,128)S(1)}, u32[]{:S(2)}) copy-start(f32[64,1536]{1,0:T(8,128)S(1)} %collective-permute-done.16.refs_18_) | copy-start | bytes 1179652
  26.4 13.3 %collective-permute-start.1 = (f32[64,1536]{1,0:T(8,128)S(1)}, f32[64,1536]{1,0:T(8,128)S(1)}, u32[]{:S(2)}, u32[]{:S(2)}) collective-permute-start(f32[64,1536]{1,0:T(8,128)S(1)} %constant_dynamic-update-slice_fusion.refs_0_), channel_id=1, source_target_pairs={{0,2},{1,3},{2,4},{3,5},{4,6},{5,7},{6,0},{7,1},{8,10},{9,11},{10,... | collective-permute-start | bytes 1179656 | tf_op jit(solution)/shard_map/ppermute | solution.py:30
  28.3 35.3 %copy-start.6 = (f32[64,1536]{1,0:T(8,128)}, f32[64,1536]{1,0:T(8,128)S(1)}, u32[]{:S(2)}) copy-start(f32[64,1536]{1,0:T(8,128)S(1)} %collective-permute-done.15.refs_17_) | copy-start | bytes 1179652
  28.3 11.4 %collective-permute-start = (f32[64,1536]{1,0:T(8,128)S(1)}, f32[64,1536]{1,0:T(8,128)S(1)}, u32[]{:S(2)}, u32[]{:S(2)}) collective-permute-start(f32[64,1536]{1,0:T(8,128)S(1)} %constant_dynamic-update-slice_fusion.refs_0_), channel_id=1, source_target_pairs={{0,6},{1,7},{2,0},{3,1},{4,2},{5,3},{6,4},{7,5},{8,14},{9,15},{10,... | collective-permute-start | bytes 1179656 | tf_op jit(solution)/shard_map/ppermute | solution.py:30
  30.6 13.6 %collective-permute-start.21 = (f32[64,1536]{1,0:T(8,128)S(1)}, f32[64,1536]{1,0:T(8,128)S(1)}, u32[]{:S(2)}, u32[]{:S(2)}) collective-permute-start(f32[64,1536]{1,0:T(8,128)S(1)} %collective-permute-done.18.refs_20_), channel_id=1, source_target_pairs={{0,64},{16,80},{32,96},{48,112},{64,0},{80,16},{96,32},{112,48},{1... | collective-permute-start | bytes 1179656 | tf_op jit(solution)/shard_map/ppermute | solution.py:34
  32.7 18.5 %collective-permute-start.20 = (f32[64,1536]{1,0:T(8,128)S(1)}, f32[64,1536]{1,0:T(8,128)S(1)}, u32[]{:S(2)}, u32[]{:S(2)}) collective-permute-start(f32[64,1536]{1,0:T(8,128)S(1)} %collective-permute-done.18.refs_20_), channel_id=1, source_target_pairs={{0,32},{16,48},{32,64},{48,80},{64,96},{80,112},{96,0},{112,16},{1... | collective-permute-start | bytes 1179656 | tf_op jit(solution)/shard_map/ppermute | solution.py:34
  34.1 18.8 %collective-permute-start.19 = (f32[64,1536]{1,0:T(8,128)S(1)}, f32[64,1536]{1,0:T(8,128)S(1)}, u32[]{:S(2)}, u32[]{:S(2)}) collective-permute-start(f32[64,1536]{1,0:T(8,128)S(1)} %collective-permute-done.18.refs_20_), channel_id=1, source_target_pairs={{0,96},{16,112},{32,0},{48,16},{64,32},{80,48},{96,64},{112,80},{1... | collective-permute-start | bytes 1179656 | tf_op jit(solution)/shard_map/ppermute | solution.py:34
  39.7 13.3 %collective-permute-start.11 = (f32[64,1536]{1,0:T(8,128)S(1)}, f32[64,1536]{1,0:T(8,128)S(1)}, u32[]{:S(2)}, u32[]{:S(2)}) collective-permute-start(f32[64,1536]{1,0:T(8,128)S(1)} %collective-permute-done.3.refs_4_), channel_id=1, source_target_pairs={{0,1},{1,0},{2,3},{3,2},{4,5},{5,4},{6,7},{7,6},{8,9},{9,8},{10,11... | collective-permute-start | bytes 1179656 | tf_op jit(solution)/shard_map/ppermute | solution.py:30
  39.7 13.7 %collective-permute-start.6 = (f32[64,1536]{1,0:T(8,128)S(1)}, f32[64,1536]{1,0:T(8,128)S(1)}, u32[]{:S(2)}, u32[]{:S(2)}) collective-permute-start(f32[64,1536]{1,0:T(8,128)S(1)} %collective-permute-done.3.refs_4_), channel_id=1, source_target_pairs={{0,4},{1,5},{2,6},{3,7},{4,0},{5,1},{6,2},{7,3},{8,12},{9,13},{10,... | collective-permute-start | bytes 1179656 | tf_op jit(solution)/shard_map/ppermute | solution.py:30
  44.1 8.7 %copy-start.7 = (f32[64,1536]{1,0:T(8,128)}, f32[64,1536]{1,0:T(8,128)S(1)}, u32[]{:S(2)}) copy-start(f32[64,1536]{1,0:T(8,128)S(1)} %collective-permute-done.21.refs_23_) | copy-start | bytes 1179652
  44.1 17.0 %collective-permute-start.5 = (f32[64,1536]{1,0:T(8,128)S(1)}, f32[64,1536]{1,0:T(8,128)S(1)}, u32[]{:S(2)}, u32[]{:S(2)}) collective-permute-start(f32[64,1536]{1,0:T(8,128)S(1)} %collective-permute-done.3.refs_4_), channel_id=1, source_target_pairs={{0,2},{1,3},{2,4},{3,5},{4,6},{5,7},{6,0},{7,1},{8,10},{9,11},{10,... | collective-permute-start | bytes 1179656 | tf_op jit(solution)/shard_map/ppermute | solution.py:30
  51.2 12.4 %copy-start.8 = (f32[64,1536]{1,0:T(8,128)}, f32[64,1536]{1,0:T(8,128)S(1)}, u32[]{:S(2)}) copy-start(f32[64,1536]{1,0:T(8,128)S(1)} %collective-permute-done.20.refs_22_) | copy-start | bytes 1179652
  51.2 11.1 %collective-permute-start.4 = (f32[64,1536]{1,0:T(8,128)S(1)}, f32[64,1536]{1,0:T(8,128)}, u32[]{:S(2)}, u32[]{:S(2)}) collective-permute-start(f32[64,1536]{1,0:T(8,128)S(1)} %collective-permute-done.3.refs_4_), channel_id=1, source_target_pairs={{0,6},{1,7},{2,0},{3,1},{4,2},{5,3},{6,4},{7,5},{8,14},{9,15},{10,... | collective-permute-start | bytes 1179656 | tf_op jit(solution)/shard_map/ppermute | solution.py:30
  52.9 10.8 %copy-start.9 = (f32[64,1536]{1,0:T(8,128)}, f32[64,1536]{1,0:T(8,128)S(1)}, u32[]{:S(2)}) copy-start(f32[64,1536]{1,0:T(8,128)S(1)} %collective-permute-done.19.refs_21_) | copy-start | bytes 1179652
  52.9 9.5 %collective-permute-start.10 = (f32[64,1536]{1,0:T(8,128)S(1)}, f32[64,1536]{1,0:T(8,128)S(1)}, u32[]{:S(2)}, u32[]{:S(2)}) collective-permute-start(f32[64,1536]{1,0:T(8,128)S(1)} %collective-permute-done.2.refs_3_), channel_id=1, source_target_pairs={{0,1},{1,0},{2,3},{3,2},{4,5},{5,4},{6,7},{7,6},{8,9},{9,8},{10,11... | collective-permute-start | bytes 1179656 | tf_op jit(solution)/shard_map/ppermute | solution.py:30
  53.0 11.0 %collective-permute-start.9 = (f32[64,1536]{1,0:T(8,128)S(1)}, f32[64,1536]{1,0:T(8,128)}, u32[]{:S(2)}, u32[]{:S(2)}) collective-permute-start(f32[64,1536]{1,0:T(8,128)S(1)} %collective-permute-done.1.refs_2_), channel_id=1, source_target_pairs={{0,1},{1,0},{2,3},{3,2},{4,5},{5,4},{6,7},{7,6},{8,9},{9,8},{10,11... | collective-permute-start | bytes 1179656 | tf_op jit(solution)/shard_map/ppermute | solution.py:30
  53.5 10.5 %collective-permute-start.8 = (f32[64,1536]{1,0:T(8,128)S(1)}, f32[64,1536]{1,0:T(8,128)}, u32[]{:S(2)}, u32[]{:S(2)}) collective-permute-start(f32[64,1536]{1,0:T(8,128)S(1)} %collective-permute-done.refs_1_), channel_id=1, source_target_pairs={{0,1},{1,0},{2,3},{3,2},{4,5},{5,4},{6,7},{7,6},{8,9},{9,8},{10,11... | collective-permute-start | bytes 1179656 | tf_op jit(solution)/shard_map/ppermute | solution.py:30
  61.2 2.8 %collective-permute-start.14 = (f32[64,1536]{1,0:T(8,128)S(1)}, f32[64,1536]{1,0:T(8,128)}, u32[]{:S(2)}, u32[]{:S(2)}) collective-permute-start(f32[64,1536]{1,0:T(8,128)S(1)} %collective-permute-done.6.refs_7_), channel_id=1, source_target_pairs={{0,1},{1,0},{2,3},{3,2},{4,5},{5,4},{6,7},{7,6},{8,9},{9,8},{10,11... | collective-permute-start | bytes 1179656 | tf_op jit(solution)/shard_map/ppermute | solution.py:30
  62.4 1.9 %collective-permute-start.13 = (f32[64,1536]{1,0:T(8,128)S(1)}, f32[64,1536]{1,0:T(8,128)}, u32[]{:S(2)}, u32[]{:S(2)}) collective-permute-start(f32[64,1536]{1,0:T(8,128)S(1)} %collective-permute-done.5.refs_6_), channel_id=1, source_target_pairs={{0,1},{1,0},{2,3},{3,2},{4,5},{5,4},{6,7},{7,6},{8,9},{9,8},{10,11... | collective-permute-start | bytes 1179656 | tf_op jit(solution)/shard_map/ppermute | solution.py:30
  62.4 0.7 copy-start
  63.1 2.2 %collective-permute-start.12 = (f32[64,1536]{1,0:T(8,128)}, f32[64,1536]{1,0:T(8,128)}, u32[]{:S(2)}, u32[]{:S(2)}) collective-permute-start(f32[64,1536]{1,0:T(8,128)} %collective-permute-done.4.refs_5_), channel_id=1, source_target_pairs={{0,1},{1,0},{2,3},{3,2},{4,5},{5,4},{6,7},{7,6},{8,9},{9,8},{10,11... | collective-permute-start | bytes 1179656 | tf_op jit(solution)/shard_map/ppermute | solution.py:30
  65.3 1.0 copy-start.1
  83.5 3.7 %collective-permute-start.22 = (f32[8,64,512]{2,1,0:T(8,128)}, f32[8,64,512]{2,1,0:T(8,128)S(1)}, u32[]{:S(2)}, u32[]{:S(2)}) collective-permute-start(f32[8,64,512]{2,1,0:T(8,128)} %get-tuple-element.15), channel_id=1, source_target_pairs={{0,1},{1,0},{2,3},{3,2},{4,5},{5,4},{6,7},{7,6},{8,9},{9,8},{10,11... | collective-permute-start | bytes 3145736 | tf_op jit(solution)/shard_map/ppermute | solution.py:30
  84.0 15.2 %collective-permute-start.27 = (f32[2,64,512]{2,1,0:T(8,128)S(1)}, f32[2,64,512]{2,1,0:T(8,128)S(1)}, u32[]{:S(2)}, u32[]{:S(2)}) collective-permute-start(f32[2,64,512]{2,1,0:T(8,128)S(1)} %get-tuple-element.20), channel_id=1, source_target_pairs={{0,32},{16,48},{32,64},{48,80},{64,96},{80,112},{96,0},{112,16},{1... | collective-permute-start | bytes 786440 | tf_op jit(solution)/shard_map/ppermute | solution.py:34
  84.0 18.0 %collective-permute-start.28 = (f32[2,64,512]{2,1,0:T(8,128)S(1)}, f32[2,64,512]{2,1,0:T(8,128)S(1)}, u32[]{:S(2)}, u32[]{:S(2)}) collective-permute-start(f32[2,64,512]{2,1,0:T(8,128)S(1)} %get-tuple-element.21), channel_id=1, source_target_pairs={{0,96},{16,112},{32,0},{48,16},{64,32},{80,48},{96,64},{112,80},{1... | collective-permute-start | bytes 786440 | tf_op jit(solution)/shard_map/ppermute | solution.py:34
  87.2 14.8 %collective-permute-start.29 = (f32[2,64,512]{2,1,0:T(8,128)S(1)}, f32[2,64,512]{2,1,0:T(8,128)S(1)}, u32[]{:S(2)}, u32[]{:S(2)}) collective-permute-start(f32[2,64,512]{2,1,0:T(8,128)S(1)} %get-tuple-element.22), channel_id=1, source_target_pairs={{0,64},{16,80},{32,96},{48,112},{64,0},{80,16},{96,32},{112,48},{1... | collective-permute-start | bytes 786440 | tf_op jit(solution)/shard_map/ppermute | solution.py:34
  87.4 14.9 %collective-permute-start.23 = (f32[2,64,512]{2,1,0:T(8,128)S(1)}, f32[2,64,512]{2,1,0:T(8,128)S(1)}, u32[]{:S(2)}, u32[]{:S(2)}) collective-permute-start(f32[2,64,512]{2,1,0:T(8,128)S(1)} %get-tuple-element.23), channel_id=1, source_target_pairs={{0,2},{1,3},{2,4},{3,5},{4,6},{5,7},{6,0},{7,1},{8,10},{9,11},{10,... | collective-permute-start | bytes 786440 | tf_op jit(solution)/shard_map/ppermute | solution.py:30
  88.8 14.4 %collective-permute-start.25 = (f32[2,64,512]{2,1,0:T(8,128)S(1)}, f32[2,64,512]{2,1,0:T(8,128)S(1)}, u32[]{:S(2)}, u32[]{:S(2)}) collective-permute-start(f32[2,64,512]{2,1,0:T(8,128)S(1)} %get-tuple-element.24), channel_id=1, source_target_pairs={{0,4},{1,5},{2,6},{3,7},{4,0},{5,1},{6,2},{7,3},{8,12},{9,13},{10,... | collective-permute-start | bytes 786440 | tf_op jit(solution)/shard_map/ppermute | solution.py:30
  99.2 7.9 %collective-permute-start.24 = (f32[2,64,512]{2,1,0:T(8,128)S(1)}, f32[2,64,512]{2,1,0:T(8,128)S(1)}, u32[]{:S(2)}, u32[]{:S(2)}) collective-permute-start(f32[2,64,512]{2,1,0:T(8,128)S(1)} %get-tuple-element.25), channel_id=1, source_target_pairs={{0,6},{1,7},{2,0},{3,1},{4,2},{5,3},{6,4},{7,5},{8,14},{9,15},{10,... | collective-permute-start | bytes 786440 | tf_op jit(solution)/shard_map/ppermute | solution.py:30
  102.1 6.6 %collective-permute-start.30 = (f32[64,512]{1,0:T(8,128)S(1)}, f32[64,512]{1,0:T(8,128)S(1)}, u32[]{:S(2)}, u32[]{:S(2)}) collective-permute-start(f32[64,512]{1,0:T(8,128)S(1)} %slice_bitcast_fusion), channel_id=1, source_target_pairs={{0,16},{16,0},{32,48},{48,32},{64,80},{80,64},{96,112},{112,96},{1... | collective-permute-start | bytes 393224 | tf_op jit(solution)/shard_map/ppermute | solution.py:34
  107.2 5.0 %collective-permute-start.26 = (f32[64,512]{1,0:T(8,128)S(1)}, f32[64,512]{1,0:T(8,128)S(1)}, u32[]{:S(2)}, u32[]{:S(2)}) collective-permute-start(f32[64,512]{1,0:T(8,128)S(1)} %slice_bitcast_fusion.2), channel_id=1, source_target_pairs={{0,8},{1,9},{2,10},{3,11},{4,12},{5,13},{6,14},{7,15},{8,0},{9,1},... | collective-permute-start | bytes 393224 | tf_op jit(solution)/shard_map/ppermute | solution.py:30

commit v2 on v1

v2 whole, which is shorter than its diff:
```python
import jax
import jax.numpy as jnp
from jax import lax
from jax.experimental import pallas as pl
from jax.experimental.pallas import tpu as pltpu
from jax.sharding import PartitionSpec as P

decay_rate = 0.125
grad_scale = 0.25

B = 64
F = 512
K = 1024
STEPS = 4
ROWS = 1024
COLS = 512
CHUNK = ROWS // STEPS
SHIFTS = (0, 2, 1, 3)


def col_perm(dy, dz, dc):
    return [(q, (((q // 8) ^ dy) * 8) + (((q // 2 + dz) % 4) * 2) + ((q % 2) ^ dc)) for q in range(16)]


def row_perm(dx, dh):
    return [(r, ((r // 2 + dx) % 4) * 2 + ((r % 2) ^ dh)) for r in range(8)]


def over_col(a, dy=0, dz=0, dc=0):
    return lax.ppermute(a, "col", col_perm(dy, dz, dc))


def over_row(a, dx=0, dh=0):
    return lax.ppermute(a, "row", row_perm(dx, dh))


def split(a):
    hi = a.astype(jnp.bfloat16)
    return hi, (a - hi.astype(jnp.float32)).astype(jnp.bfloat16)


def dot3(ah, al, bh, bl, dims):
    def one(p, q):
        return lax.dot_general(p, q, (dims, ((), ())), preferred_element_type=jnp.float32)

    return one(ah, bh) + (one(ah, bl) + one(al, bh))


NT = ((1,), (1,))
NN = ((1,), (0,))
TN = ((0,), (0,))


f32, bf16 = jnp.float32, jnp.bfloat16
whole = pl.BlockSpec(memory_space=pltpu.VMEM)
block = pl.BlockSpec((CHUNK, COLS), lambda i: (i, 0))
W = F + K


def places():
    q, r = lax.axis_index("col"), lax.axis_index("row")
    y, z, c = q // 8, (q // 2) % 4, q % 2
    x, h = r // 2, r % 2

    def row_at(dy, dz, core):
        return (y ^ dy) * 8 + ((z + dz) % 4) * 2 + core

    def col_at(dx, dh):
        return ((x + dx) % 4) * 2 + (h ^ dh)

    return (
        [c]
        + [row_at(dy, d, 0) for dy in range(2) for d in SHIFTS]
        + [col_at(d, dh) for dh in range(2) for d in SHIFTS]
        + [row_at(dy, d, c) for d in SHIFTS for dy in range(2)]
        + [row_at(dy, d, 1 - c) for d in SHIFTS for dy in range(2)]
        + [col_at(d, dh) for d in SHIFTS for dh in range(2)]
    )


def pack_kernel(feat_rows, feat_cols, panel_rows, panel_cols, keep, give):
    def fill(mine, other):
        keep[:B, :F], keep[:B, F:] = mine[0][...], mine[1][...]
        give[:, :F], give[:, F:] = other[0][...], other[1][...]

    rows, cols = (feat_rows, panel_rows), (feat_cols, panel_cols)
    c = lax.axis_index("col") % 2
    pl.when(c == 0)(lambda: fill(rows, cols))
    pl.when(c == 1)(lambda: fill(cols, rows))


def pack(*shards):
    return pl.pallas_call(
        pack_kernel,
        out_shape=[jax.ShapeDtypeStruct((2 * B, W), f32), jax.ShapeDtypeStruct((B, W), f32)],
        in_specs=[whole] * 4,
        out_specs=[whole] * 2,
        compiler_params=pltpu.CompilerParams(vmem_limit_bytes=4 * 1024 * 1024),
        cost_estimate=pl.CostEstimate(flops=0, bytes_accessed=1_600_000, transcendentals=0),
        name="pack",
    )(*shards)


def tile_kernel(*refs):
    place = places()
    native, swapped, acc, acc_new = refs[:8], refs[8:16], refs[16], refs[17]
    own_out, sib_out, col_out = refs[18:22], refs[22], refs[23:27]
    rh, rl, rf, ch, cl, cf, nr, nc, row_term, col_term, tsum = refs[27:]
    step = pl.program_id(0)

    def put(a, at, hi, lo, feat, norm):
        hi[at, :], lo[at, :] = split(a)
        a = a[:, :F]
        feat[at, :] = a
        norm[at, :] = jnp.broadcast_to(jnp.sum(a * a, axis=1, keepdims=True), (a.shape[0], 128))

    @pl.when(step == 0)
    def _():
        def prepare(row_source, col_source, start):
            for n in range(8):
                at = pl.ds(pl.multiple_of(place[1 + n] * B, 2 * B), 2 * B)
                put(row_source[n][...], at, rh, rl, rf, nr)
                at = pl.ds(pl.multiple_of(place[9 + n] * B, B), B)
                put(col_source[n][start : start + B, :], at, ch, cl, cf, nc)

        pl.when(place[0] == 0)(lambda: prepare(native, swapped, B))
        pl.when(place[0] == 1)(lambda: prepare(swapped, native, 0))
        col_term[...] = jnp.zeros_like(col_term)
        tsum[...] = jnp.zeros_like(tsum)

    at = pl.ds(pl.multiple_of(step * CHUNK, CHUNK), CHUNK)
    grams = acc[...] + dot3(rh[at, F:], rl[at, F:], ch[:, F:], cl[:, F:], NT)
    acc_new[...] = grams
    cross = dot3(rh[at, :F], rl[at, :F], ch[:, :F], cl[:, :F], NT)
    nc_row = nc[...].T[0:1, :]
    dist_sq = nr[at, :][:, 0:1] + nc_row - 2.0 * cross
    weights = grams * jnp.exp(-decay_rate * dist_sq)
    wh, wl = split(weights)
    s = jnp.sum(weights, axis=1, keepdims=True)
    row_term[at, :] = grad_scale * (dot3(wh, wl, ch[:, :F], cl[:, :F], NN) - s * rf[at, :])
    col_term[...] += dot3(wh, wl, rh[at, :F], rl[at, :F], TN)
    tsum[...] += jnp.broadcast_to(jnp.sum(weights, axis=0, keepdims=True), (8, COLS))

    @pl.when(step == STEPS - 1)
    def _():
        def take(k, src):
            return src[pl.ds(pl.multiple_of(place[17 + k] * B, B), B), :]

        t = jnp.broadcast_to(tsum[0:1, :], (128, COLS)).T[:, 0:1]
        col_term[...] = grad_scale * (col_term[...] - t * cf[...])
        for n in range(4):
            for d in range(2):
                k = n * 2 + d
                own_out[n][d] = take(k, row_term)
                sib_out[k] = take(8 + k, row_term)
                col_out[n][d] = take(16 + k, col_term)


def tile(native, swapped, accumulator):
    pair = jax.ShapeDtypeStruct((2, B, F), f32)
    return pl.pallas_call(
        tile_kernel,
        out_shape=[jax.ShapeDtypeStruct((ROWS, COLS), f32)]
        + [pair] * 4
        + [jax.ShapeDtypeStruct((8, B, F), f32)]
        + [pair] * 4,
        grid_spec=pl.GridSpec(
            grid=(STEPS,),
            in_specs=[whole] * 16 + [block],
            out_specs=[block] + [whole] * 9,
            scratch_shapes=[
                pltpu.VMEM((ROWS, W), bf16),
                pltpu.VMEM((ROWS, W), bf16),
                pltpu.VMEM((ROWS, F), f32),
                pltpu.VMEM((COLS, W), bf16),
                pltpu.VMEM((COLS, W), bf16),
                pltpu.VMEM((COLS, F), f32),
                pltpu.VMEM((ROWS, 128), f32),
                pltpu.VMEM((COLS, 128), f32),
                pltpu.VMEM((ROWS, F), f32),
                pltpu.VMEM((COLS, F), f32),
                pltpu.VMEM((8, COLS), f32),
            ],
        ),
        compiler_params=pltpu.CompilerParams(vmem_limit_bytes=TILE_VMEM * 1024 * 1024),
        cost_estimate=pl.CostEstimate(flops=8_000_000_000, bytes_accessed=20_000_000, transcendentals=524288),
        name="tile",
    )(*native, *swapped, accumulator)


TILE_VMEM = 36


def both_perm(flip, shift):
    pairs = []
    for r in range(8):
        for q in range(16):
            if q % 2 == 0:
                to = r * 16 + ((q // 8) ^ flip) * 8 + ((q // 2 + shift) % 4) * 2
            else:
                to = (((r // 2 + shift) % 4) * 2 + ((r % 2) ^ flip)) * 16 + q
            pairs.append((r * 16 + q, to))
    return pairs


def over_both(a, flip=0, shift=0):
    return lax.ppermute(a, ("row", "col"), both_perm(flip, shift))


def gather(shards):
    keep, give = pack(*shards)
    own = lax.dynamic_update_slice(keep, over_col(give, dc=1), (B, 0))
    far = over_both(own, flip=1)
    native = []
    for a in (own, far):
        native += [a] + [over_both(a, shift=-d) for d in SHIFTS[1:]]
    return native, [over_col(a, dc=1) for a in native]


def local(feat_rows, feat_cols, panel_rows, panel_cols, accumulator):
    native, swapped = gather((feat_rows, feat_cols, panel_rows, panel_cols))
    out = tile(native, swapped, accumulator)
    acc_new, own, sib, col = out[0], out[1:5], out[5], out[6:10]
    sib = over_col(sib, dc=1)
    own = [a + sib[2 * n : 2 * n + 2] for n, a in enumerate(own)]
    row_sum, col_sum = own[0], col[0]
    for n in range(1, 4):
        row_sum = row_sum + over_col(own[n], dz=SHIFTS[n])
        col_sum = col_sum + over_row(col[n], dx=SHIFTS[n])
    grad_rows = row_sum[0] + over_col(row_sum[1], dy=1)
    grad_cols = col_sum[0] + over_row(col_sum[1], dh=1)
    return (acc_new, grad_rows, grad_cols)


def solution(mesh):
    in_specs = (
        P(("row", "col"), None),
        P(("col", "row"), None),
        P(("row", "col"), None),
        P(("col", "row"), None),
        P("row", "col"),
    )
    out_specs = (P("row", "col"), P(("row", "col"), None), P(("col", "row"), None))
    return jax.shard_map(local, mesh=mesh, in_specs=in_specs, out_specs=out_specs, check_vma=False)
```

time: 113 us -> 97.8 us (0.87)
  waiting for transfers between devices: 45 us -> 38 us
  starting transfers between devices: 42.4 us -> 37.7 us
  Pallas kernels: 17.2 us -> 13.9 us
    ppermute x0 -> x7, waiting for transfers between devices: none -> 27 us  [over_both(): return lax.ppermute(a, ('row', 'col'), both_perm(flip, shift))]
    ppermute x11 -> x4, waiting for transfers between devices: 23.4 us -> 1.82 us  [over_row(): return lax.ppermute(a, 'row', row_perm(dx, dh))]
    ppermute x0 -> x7, starting transfers between devices: none -> 14 us  [over_both(): return lax.ppermute(a, ('row', 'col'), both_perm(flip, shift))]
    ppermute x20 -> x14, waiting for transfers between devices: 21.6 us -> 9.19 us  [over_col(): return lax.ppermute(a, 'col', col_perm(dy, dz, dc))]
    ppermute x20 -> x14, starting transfers between devices: 24.1 us -> 13.6 us  [over_col(): return lax.ppermute(a, 'col', col_perm(dy, dz, dc))]
    ppermute x11 -> x4, starting transfers between devices: 18.3 us -> 10 us  [over_row(): return lax.ppermute(a, 'row', row_perm(dx, dh))]
    pallas_call x1, Pallas kernels: 17.2 us -> 13.8 us  [tile(): pl.pallas_call(tile_kernel, out_shape=[jax.ShapeDtypeStruct((ROWS, COLS),...]
    concatenate x2 -> x0, local copies, waits for them, and re-layouts: 1.94 us -> none  [the longest x1 0.97 us: local(): own_c = jnp.concatenate([feat_cols, panel_cols], axis=1)]
  transfers between devices with their start and end apart: 31 -> 25, of which waited for: 15 -> 12; matrix products, arithmetic and copies ran while one was open for 3% -> 1% of each run, Pallas kernels for 0% -> 0%
where the time goes in v2:
time: 97.8 us; the launch traced here: 97.4 us
  waiting for transfers between devices  38 us (39%)
  starting transfers between devices  37.7 us (39%)
  Pallas kernels  13.9 us (14%)
  local copies, waits for them, and re-layouts  5.34 us (5%)
  other arithmetic  1.69 us (2%)
    ppermute x7, waiting for transfers between devices, over_both(): return lax.ppermute(a, ('row', 'col'), both_perm(flip, shift))  27 us
    ppermute x7, starting transfers between devices, over_both(): return lax.ppermute(a, ('row', 'col'), both_perm(flip, shift))  14 us
    pallas_call x1, Pallas kernels, tile(): pl.pallas_call(tile_kernel, out_shape=[jax.ShapeDtypeStruct((ROWS, COLS),...  13.8 us
    ppermute x14, starting transfers between devices, over_col(): return lax.ppermute(a, 'col', col_perm(dy, dz, dc))  13.6 us
    ppermute x4, starting transfers between devices, over_row(): return lax.ppermute(a, 'row', row_perm(dx, dh))  10 us
    ppermute x14, waiting for transfers between devices, over_col(): return lax.ppermute(a, 'col', col_perm(dy, dz, dc))  9.19 us
    unnamed x10, local copies, waits for them, and re-layouts  5.29 us
  transfers between devices with their start and end apart: 25, of which 12 were waited for; matrix products, arithmetic and copies ran while one was open for 1% of the time, Pallas kernels for 0%

profile of v2, /device:TPU:0, one launch (start us, length us, event | category | flops | bytes accessed | tf_op | source)
XLA Modules:
  0.0 97.4 jit_solution(9528510890064014497)
XLA Ops:
  0.6 0.0 copy-start
  0.6 0.9 copy-done
  1.6 0.0 copy-start.1
  1.6 0.9 copy-done.1
  2.5 0.9 copy-done.2
  3.4 0.9 copy-done.3
  4.3 0.1 pack.1
  4.4 0.1 collective-permute-start
  4.5 1.7 %collective-permute-done = f32[64,1536]{1,0:T(8,128)S(1)} collective-permute-done((f32[64,1536]{1,0:T(8,128)S(1)}, f32[64,1536]{1,0:T(8,128)S(1)}, u32[]{:S(2)}, u32[]{:S(2)}) %collective-permute-start) | collective-permute-done | bytes 393248 | tf_op jit(solution)/shard_map/ppermute | solution.py:30
  6.2 1.7 %collective-permute-start.4 = (f32[128,1536]{1,0:T(8,128)S(1)}, f32[128,1536]{1,0:T(8,128)S(1)}, u32[]{:S(2)}, u32[]{:S(2)}) collective-permute-start(f32[128,1536]{1,0:T(8,128)S(1)} %constant_dynamic-update-slice_fusion.refs_0_), channel_id=1, source_target_pairs={{0,8},{1,17},{2,10},{3,19},{4,12},{5,21},{6,14},{7,23},{8,0},{9,25... | collective-permute-start | bytes 2359304 | tf_op jit(solution)/shard_map/ppermute | solution.py:207
  8.0 1.5 %collective-permute-start.8 = (f32[128,1536]{1,0:T(8,128)S(1)}, f32[128,1536]{1,0:T(8,128)S(1)}, u32[]{:S(2)}, u32[]{:S(2)}) collective-permute-start(f32[128,1536]{1,0:T(8,128)S(1)} %constant_dynamic-update-slice_fusion.refs_0_), channel_id=1, source_target_pairs={{0,1},{1,0},{2,3},{3,2},{4,5},{5,4},{6,7},{7,6},{8,9},{9,8},{10,11... | collective-permute-start | bytes 2359304 | tf_op jit(solution)/shard_map/ppermute | solution.py:30
  9.5 1.9 %collective-permute-start.3 = (f32[128,1536]{1,0:T(8,128)S(1)}, f32[128,1536]{1,0:T(8,128)S(1)}, u32[]{:S(2)}, u32[]{:S(2)}) collective-permute-start(f32[128,1536]{1,0:T(8,128)S(1)} %constant_dynamic-update-slice_fusion.refs_0_), channel_id=1, source_target_pairs={{0,2},{1,33},{2,4},{3,35},{4,6},{5,37},{6,0},{7,39},{8,10},{9,41},... | collective-permute-start | bytes 2359304 | tf_op jit(solution)/shard_map/ppermute | solution.py:207
  11.4 2.1 %collective-permute-start.2 = (f32[128,1536]{1,0:T(8,128)S(1)}, f32[128,1536]{1,0:T(8,128)S(1)}, u32[]{:S(2)}, u32[]{:S(2)}) collective-permute-start(f32[128,1536]{1,0:T(8,128)S(1)} %constant_dynamic-update-slice_fusion.refs_0_), channel_id=1, source_target_pairs={{0,6},{1,97},{2,0},{3,99},{4,2},{5,101},{6,4},{7,103},{8,14},{9,10... | collective-permute-start | bytes 2359304 | tf_op jit(solution)/shard_map/ppermute | solution.py:207
  13.5 1.9 %collective-permute-start.1 = (f32[128,1536]{1,0:T(8,128)S(1)}, f32[128,1536]{1,0:T(8,128)S(1)}, u32[]{:S(2)}, u32[]{:S(2)}) collective-permute-start(f32[128,1536]{1,0:T(8,128)S(1)} %constant_dynamic-update-slice_fusion.refs_0_), channel_id=1, source_target_pairs={{0,4},{1,65},{2,6},{3,67},{4,0},{5,69},{6,2},{7,71},{8,12},{9,73},... | collective-permute-start | bytes 2359304 | tf_op jit(solution)/shard_map/ppermute | solution.py:207
  15.4 10.3 %collective-permute-done.4.refs_4_ = f32[128,1536]{1,0:T(8,128)S(1)} collective-permute-done((f32[128,1536]{1,0:T(8,128)S(1)}, f32[128,1536]{1,0:T(8,128)S(1)}, u32[]{:S(2)}, u32[]{:S(2)}) %collective-permute-start.4) | collective-permute-done | bytes 786464 | tf_op jit(solution)/shard_map/ppermute | solution.py:207
  25.6 0.4 collective-permute-start.12
  26.0 0.0 collective-permute-done.8.refs_8_
  26.0 1.9 %collective-permute-start.7 = (f32[128,1536]{1,0:T(8,128)S(1)}, f32[128,1536]{1,0:T(8,128)S(1)}, u32[]{:S(2)}, u32[]{:S(2)}) collective-permute-start(f32[128,1536]{1,0:T(8,128)S(1)} %collective-permute-done.4.refs_4_), channel_id=1, source_target_pairs={{0,2},{1,33},{2,4},{3,35},{4,6},{5,37},{6,0},{7,39},{8,10},{9,41},... | collective-permute-start | bytes 2359304 | tf_op jit(solution)/shard_map/ppermute | solution.py:207
  27.9 0.0 collective-permute-done.3.refs_3_
  28.0 2.2 %collective-permute-start.6 = (f32[128,1536]{1,0:T(8,128)S(1)}, f32[128,1536]{1,0:T(8,128)S(1)}, u32[]{:S(2)}, u32[]{:S(2)}) collective-permute-start(f32[128,1536]{1,0:T(8,128)S(1)} %collective-permute-done.4.refs_4_), channel_id=1, source_target_pairs={{0,6},{1,97},{2,0},{3,99},{4,2},{5,101},{6,4},{7,103},{8,14},{9,10... | collective-permute-start | bytes 2359304 | tf_op jit(solution)/shard_map/ppermute | solution.py:207
  30.1 1.3 %collective-permute-done.2.refs_2_ = f32[128,1536]{1,0:T(8,128)S(1)} collective-permute-done((f32[128,1536]{1,0:T(8,128)S(1)}, f32[128,1536]{1,0:T(8,128)S(1)}, u32[]{:S(2)}, u32[]{:S(2)}) %collective-permute-start.2) | collective-permute-done | bytes 786464 | tf_op jit(solution)/shard_map/ppermute | solution.py:207
  31.5 2.3 %collective-permute-start.5 = (f32[128,1536]{1,0:T(8,128)S(1)}, f32[128,1536]{1,0:T(8,128)S(1)}, u32[]{:S(2)}, u32[]{:S(2)}) collective-permute-start(f32[128,1536]{1,0:T(8,128)S(1)} %collective-permute-done.4.refs_4_), channel_id=1, source_target_pairs={{0,4},{1,65},{2,6},{3,67},{4,0},{5,69},{6,2},{7,71},{8,12},{9,73},... | collective-permute-start | bytes 2359304 | tf_op jit(solution)/shard_map/ppermute | solution.py:207
  33.8 0.0 collective-permute-done.1.refs_1_
  33.8 0.0 collective-permute-start.11
  33.8 0.0 collective-permute-done.12.refs_12_
  33.8 0.5 collective-permute-start.10
  34.3 7.5 %collective-permute-done.7.refs_7_ = f32[128,1536]{1,0:T(8,128)S(1)} collective-permute-done((f32[128,1536]{1,0:T(8,128)S(1)}, f32[128,1536]{1,0:T(8,128)S(1)}, u32[]{:S(2)}, u32[]{:S(2)}) %collective-permute-start.7) | collective-permute-done | bytes 786464 | tf_op jit(solution)/shard_map/ppermute | solution.py:207
  41.8 0.0 collective-permute-start.9
  41.8 0.0 collective-permute-done.6.refs_6_
  41.8 0.5 collective-permute-start.15
  42.3 7.9 %collective-permute-done.5.refs_5_ = f32[128,1536]{1,0:T(8,128)S(1)} collective-permute-done((f32[128,1536]{1,0:T(8,128)S(1)}, f32[128,1536]{1,0:T(8,128)S(1)}, u32[]{:S(2)}, u32[]{:S(2)}) %collective-permute-start.5) | collective-permute-done | bytes 786464 | tf_op jit(solution)/shard_map/ppermute | solution.py:207
  50.2 0.0 collective-permute-start.14
  50.2 0.0 collective-permute-done.11.refs_11_
  50.2 0.5 collective-permute-start.13
  50.7 0.0 collective-permute-done.10.refs_10_
  50.7 0.0 collective-permute-done.9.refs_9_
  50.7 0.0 collective-permute-done.15.refs_15_
  50.7 1.8 %collective-permute-done.14.refs_14_ = f32[128,1536]{1,0:T(8,128)S(1)} collective-permute-done((f32[128,1536]{1,0:T(8,128)S(1)}, f32[128,1536]{1,0:T(8,128)S(1)}, u32[]{:S(2)}, u32[]{:S(2)}) %collective-permute-start.14) | collective-permute-done | bytes 786464 | tf_op jit(solution)/shard_map/ppermute | solution.py:30
  52.5 1.1 %collective-permute-done.13.refs_13_ = f32[128,1536]{1,0:T(8,128)S(1)} collective-permute-done((f32[128,1536]{1,0:T(8,128)S(1)}, f32[128,1536]{1,0:T(8,128)S(1)}, u32[]{:S(2)}, u32[]{:S(2)}) %collective-permute-start.13) | collective-permute-done | bytes 786464 | tf_op jit(solution)/shard_map/ppermute | solution.py:30
  53.6 1.6 %copy-done.4 = f32[1024,512]{1,0:T(8,128)S(1)} copy-done((f32[1024,512]{1,0:T(8,128)S(1)}, f32[1024,512]{1,0:T(8,128)}, u32[]{:S(2)}) %copy-start.4) | copy-done | bytes 2097176
  55.2 13.8 %tile.1 = (f32[1024,512]{1,0:T(8,128)}, f32[2,64,512]{2,1,0:T(8,128)S(1)}, f32[2,64,512]{2,1,0:T(8,128)S(1)}, f32[2,64,512]{2,1,0:T(8,128)S(1)}, f32[2,64,512]{2...) custom-call(f32[128,1536]{1,0:T(8,128)S(1)} %constant_dynamic-update, ...), custom_call_target="tpu_custom_call" | custom-call | flops 8000000000 | bytes 20000000 | tf_op jit(solution)/shard_map/tile/pallas_call | solution.py:161
  69.0 0.1 collective-permute-start.16
  69.2 3.0 %collective-permute-start.21 = (f32[2,64,512]{2,1,0:T(8,128)S(1)}, f32[2,64,512]{2,1,0:T(8,128)S(1)}, u32[]{:S(2)}, u32[]{:S(2)}) collective-permute-start(f32[2,64,512]{2,1,0:T(8,128)S(1)} %get-tuple-element.24), channel_id=1, source_target_pairs={{0,64},{16,80},{32,96},{48,112},{64,0},{80,16},{96,32},{112,48},{1... | collective-permute-start | bytes 786440 | tf_op jit(solution)/shard_map/ppermute | solution.py:34
  72.2 0.6 collective-permute-start.22
  72.8 2.6 %collective-permute-start.23 = (f32[2,64,512]{2,1,0:T(8,128)S(1)}, f32[2,64,512]{2,1,0:T(8,128)S(1)}, u32[]{:S(2)}, u32[]{:S(2)}) collective-permute-start(f32[2,64,512]{2,1,0:T(8,128)S(1)} %get-tuple-element.26), channel_id=1, source_target_pairs={{0,96},{16,112},{32,0},{48,16},{64,32},{80,48},{96,64},{112,80},{1... | collective-permute-start | bytes 786440 | tf_op jit(solution)/shard_map/ppermute | solution.py:34
  75.5 0.0 collective-permute-done.16
  75.5 0.1 slice_add_fusion.2
  75.6 2.7 %collective-permute-start.17 = (f32[2,64,512]{2,1,0:T(8,128)S(1)}, f32[2,64,512]{2,1,0:T(8,128)S(1)}, u32[]{:S(2)}, u32[]{:S(2)}) collective-permute-start(f32[2,64,512]{2,1,0:T(8,128)S(1)} %get-tuple-element.27), channel_id=1, source_target_pairs={{0,4},{1,5},{2,6},{3,7},{4,0},{5,1},{6,2},{7,3},{8,12},{9,13},{10,... | collective-permute-start | bytes 786440 | tf_op jit(solution)/shard_map/ppermute | solution.py:30
  78.3 3.4 %collective-permute-start.19 = (f32[2,64,512]{2,1,0:T(8,128)S(1)}, f32[2,64,512]{2,1,0:T(8,128)S(1)}, u32[]{:S(2)}, u32[]{:S(2)}) collective-permute-start(f32[2,64,512]{2,1,0:T(8,128)S(1)} %get-tuple-element.28), channel_id=1, source_target_pairs={{0,6},{1,7},{2,0},{3,1},{4,2},{5,3},{6,4},{7,5},{8,14},{9,15},{10,... | collective-permute-start | bytes 786440 | tf_op jit(solution)/shard_map/ppermute | solution.py:30
  81.7 0.0 collective-permute-done.21
  81.7 1.5 %collective-permute-start.18 = (f32[2,64,512]{2,1,0:T(8,128)S(1)}, f32[2,64,512]{2,1,0:T(8,128)S(1)}, u32[]{:S(2)}, u32[]{:S(2)}) collective-permute-start(f32[2,64,512]{2,1,0:T(8,128)S(1)} %get-tuple-element.29), channel_id=1, source_target_pairs={{0,2},{1,3},{2,4},{3,5},{4,6},{5,7},{6,0},{7,1},{8,10},{9,11},{10,... | collective-permute-start | bytes 786440 | tf_op jit(solution)/shard_map/ppermute | solution.py:30
  83.2 1.7 %collective-permute-done.22 = f32[2,64,512]{2,1,0:T(8,128)S(1)} collective-permute-done((f32[2,64,512]{2,1,0:T(8,128)S(1)}, f32[2,64,512]{2,1,0:T(8,128)S(1)}, u32[]{:S(2)}, u32[]{:S(2)}) %collective-permute-start.22) | collective-permute-done | bytes 262176 | tf_op jit(solution)/shard_map/ppermute | solution.py:34
  84.9 0.1 collective-permute-done.23
  85.0 0.1 add_add_fusion
  85.1 3.8 %collective-permute-start.24 = (f32[64,512]{1,0:T(8,128)S(1)}, f32[64,512]{1,0:T(8,128)S(1)}, u32[]{:S(2)}, u32[]{:S(2)}) collective-permute-start(f32[64,512]{1,0:T(8,128)S(1)} %slice_bitcast_fusion), channel_id=1, source_target_pairs={{0,16},{16,0},{32,48},{48,32},{64,80},{80,64},{96,112},{112,96},{1... | collective-permute-start | bytes 393224 | tf_op jit(solution)/shard_map/ppermute | solution.py:34
  88.9 0.0 collective-permute-done.17
  88.9 1.8 %collective-permute-done.19 = f32[2,64,512]{2,1,0:T(8,128)S(1)} collective-permute-done((f32[2,64,512]{2,1,0:T(8,128)S(1)}, f32[2,64,512]{2,1,0:T(8,128)S(1)}, u32[]{:S(2)}, u32[]{:S(2)}) %collective-permute-start.19) | collective-permute-done | bytes 262176 | tf_op jit(solution)/shard_map/ppermute | solution.py:30
  90.7 0.4 collective-permute-done.18
  91.1 0.1 fusion.2
  91.2 2.4 %collective-permute-start.20 = (f32[64,512]{1,0:T(8,128)S(1)}, f32[64,512]{1,0:T(8,128)S(1)}, u32[]{:S(2)}, u32[]{:S(2)}) collective-permute-start(f32[64,512]{1,0:T(8,128)S(1)} %slice_bitcast_fusion.2), channel_id=1, source_target_pairs={{0,8},{1,9},{2,10},{3,11},{4,12},{5,13},{6,14},{7,15},{8,0},{9,1},... | collective-permute-start | bytes 393224 | tf_op jit(solution)/shard_map/ppermute | solution.py:30
  93.6 0.0 collective-permute-done.24
  93.6 0.7 fusion.3
  94.3 2.4 %collective-permute-done.20 = f32[64,512]{1,0:T(8,128)S(1)} collective-permute-done((f32[64,512]{1,0:T(8,128)S(1)}, f32[64,512]{1,0:T(8,128)S(1)}, u32[]{:S(2)}, u32[]{:S(2)}) %collective-permute-start.20) | collective-permute-done | bytes 131104 | tf_op jit(solution)/shard_map/ppermute | solution.py:30
  96.7 0.7 fusion.4
  (6 shorter events, 0.1 us)
Async XLA Ops:
  0.6 1.0 copy-start
  1.6 0.9 copy-start.1
  2.5 0.9 copy-start.2
  3.4 0.9 copy-start.3
  4.4 1.8 %collective-permute-start = (f32[64,1536]{1,0:T(8,128)S(1)}, f32[64,1536]{1,0:T(8,128)S(1)}, u32[]{:S(2)}, u32[]{:S(2)}) collective-permute-start(f32[64,1536]{1,0:T(8,128)S(1)} %get-tuple-element.16), channel_id=1, source_target_pairs={{0,1},{1,0},{2,3},{3,2},{4,5},{5,4},{6,7},{7,6},{8,9},{9,8},{10,11... | collective-permute-start | bytes 1179656 | tf_op jit(solution)/shard_map/ppermute | solution.py:30
  6.2 19.4 %collective-permute-start.4 = (f32[128,1536]{1,0:T(8,128)S(1)}, f32[128,1536]{1,0:T(8,128)S(1)}, u32[]{:S(2)}, u32[]{:S(2)}) collective-permute-start(f32[128,1536]{1,0:T(8,128)S(1)} %constant_dynamic-update-slice_fusion.refs_0_), channel_id=1, source_target_pairs={{0,8},{1,17},{2,10},{3,19},{4,12},{5,21},{6,14},{7,23},{8,0},{9,25... | collective-permute-start | bytes 2359304 | tf_op jit(solution)/shard_map/ppermute | solution.py:207
  8.0 18.1 %collective-permute-start.8 = (f32[128,1536]{1,0:T(8,128)S(1)}, f32[128,1536]{1,0:T(8,128)S(1)}, u32[]{:S(2)}, u32[]{:S(2)}) collective-permute-start(f32[128,1536]{1,0:T(8,128)S(1)} %constant_dynamic-update-slice_fusion.refs_0_), channel_id=1, source_target_pairs={{0,1},{1,0},{2,3},{3,2},{4,5},{5,4},{6,7},{7,6},{8,9},{9,8},{10,11... | collective-permute-start | bytes 2359304 | tf_op jit(solution)/shard_map/ppermute | solution.py:30
  9.5 18.5 %collective-permute-start.3 = (f32[128,1536]{1,0:T(8,128)S(1)}, f32[128,1536]{1,0:T(8,128)S(1)}, u32[]{:S(2)}, u32[]{:S(2)}) collective-permute-start(f32[128,1536]{1,0:T(8,128)S(1)} %constant_dynamic-update-slice_fusion.refs_0_), channel_id=1, source_target_pairs={{0,2},{1,33},{2,4},{3,35},{4,6},{5,37},{6,0},{7,39},{8,10},{9,41},... | collective-permute-start | bytes 2359304 | tf_op jit(solution)/shard_map/ppermute | solution.py:207
  11.4 20.1 %collective-permute-start.2 = (f32[128,1536]{1,0:T(8,128)S(1)}, f32[128,1536]{1,0:T(8,128)S(1)}, u32[]{:S(2)}, u32[]{:S(2)}) collective-permute-start(f32[128,1536]{1,0:T(8,128)S(1)} %constant_dynamic-update-slice_fusion.refs_0_), channel_id=1, source_target_pairs={{0,6},{1,97},{2,0},{3,99},{4,2},{5,101},{6,4},{7,103},{8,14},{9,10... | collective-permute-start | bytes 2359304 | tf_op jit(solution)/shard_map/ppermute | solution.py:207
  13.5 20.3 %collective-permute-start.1 = (f32[128,1536]{1,0:T(8,128)S(1)}, f32[128,1536]{1,0:T(8,128)S(1)}, u32[]{:S(2)}, u32[]{:S(2)}) collective-permute-start(f32[128,1536]{1,0:T(8,128)S(1)} %constant_dynamic-update-slice_fusion.refs_0_), channel_id=1, source_target_pairs={{0,4},{1,65},{2,6},{3,67},{4,0},{5,69},{6,2},{7,71},{8,12},{9,73},... | collective-permute-start | bytes 2359304 | tf_op jit(solution)/shard_map/ppermute | solution.py:207
  25.6 8.1 %collective-permute-start.12 = (f32[128,1536]{1,0:T(8,128)S(1)}, f32[128,1536]{1,0:T(8,128)S(1)}, u32[]{:S(2)}, u32[]{:S(2)}) collective-permute-start(f32[128,1536]{1,0:T(8,128)S(1)} %collective-permute-done.4.refs_4_), channel_id=1, source_target_pairs={{0,1},{1,0},{2,3},{3,2},{4,5},{5,4},{6,7},{7,6},{8,9},{9,8},{10,11... | collective-permute-start | bytes 2359304 | tf_op jit(solution)/shard_map/ppermute | solution.py:30
  26.0 15.7 %collective-permute-start.7 = (f32[128,1536]{1,0:T(8,128)S(1)}, f32[128,1536]{1,0:T(8,128)S(1)}, u32[]{:S(2)}, u32[]{:S(2)}) collective-permute-start(f32[128,1536]{1,0:T(8,128)S(1)} %collective-permute-done.4.refs_4_), channel_id=1, source_target_pairs={{0,2},{1,33},{2,4},{3,35},{4,6},{5,37},{6,0},{7,39},{8,10},{9,41},... | collective-permute-start | bytes 2359304 | tf_op jit(solution)/shard_map/ppermute | solution.py:207
  28.0 13.8 %collective-permute-start.6 = (f32[128,1536]{1,0:T(8,128)S(1)}, f32[128,1536]{1,0:T(8,128)S(1)}, u32[]{:S(2)}, u32[]{:S(2)}) collective-permute-start(f32[128,1536]{1,0:T(8,128)S(1)} %collective-permute-done.4.refs_4_), channel_id=1, source_target_pairs={{0,6},{1,97},{2,0},{3,99},{4,2},{5,101},{6,4},{7,103},{8,14},{9,10... | collective-permute-start | bytes 2359304 | tf_op jit(solution)/shard_map/ppermute | solution.py:207
  31.5 18.8 %collective-permute-start.5 = (f32[128,1536]{1,0:T(8,128)S(1)}, f32[128,1536]{1,0:T(8,128)S(1)}, u32[]{:S(2)}, u32[]{:S(2)}) collective-permute-start(f32[128,1536]{1,0:T(8,128)S(1)} %collective-permute-done.4.refs_4_), channel_id=1, source_target_pairs={{0,4},{1,65},{2,6},{3,67},{4,0},{5,69},{6,2},{7,71},{8,12},{9,73},... | collective-permute-start | bytes 2359304 | tf_op jit(solution)/shard_map/ppermute | solution.py:207
  33.8 16.5 %collective-permute-start.11 = (f32[128,1536]{1,0:T(8,128)S(1)}, f32[128,1536]{1,0:T(8,128)S(1)}, u32[]{:S(2)}, u32[]{:S(2)}) collective-permute-start(f32[128,1536]{1,0:T(8,128)S(1)} %collective-permute-done.3.refs_3_), channel_id=1, source_target_pairs={{0,1},{1,0},{2,3},{3,2},{4,5},{5,4},{6,7},{7,6},{8,9},{9,8},{10,11... | collective-permute-start | bytes 2359304 | tf_op jit(solution)/shard_map/ppermute | solution.py:30
  33.8 17.0 %collective-permute-start.10 = (f32[128,1536]{1,0:T(8,128)S(1)}, f32[128,1536]{1,0:T(8,128)S(1)}, u32[]{:S(2)}, u32[]{:S(2)}) collective-permute-start(f32[128,1536]{1,0:T(8,128)S(1)} %collective-permute-done.2.refs_2_), channel_id=1, source_target_pairs={{0,1},{1,0},{2,3},{3,2},{4,5},{5,4},{6,7},{7,6},{8,9},{9,8},{10,11... | collective-permute-start | bytes 2359304 | tf_op jit(solution)/shard_map/ppermute | solution.py:30
  41.8 9.0 %collective-permute-start.9 = (f32[128,1536]{1,0:T(8,128)S(1)}, f32[128,1536]{1,0:T(8,128)S(1)}, u32[]{:S(2)}, u32[]{:S(2)}) collective-permute-start(f32[128,1536]{1,0:T(8,128)S(1)} %collective-permute-done.1.refs_1_), channel_id=1, source_target_pairs={{0,1},{1,0},{2,3},{3,2},{4,5},{5,4},{6,7},{7,6},{8,9},{9,8},{10,11... | collective-permute-start | bytes 2359304 | tf_op jit(solution)/shard_map/ppermute | solution.py:30
  41.8 9.0 %collective-permute-start.15 = (f32[128,1536]{1,0:T(8,128)S(1)}, f32[128,1536]{1,0:T(8,128)S(1)}, u32[]{:S(2)}, u32[]{:S(2)}) collective-permute-start(f32[128,1536]{1,0:T(8,128)S(1)} %collective-permute-done.7.refs_7_), channel_id=1, source_target_pairs={{0,1},{1,0},{2,3},{3,2},{4,5},{5,4},{6,7},{7,6},{8,9},{9,8},{10,11... | collective-permute-start | bytes 2359304 | tf_op jit(solution)/shard_map/ppermute | solution.py:30
  50.2 2.3 %collective-permute-start.14 = (f32[128,1536]{1,0:T(8,128)S(1)}, f32[128,1536]{1,0:T(8,128)S(1)}, u32[]{:S(2)}, u32[]{:S(2)}) collective-permute-start(f32[128,1536]{1,0:T(8,128)S(1)} %collective-permute-done.6.refs_6_), channel_id=1, source_target_pairs={{0,1},{1,0},{2,3},{3,2},{4,5},{5,4},{6,7},{7,6},{8,9},{9,8},{10,11... | collective-permute-start | bytes 2359304 | tf_op jit(solution)/shard_map/ppermute | solution.py:30
  50.2 3.4 %collective-permute-start.13 = (f32[128,1536]{1,0:T(8,128)S(1)}, f32[128,1536]{1,0:T(8,128)S(1)}, u32[]{:S(2)}, u32[]{:S(2)}) collective-permute-start(f32[128,1536]{1,0:T(8,128)S(1)} %collective-permute-done.5.refs_5_), channel_id=1, source_target_pairs={{0,1},{1,0},{2,3},{3,2},{4,5},{5,4},{6,7},{7,6},{8,9},{9,8},{10,11... | collective-permute-start | bytes 2359304 | tf_op jit(solution)/shard_map/ppermute | solution.py:30
  53.6 1.6 %copy-start.4 = (f32[1024,512]{1,0:T(8,128)S(1)}, f32[1024,512]{1,0:T(8,128)}, u32[]{:S(2)}) copy-start(f32[1024,512]{1,0:T(8,128)} %refs_16_.1) | copy-start | bytes 6291460
  69.0 6.4 %collective-permute-start.16 = (f32[8,64,512]{2,1,0:T(8,128)S(1)}, f32[8,64,512]{2,1,0:T(8,128)S(1)}, u32[]{:S(2)}, u32[]{:S(2)}) collective-permute-start(f32[8,64,512]{2,1,0:T(8,128)S(1)} %get-tuple-element.19), channel_id=1, source_target_pairs={{0,1},{1,0},{2,3},{3,2},{4,5},{5,4},{6,7},{7,6},{8,9},{9,8},{10,11... | collective-permute-start | bytes 3145736 | tf_op jit(solution)/shard_map/ppermute | solution.py:30
  69.2 12.5 %collective-permute-start.21 = (f32[2,64,512]{2,1,0:T(8,128)S(1)}, f32[2,64,512]{2,1,0:T(8,128)S(1)}, u32[]{:S(2)}, u32[]{:S(2)}) collective-permute-start(f32[2,64,512]{2,1,0:T(8,128)S(1)} %get-tuple-element.24), channel_id=1, source_target_pairs={{0,64},{16,80},{32,96},{48,112},{64,0},{80,16},{96,32},{112,48},{1... | collective-permute-start | bytes 786440 | tf_op jit(solution)/shard_map/ppermute | solution.py:34
  72.2 12.7 %collective-permute-start.22 = (f32[2,64,512]{2,1,0:T(8,128)S(1)}, f32[2,64,512]{2,1,0:T(8,128)S(1)}, u32[]{:S(2)}, u32[]{:S(2)}) collective-permute-start(f32[2,64,512]{2,1,0:T(8,128)S(1)} %get-tuple-element.25), channel_id=1, source_target_pairs={{0,32},{16,48},{32,64},{48,80},{64,96},{80,112},{96,0},{112,16},{1... | collective-permute-start | bytes 786440 | tf_op jit(solution)/shard_map/ppermute | solution.py:34
  72.8 12.2 %collective-permute-start.23 = (f32[2,64,512]{2,1,0:T(8,128)S(1)}, f32[2,64,512]{2,1,0:T(8,128)S(1)}, u32[]{:S(2)}, u32[]{:S(2)}) collective-permute-start(f32[2,64,512]{2,1,0:T(8,128)S(1)} %get-tuple-element.26), channel_id=1, source_target_pairs={{0,96},{16,112},{32,0},{48,16},{64,32},{80,48},{96,64},{112,80},{1... | collective-permute-start | bytes 786440 | tf_op jit(solution)/shard_map/ppermute | solution.py:34
  75.6 13.3 %collective-permute-start.17 = (f32[2,64,512]{2,1,0:T(8,128)S(1)}, f32[2,64,512]{2,1,0:T(8,128)S(1)}, u32[]{:S(2)}, u32[]{:S(2)}) collective-permute-start(f32[2,64,512]{2,1,0:T(8,128)S(1)} %get-tuple-element.27), channel_id=1, source_target_pairs={{0,4},{1,5},{2,6},{3,7},{4,0},{5,1},{6,2},{7,3},{8,12},{9,13},{10,... | collective-permute-start | bytes 786440 | tf_op jit(solution)/shard_map/ppermute | solution.py:30
  78.3 12.3 %collective-permute-start.19 = (f32[2,64,512]{2,1,0:T(8,128)S(1)}, f32[2,64,512]{2,1,0:T(8,128)S(1)}, u32[]{:S(2)}, u32[]{:S(2)}) collective-permute-start(f32[2,64,512]{2,1,0:T(8,128)S(1)} %get-tuple-element.28), channel_id=1, source_target_pairs={{0,6},{1,7},{2,0},{3,1},{4,2},{5,3},{6,4},{7,5},{8,14},{9,15},{10,... | collective-permute-start | bytes 786440 | tf_op jit(solution)/shard_map/ppermute | solution.py:30
  81.7 9.4 %collective-permute-start.18 = (f32[2,64,512]{2,1,0:T(8,128)S(1)}, f32[2,64,512]{2,1,0:T(8,128)S(1)}, u32[]{:S(2)}, u32[]{:S(2)}) collective-permute-start(f32[2,64,512]{2,1,0:T(8,128)S(1)} %get-tuple-element.29), channel_id=1, source_target_pairs={{0,2},{1,3},{2,4},{3,5},{4,6},{5,7},{6,0},{7,1},{8,10},{9,11},{10,... | collective-permute-start | bytes 786440 | tf_op jit(solution)/shard_map/ppermute | solution.py:30
  85.1 8.5 %collective-permute-start.24 = (f32[64,512]{1,0:T(8,128)S(1)}, f32[64,512]{1,0:T(8,128)S(1)}, u32[]{:S(2)}, u32[]{:S(2)}) collective-permute-start(f32[64,512]{1,0:T(8,128)S(1)} %slice_bitcast_fusion), channel_id=1, source_target_pairs={{0,16},{16,0},{32,48},{48,32},{64,80},{80,64},{96,112},{112,96},{1... | collective-permute-start | bytes 393224 | tf_op jit(solution)/shard_map/ppermute | solution.py:34
  91.2 5.5 %collective-permute-start.20 = (f32[64,512]{1,0:T(8,128)S(1)}, f32[64,512]{1,0:T(8,128)S(1)}, u32[]{:S(2)}, u32[]{:S(2)}) collective-permute-start(f32[64,512]{1,0:T(8,128)S(1)} %slice_bitcast_fusion.2), channel_id=1, source_target_pairs={{0,8},{1,9},{2,10},{3,11},{4,12},{5,13},{6,14},{7,15},{8,0},{9,1},... | collective-permute-start | bytes 393224 | tf_op jit(solution)/shard_map/ppermute | solution.py:30

commit v3 on v2

--- a/solution.py
+++ b/solution.py
@@ -78,34 +78,52 @@
     )
 
 
-def pack_kernel(feat_rows, feat_cols, panel_rows, panel_cols, keep, give):
-    def fill(mine, other):
-        keep[:B, :F], keep[:B, F:] = mine[0][...], mine[1][...]
-        give[:, :F], give[:, F:] = other[0][...], other[1][...]
+anywhere = pl.BlockSpec(memory_space=pl.ANY)
+
+
+def pack_kernel(feat_rows, feat_cols, panel_rows, panel_cols, keep, give, sems):
+    def copies(mine, other):
+        return [
+            pltpu.make_async_copy(other[0], give.at[:, :F], sems.at[0]),
+            pltpu.make_async_copy(other[1], give.at[:, F:], sems.at[1]),
+            pltpu.make_async_copy(mine[0], keep.at[:B, :F], sems.at[2]),
+            pltpu.make_async_copy(mine[1], keep.at[:B, F:], sems.at[3]),
+        ]
 
     rows, cols = (feat_rows, panel_rows), (feat_cols, panel_cols)
+
+    def start(mine, other):
+        for copy in copies(mine, other):
+            copy.start()
+
     c = lax.axis_index("col") % 2
-    pl.when(c == 0)(lambda: fill(rows, cols))
-    pl.when(c == 1)(lambda: fill(cols, rows))
+    pl.when(c == 0)(lambda: start(rows, cols))
+    pl.when(c == 1)(lambda: start(cols, rows))
+    for copy in copies(rows, cols):
+        copy.wait()
 
 
 def pack(*shards):
     return pl.pallas_call(
         pack_kernel,
         out_shape=[jax.ShapeDtypeStruct((2 * B, W), f32), jax.ShapeDtypeStruct((B, W), f32)],
-        in_specs=[whole] * 4,
+        in_specs=[anywhere] * 4,
         out_specs=[whole] * 2,
-        compiler_params=pltpu.CompilerParams(vmem_limit_bytes=4 * 1024 * 1024),
+        scratch_shapes=[pltpu.SemaphoreType.DMA((4,))],
+        compiler_params=pltpu.CompilerParams(vmem_limit_bytes=PACK_VMEM * 1024 * 1024),
         cost_estimate=pl.CostEstimate(flops=0, bytes_accessed=1_600_000, transcendentals=0),
         name="pack",
     )(*shards)
 
 
+PACK_VMEM = 4
+
+
 def tile_kernel(*refs):
     place = places()
-    native, swapped, acc, acc_new = refs[:8], refs[8:16], refs[16], refs[17]
-    own_out, sib_out, col_out = refs[18:22], refs[22], refs[23:27]
-    rh, rl, rf, ch, cl, cf, nr, nc, row_term, col_term, tsum = refs[27:]
+    native, swapped, acc, acc_new = refs[:9], refs[9:18], refs[18], refs[19]
+    own_out, sib_out, col_out = refs[20:24], refs[24], refs[25:29]
+    rh, rl, rf, ch, cl, cf, nr, nc, row_term, col_term, tsum = refs[29:]
     step = pl.program_id(0)
 
     def put(a, at, hi, lo, feat, norm):
@@ -118,10 +136,16 @@
     def _():
         def prepare(row_source, col_source, start):
             for n in range(8):
-                at = pl.ds(pl.multiple_of(place[1 + n] * B, 2 * B), 2 * B)
-                put(row_source[n][...], at, rh, rl, rf, nr)
-                at = pl.ds(pl.multiple_of(place[9 + n] * B, B), B)
-                put(col_source[n][start : start + B, :], at, ch, cl, cf, nc)
+                at = place[1 + n] * B
+                col_at = pl.ds(pl.multiple_of(place[9 + n] * B, B), B)
+                if n == HALVED:
+                    for half in range(2):
+                        put(row_source[n + half][...], pl.ds(pl.multiple_of(at + half * B, B), B), rh, rl, rf, nr)
+                    put(col_source[n + start // B][...], col_at, ch, cl, cf, nc)
+                    continue
+                k = n + (n > HALVED)
+                put(row_source[k][...], pl.ds(pl.multiple_of(at, 2 * B), 2 * B), rh, rl, rf, nr)
+                put(col_source[k][start : start + B, :], col_at, ch, cl, cf, nc)
 
         pl.when(place[0] == 0)(lambda: prepare(native, swapped, B))
         pl.when(place[0] == 1)(lambda: prepare(swapped, native, 0))
@@ -166,7 +190,7 @@
         + [pair] * 4,
         grid_spec=pl.GridSpec(
             grid=(STEPS,),
-            in_specs=[whole] * 16 + [block],
+            in_specs=[whole] * 18 + [block],
             out_specs=[block] + [whole] * 9,
             scratch_shapes=[
                 pltpu.VMEM((ROWS, W), bf16),
@@ -207,13 +231,17 @@
     return lax.ppermute(a, ("row", "col"), both_perm(flip, shift))
 
 
+HALVED = 5
+
+
 def gather(shards):
     keep, give = pack(*shards)
     own = lax.dynamic_update_slice(keep, over_col(give, dc=1), (B, 0))
     far = over_both(own, flip=1)
-    native = []
-    for a in (own, far):
-        native += [a] + [over_both(a, shift=-d) for d in SHIFTS[1:]]
+    near = [own] + [over_both(own, shift=-d) for d in SHIFTS[1:]]
+    other = [far] + [over_both(far, shift=-d) for d in SHIFTS[2:]]
+    halves = [over_both(far[:B], shift=-SHIFTS[1]), over_both(near[1][B:], flip=1)]
+    native = near + other[:1] + halves + other[1:]
     return native, [over_col(a, dc=1) for a in native]
 
 

time: 97.8 us -> 90.6 us (0.926)
  starting transfers between devices: 37.7 us -> 34.8 us
  waiting for transfers between devices: 38 us -> 35.3 us
  local copies, waits for them, and re-layouts: 5.34 us -> 3.8 us
    ppermute x7 -> x8, waiting for transfers between devices: 27 us -> 18.7 us  [over_both(): return lax.ppermute(a, ('row', 'col'), both_perm(flip, shift))]
    ppermute x4, waiting for transfers between devices: 1.82 us -> 8.17 us  [over_row(): return lax.ppermute(a, 'row', row_perm(dx, dh))]
    ppermute x7 -> x8, starting transfers between devices: 14 us -> 19.8 us  [over_both(): return lax.ppermute(a, ('row', 'col'), both_perm(flip, shift))]
    ppermute x14 -> x15, starting transfers between devices: 13.6 us -> 8.72 us  [over_col(): return lax.ppermute(a, 'col', col_perm(dy, dz, dc))]
    ppermute x4, starting transfers between devices: 10 us -> 6.3 us  [over_row(): return lax.ppermute(a, 'row', row_perm(dx, dh))]
    unnamed x10, local copies, waits for them, and re-layouts: 5.29 us -> 3.7 us
    ppermute x14 -> x15, waiting for transfers between devices: 9.19 us -> 8.4 us  [over_col(): return lax.ppermute(a, 'col', col_perm(dy, dz, dc))]
  transfers between devices with their start and end apart: 25 -> 27, of which waited for: 12 -> 11; matrix products, arithmetic and copies ran while one was open for 1% -> 1% of each run, Pallas kernels for 0% -> 0%
where the time goes in v3:
time: 90.6 us; the launch traced here: 90.4 us
  waiting for transfers between devices  35.3 us (39%)
  starting transfers between devices  34.8 us (38%)
  Pallas kernels  14 us (15%)
  local copies, waits for them, and re-layouts  3.8 us (4%)
  other arithmetic  1.69 us (2%)
    ppermute x8, starting transfers between devices, over_both(): return lax.ppermute(a, ('row', 'col'), both_perm(flip, shift))  19.8 us
    ppermute x8, waiting for transfers between devices, over_both(): return lax.ppermute(a, ('row', 'col'), both_perm(flip, shift))  18.7 us
    pallas_call x1, Pallas kernels, tile(): pl.pallas_call(tile_kernel, out_shape=[jax.ShapeDtypeStruct((ROWS, COLS),...  13.9 us
    ppermute x15, starting transfers between devices, over_col(): return lax.ppermute(a, 'col', col_perm(dy, dz, dc))  8.72 us
    ppermute x15, waiting for transfers between devices, over_col(): return lax.ppermute(a, 'col', col_perm(dy, dz, dc))  8.4 us
    ppermute x4, waiting for transfers between devices, over_row(): return lax.ppermute(a, 'row', row_perm(dx, dh))  8.17 us
    ppermute x4, starting transfers between devices, over_row(): return lax.ppermute(a, 'row', row_perm(dx, dh))  6.3 us
    unnamed x10, local copies, waits for them, and re-layouts  3.7 us
  transfers between devices with their start and end apart: 27, of which 11 were waited for; matrix products, arithmetic and copies ran while one was open for 1% of the time, Pallas kernels for 0%

profile of v3, /device:TPU:0, one launch (start us, length us, event | category | flops | bytes accessed | tf_op | source)
XLA Modules:
  0.0 90.4 jit_solution(8974358085868444472)
XLA Ops:
  0.6 0.9 %copy-done = f32[64,1024]{1,0:T(8,128)S(1)} copy-done((f32[64,1024]{1,0:T(8,128)S(1)}, f32[64,1024]{1,0:T(8,128)}, u32[]{:S(2)}) %copy-start) | copy-done | bytes 262168
  1.6 0.9 %copy-done.1 = f32[64,1024]{1,0:T(8,128)S(1)} copy-done((f32[64,1024]{1,0:T(8,128)S(1)}, f32[64,1024]{1,0:T(8,128)}, u32[]{:S(2)}) %copy-start.1) | copy-done | bytes 262168
  2.5 0.9 copy-done.2
  3.4 0.9 copy-done.3
  4.3 0.1 pack.1
  4.5 0.1 collective-permute-start
  4.6 1.7 %collective-permute-done = f32[64,1536]{1,0:T(8,128)S(1)} collective-permute-done((f32[64,1536]{1,0:T(8,128)S(1)}, f32[64,1536]{1,0:T(8,128)S(1)}, u32[]{:S(2)}, u32[]{:S(2)}) %collective-permute-start) | collective-permute-done | bytes 393248 | tf_op jit(solution)/shard_map/ppermute | solution.py:30
  6.3 1.7 %collective-permute-start.4 = (f32[128,1536]{1,0:T(8,128)S(1)}, f32[128,1536]{1,0:T(8,128)S(1)}, u32[]{:S(2)}, u32[]{:S(2)}) collective-permute-start(f32[128,1536]{1,0:T(8,128)S(1)} %constant_dynamic-update-slice_fusion.refs_0_), channel_id=1, source_target_pairs={{0,8},{1,17},{2,10},{3,19},{4,12},{5,21},{6,14},{7,23},{8,0},{9,25... | collective-permute-start | bytes 2359304 | tf_op jit(solution)/shard_map/ppermute | solution.py:231
  8.0 3.9 %collective-permute-start.1 = (f32[128,1536]{1,0:T(8,128)S(1)}, f32[128,1536]{1,0:T(8,128)S(1)}, u32[]{:S(2)}, u32[]{:S(2)}) collective-permute-start(f32[128,1536]{1,0:T(8,128)S(1)} %constant_dynamic-update-slice_fusion.refs_0_), channel_id=1, source_target_pairs={{0,4},{1,65},{2,6},{3,67},{4,0},{5,69},{6,2},{7,71},{8,12},{9,73},... | collective-permute-start | bytes 2359304 | tf_op jit(solution)/shard_map/ppermute | solution.py:231
  11.9 0.3 collective-permute-start.9
  12.3 1.9 %collective-permute-start.3 = (f32[128,1536]{1,0:T(8,128)S(1)}, f32[128,1536]{1,0:T(8,128)S(1)}, u32[]{:S(2)}, u32[]{:S(2)}) collective-permute-start(f32[128,1536]{1,0:T(8,128)S(1)} %constant_dynamic-update-slice_fusion.refs_0_), channel_id=1, source_target_pairs={{0,2},{1,33},{2,4},{3,35},{4,6},{5,37},{6,0},{7,39},{8,10},{9,41},... | collective-permute-start | bytes 2359304 | tf_op jit(solution)/shard_map/ppermute | solution.py:231
  14.2 2.1 %collective-permute-start.2 = (f32[128,1536]{1,0:T(8,128)S(1)}, f32[128,1536]{1,0:T(8,128)S(1)}, u32[]{:S(2)}, u32[]{:S(2)}) collective-permute-start(f32[128,1536]{1,0:T(8,128)S(1)} %constant_dynamic-update-slice_fusion.refs_0_), channel_id=1, source_target_pairs={{0,6},{1,97},{2,0},{3,99},{4,2},{5,101},{6,4},{7,103},{8,14},{9,10... | collective-permute-start | bytes 2359304 | tf_op jit(solution)/shard_map/ppermute | solution.py:231
  16.3 9.4 %collective-permute-done.4.refs_4_ = f32[128,1536]{1,0:T(8,128)S(1)} collective-permute-done((f32[128,1536]{1,0:T(8,128)S(1)}, f32[128,1536]{1,0:T(8,128)S(1)}, u32[]{:S(2)}, u32[]{:S(2)}) %collective-permute-start.4) | collective-permute-done | bytes 786464 | tf_op jit(solution)/shard_map/ppermute | solution.py:231
  25.7 4.1 %collective-permute-start.5 = (f32[64,1536]{1,0:T(8,128)S(1)}, f32[64,1536]{1,0:T(8,128)S(1)}, u32[]{:S(2)}, u32[]{:S(2)}) collective-permute-start(f32[64,1536]{1,0:T(8,128)S(1)} %slice.40), channel_id=1, source_target_pairs={{0,4},{1,65},{2,6},{3,67},{4,0},{5,69},{6,2},{7,71},{8,12},{9,73},... | collective-permute-start | bytes 1179656 | tf_op jit(solution)/shard_map/ppermute | solution.py:231
  29.9 0.0 collective-permute-done.1.refs_1_
  29.9 1.9 %collective-permute-start.6 = (f32[64,1536]{1,0:T(8,128)S(1)}, f32[64,1536]{1,0:T(8,128)S(1)}, u32[]{:S(2)}, u32[]{:S(2)}) collective-permute-start(f32[64,1536]{1,0:T(8,128)S(1)} %slice.41), channel_id=1, source_target_pairs={{0,8},{1,17},{2,10},{3,19},{4,12},{5,21},{6,14},{7,23},{8,0},{9,25... | collective-permute-start | bytes 1179656 | tf_op jit(solution)/shard_map/ppermute | solution.py:231
  31.8 0.0 collective-permute-done.9.refs_9_
  31.8 1.0 %collective-permute-start.13 = (f32[128,1536]{1,0:T(8,128)S(1)}, f32[128,1536]{1,0:T(8,128)S(1)}, u32[]{:S(2)}, u32[]{:S(2)}) collective-permute-start(f32[128,1536]{1,0:T(8,128)S(1)} %collective-permute-done.4.refs_4_), channel_id=1, source_target_pairs={{0,1},{1,0},{2,3},{3,2},{4,5},{5,4},{6,7},{7,6},{8,9},{9,8},{10,11... | collective-permute-start | bytes 2359304 | tf_op jit(solution)/shard_map/ppermute | solution.py:30
  32.8 0.0 collective-permute-done.3.refs_3_
  32.8 1.6 %collective-permute-start.8 = (f32[128,1536]{1,0:T(8,128)S(1)}, f32[128,1536]{1,0:T(8,128)S(1)}, u32[]{:S(2)}, u32[]{:S(2)}) collective-permute-start(f32[128,1536]{1,0:T(8,128)S(1)} %collective-permute-done.4.refs_4_), channel_id=1, source_target_pairs={{0,2},{1,33},{2,4},{3,35},{4,6},{5,37},{6,0},{7,39},{8,10},{9,41},... | collective-permute-start | bytes 2359304 | tf_op jit(solution)/shard_map/ppermute | solution.py:231
  34.4 0.0 collective-permute-done.2.refs_2_
  34.4 2.5 %collective-permute-start.7 = (f32[128,1536]{1,0:T(8,128)S(1)}, f32[128,1536]{1,0:T(8,128)S(1)}, u32[]{:S(2)}, u32[]{:S(2)}) collective-permute-start(f32[128,1536]{1,0:T(8,128)S(1)} %collective-permute-done.4.refs_4_), channel_id=1, source_target_pairs={{0,6},{1,97},{2,0},{3,99},{4,2},{5,101},{6,4},{7,103},{8,14},{9,10... | collective-permute-start | bytes 2359304 | tf_op jit(solution)/shard_map/ppermute | solution.py:231
  36.9 0.0 collective-permute-done.5.refs_5_
  36.9 0.0 collective-permute-start.14
  36.9 4.8 %collective-permute-done.6.refs_6_ = f32[64,1536]{1,0:T(8,128)S(1)} collective-permute-done((f32[64,1536]{1,0:T(8,128)S(1)}, f32[64,1536]{1,0:T(8,128)S(1)}, u32[]{:S(2)}, u32[]{:S(2)}) %collective-permute-start.6) | collective-permute-done | bytes 393248 | tf_op jit(solution)/shard_map/ppermute | solution.py:231
  41.7 0.0 collective-permute-start.12
  41.7 0.0 collective-permute-done.14.refs_14_
  41.7 0.5 collective-permute-start.10
  42.2 0.0 collective-permute-done.13.refs_13_
  42.2 0.1 collective-permute-start.11
  42.3 4.5 %collective-permute-done.8.refs_8_ = f32[128,1536]{1,0:T(8,128)S(1)} collective-permute-done((f32[128,1536]{1,0:T(8,128)S(1)}, f32[128,1536]{1,0:T(8,128)S(1)}, u32[]{:S(2)}, u32[]{:S(2)}) %collective-permute-start.8) | collective-permute-done | bytes 786464 | tf_op jit(solution)/shard_map/ppermute | solution.py:231
  46.8 0.0 collective-permute-start.17
  46.8 0.0 collective-permute-done.7.refs_7_
  46.8 0.5 collective-permute-start.16
  47.3 0.0 collective-permute-done.12.refs_12_
  47.3 0.3 collective-permute-start.15
  47.6 0.0 collective-permute-done.11.refs_11_
  47.6 3.2 %collective-permute-done.15.refs_15_ = f32[64,1536]{1,0:T(8,128)S(1)} collective-permute-done((f32[64,1536]{1,0:T(8,128)S(1)}, f32[64,1536]{1,0:T(8,128)S(1)}, u32[]{:S(2)}, u32[]{:S(2)}) %collective-permute-start.15) | collective-permute-done | bytes 393248 | tf_op jit(solution)/shard_map/ppermute | solution.py:30
  50.8 0.0 collective-permute-done.10.refs_10_
  50.8 0.0 collective-permute-done.17.refs_17_
  50.8 0.0 collective-permute-done.16.refs_16_
  50.8 13.9 %tile.1 = (f32[1024,512]{1,0:T(8,128)}, f32[2,64,512]{2,1,0:T(8,128)S(1)}, f32[2,64,512]{2,1,0:T(8,128)S(1)}, f32[2,64,512]{2,1,0:T(8,128)S(1)}, f32[2,64,512]{2...) custom-call(f32[128,1536]{1,0:T(8,128)S(1)} %constant_dynamic-update, ...), custom_call_target="tpu_custom_call" | custom-call | flops 8000000000 | bytes 20000000 | tf_op jit(solution)/shard_map/tile/pallas_call | solution.py:185
  64.7 0.1 collective-permute-start.18
  64.8 1.3 %collective-permute-start.23 = (f32[2,64,512]{2,1,0:T(8,128)S(1)}, f32[2,64,512]{2,1,0:T(8,128)S(1)}, u32[]{:S(2)}, u32[]{:S(2)}) collective-permute-start(f32[2,64,512]{2,1,0:T(8,128)S(1)} %get-tuple-element.24), channel_id=1, source_target_pairs={{0,64},{16,80},{32,96},{48,112},{64,0},{80,16},{96,32},{112,48},{1... | collective-permute-start | bytes 786440 | tf_op jit(solution)/shard_map/ppermute | solution.py:34
  66.2 0.7 collective-permute-start.24
  66.9 2.6 %collective-permute-start.25 = (f32[2,64,512]{2,1,0:T(8,128)S(1)}, f32[2,64,512]{2,1,0:T(8,128)S(1)}, u32[]{:S(2)}, u32[]{:S(2)}) collective-permute-start(f32[2,64,512]{2,1,0:T(8,128)S(1)} %get-tuple-element.26), channel_id=1, source_target_pairs={{0,96},{16,112},{32,0},{48,16},{64,32},{80,48},{96,64},{112,80},{1... | collective-permute-start | bytes 786440 | tf_op jit(solution)/shard_map/ppermute | solution.py:34
  69.4 0.0 collective-permute-done.18
  69.4 0.1 slice_add_fusion.2
  69.6 2.6 %collective-permute-start.19 = (f32[2,64,512]{2,1,0:T(8,128)S(1)}, f32[2,64,512]{2,1,0:T(8,128)S(1)}, u32[]{:S(2)}, u32[]{:S(2)}) collective-permute-start(f32[2,64,512]{2,1,0:T(8,128)S(1)} %get-tuple-element.27), channel_id=1, source_target_pairs={{0,4},{1,5},{2,6},{3,7},{4,0},{5,1},{6,2},{7,3},{8,12},{9,13},{10,... | collective-permute-start | bytes 786440 | tf_op jit(solution)/shard_map/ppermute | solution.py:30
  72.1 1.2 %collective-permute-start.21 = (f32[2,64,512]{2,1,0:T(8,128)S(1)}, f32[2,64,512]{2,1,0:T(8,128)S(1)}, u32[]{:S(2)}, u32[]{:S(2)}) collective-permute-start(f32[2,64,512]{2,1,0:T(8,128)S(1)} %get-tuple-element.28), channel_id=1, source_target_pairs={{0,6},{1,7},{2,0},{3,1},{4,2},{5,3},{6,4},{7,5},{8,14},{9,15},{10,... | collective-permute-start | bytes 786440 | tf_op jit(solution)/shard_map/ppermute | solution.py:30
  73.3 2.2 %collective-permute-done.23 = f32[2,64,512]{2,1,0:T(8,128)S(1)} collective-permute-done((f32[2,64,512]{2,1,0:T(8,128)S(1)}, f32[2,64,512]{2,1,0:T(8,128)S(1)}, u32[]{:S(2)}, u32[]{:S(2)}) %collective-permute-start.23) | collective-permute-done | bytes 262176 | tf_op jit(solution)/shard_map/ppermute | solution.py:34
  75.5 0.4 collective-permute-start.20
  75.9 4.6 %collective-permute-done.24 = f32[2,64,512]{2,1,0:T(8,128)S(1)} collective-permute-done((f32[2,64,512]{2,1,0:T(8,128)S(1)}, f32[2,64,512]{2,1,0:T(8,128)S(1)}, u32[]{:S(2)}, u32[]{:S(2)}) %collective-permute-start.24) | collective-permute-done | bytes 262176 | tf_op jit(solution)/shard_map/ppermute | solution.py:34
  80.5 0.1 add_add_fusion
  80.7 1.7 %collective-permute-start.26 = (f32[64,512]{1,0:T(8,128)S(1)}, f32[64,512]{1,0:T(8,128)S(1)}, u32[]{:S(2)}, u32[]{:S(2)}) collective-permute-start(f32[64,512]{1,0:T(8,128)S(1)} %slice_bitcast_fusion), channel_id=1, source_target_pairs={{0,16},{16,0},{32,48},{48,32},{64,80},{80,64},{96,112},{112,96},{1... | collective-permute-start | bytes 393224 | tf_op jit(solution)/shard_map/ppermute | solution.py:34
  82.4 0.0 collective-permute-done.19
  82.4 1.6 %collective-permute-done.21 = f32[2,64,512]{2,1,0:T(8,128)S(1)} collective-permute-done((f32[2,64,512]{2,1,0:T(8,128)S(1)}, f32[2,64,512]{2,1,0:T(8,128)S(1)}, u32[]{:S(2)}, u32[]{:S(2)}) %collective-permute-start.21) | collective-permute-done | bytes 262176 | tf_op jit(solution)/shard_map/ppermute | solution.py:30
  84.0 0.5 collective-permute-done.20
  84.5 0.1 fusion.2
  84.6 1.7 %collective-permute-start.22 = (f32[64,512]{1,0:T(8,128)S(1)}, f32[64,512]{1,0:T(8,128)S(1)}, u32[]{:S(2)}, u32[]{:S(2)}) collective-permute-start(f32[64,512]{1,0:T(8,128)S(1)} %slice_bitcast_fusion.2), channel_id=1, source_target_pairs={{0,8},{1,9},{2,10},{3,11},{4,12},{5,13},{6,14},{7,15},{8,0},{9,1},... | collective-permute-start | bytes 393224 | tf_op jit(solution)/shard_map/ppermute | solution.py:30
  86.3 1.3 %collective-permute-done.26 = f32[64,512]{1,0:T(8,128)S(1)} collective-permute-done((f32[64,512]{1,0:T(8,128)S(1)}, f32[64,512]{1,0:T(8,128)S(1)}, u32[]{:S(2)}, u32[]{:S(2)}) %collective-permute-start.26) | collective-permute-done | bytes 131104 | tf_op jit(solution)/shard_map/ppermute | solution.py:34
  87.7 0.7 fusion.3
  88.3 1.3 %collective-permute-done.22 = f32[64,512]{1,0:T(8,128)S(1)} collective-permute-done((f32[64,512]{1,0:T(8,128)S(1)}, f32[64,512]{1,0:T(8,128)S(1)}, u32[]{:S(2)}, u32[]{:S(2)}) %collective-permute-start.22) | collective-permute-done | bytes 131104 | tf_op jit(solution)/shard_map/ppermute | solution.py:30
  89.7 0.7 fusion.4
  (12 shorter events, 0.1 us)
Async XLA Ops:
  0.6 1.0 %copy-start = (f32[64,1024]{1,0:T(8,128)S(1)}, f32[64,1024]{1,0:T(8,128)}, u32[]{:S(2)}) copy-start(f32[64,1024]{1,0:T(8,128)} %panel_rows.1) | copy-start | bytes 786436
  1.6 0.9 %copy-start.1 = (f32[64,1024]{1,0:T(8,128)S(1)}, f32[64,1024]{1,0:T(8,128)}, u32[]{:S(2)}) copy-start(f32[64,1024]{1,0:T(8,128)} %panel_cols.1) | copy-start | bytes 786436
  2.5 0.9 %copy-start.2 = (f32[64,512]{1,0:T(8,128)S(1)}, f32[64,512]{1,0:T(8,128)}, u32[]{:S(2)}) copy-start(f32[64,512]{1,0:T(8,128)} %feat_rows.1) | copy-start | bytes 393220
  3.4 0.9 %copy-start.3 = (f32[64,512]{1,0:T(8,128)S(1)}, f32[64,512]{1,0:T(8,128)}, u32[]{:S(2)}) copy-start(f32[64,512]{1,0:T(8,128)} %feat_cols.1) | copy-start | bytes 393220
  4.3 46.4 %copy-start.4 = (f32[1024,512]{1,0:T(8,128)S(1)}, f32[1024,512]{1,0:T(8,128)}, u32[]{:S(2)}) copy-start(f32[1024,512]{1,0:T(8,128)} %refs_18_.1) | copy-start | bytes 6291460
  4.5 1.8 %collective-permute-start = (f32[64,1536]{1,0:T(8,128)S(1)}, f32[64,1536]{1,0:T(8,128)S(1)}, u32[]{:S(2)}, u32[]{:S(2)}) collective-permute-start(f32[64,1536]{1,0:T(8,128)S(1)} %get-tuple-element.16), channel_id=1, source_target_pairs={{0,1},{1,0},{2,3},{3,2},{4,5},{5,4},{6,7},{7,6},{8,9},{9,8},{10,11... | collective-permute-start | bytes 1179656 | tf_op jit(solution)/shard_map/ppermute | solution.py:30
  6.3 19.4 %collective-permute-start.4 = (f32[128,1536]{1,0:T(8,128)S(1)}, f32[128,1536]{1,0:T(8,128)S(1)}, u32[]{:S(2)}, u32[]{:S(2)}) collective-permute-start(f32[128,1536]{1,0:T(8,128)S(1)} %constant_dynamic-update-slice_fusion.refs_0_), channel_id=1, source_target_pairs={{0,8},{1,17},{2,10},{3,19},{4,12},{5,21},{6,14},{7,23},{8,0},{9,25... | collective-permute-start | bytes 2359304 | tf_op jit(solution)/shard_map/ppermute | solution.py:231
  8.0 21.8 %collective-permute-start.1 = (f32[128,1536]{1,0:T(8,128)S(1)}, f32[128,1536]{1,0:T(8,128)S(1)}, u32[]{:S(2)}, u32[]{:S(2)}) collective-permute-start(f32[128,1536]{1,0:T(8,128)S(1)} %constant_dynamic-update-slice_fusion.refs_0_), channel_id=1, source_target_pairs={{0,4},{1,65},{2,6},{3,67},{4,0},{5,69},{6,2},{7,71},{8,12},{9,73},... | collective-permute-start | bytes 2359304 | tf_op jit(solution)/shard_map/ppermute | solution.py:231
  11.9 19.9 %collective-permute-start.9 = (f32[128,1536]{1,0:T(8,128)S(1)}, f32[128,1536]{1,0:T(8,128)S(1)}, u32[]{:S(2)}, u32[]{:S(2)}) collective-permute-start(f32[128,1536]{1,0:T(8,128)S(1)} %constant_dynamic-update-slice_fusion.refs_0_), channel_id=1, source_target_pairs={{0,1},{1,0},{2,3},{3,2},{4,5},{5,4},{6,7},{7,6},{8,9},{9,8},{10,11... | collective-permute-start | bytes 2359304 | tf_op jit(solution)/shard_map/ppermute | solution.py:30
  12.3 20.5 %collective-permute-start.3 = (f32[128,1536]{1,0:T(8,128)S(1)}, f32[128,1536]{1,0:T(8,128)S(1)}, u32[]{:S(2)}, u32[]{:S(2)}) collective-permute-start(f32[128,1536]{1,0:T(8,128)S(1)} %constant_dynamic-update-slice_fusion.refs_0_), channel_id=1, source_target_pairs={{0,2},{1,33},{2,4},{3,35},{4,6},{5,37},{6,0},{7,39},{8,10},{9,41},... | collective-permute-start | bytes 2359304 | tf_op jit(solution)/shard_map/ppermute | solution.py:231
  14.2 20.2 %collective-permute-start.2 = (f32[128,1536]{1,0:T(8,128)S(1)}, f32[128,1536]{1,0:T(8,128)S(1)}, u32[]{:S(2)}, u32[]{:S(2)}) collective-permute-start(f32[128,1536]{1,0:T(8,128)S(1)} %constant_dynamic-update-slice_fusion.refs_0_), channel_id=1, source_target_pairs={{0,6},{1,97},{2,0},{3,99},{4,2},{5,101},{6,4},{7,103},{8,14},{9,10... | collective-permute-start | bytes 2359304 | tf_op jit(solution)/shard_map/ppermute | solution.py:231
  25.7 11.2 %collective-permute-start.5 = (f32[64,1536]{1,0:T(8,128)S(1)}, f32[64,1536]{1,0:T(8,128)S(1)}, u32[]{:S(2)}, u32[]{:S(2)}) collective-permute-start(f32[64,1536]{1,0:T(8,128)S(1)} %slice.40), channel_id=1, source_target_pairs={{0,4},{1,65},{2,6},{3,67},{4,0},{5,69},{6,2},{7,71},{8,12},{9,73},... | collective-permute-start | bytes 1179656 | tf_op jit(solution)/shard_map/ppermute | solution.py:231
  29.9 11.8 %collective-permute-start.6 = (f32[64,1536]{1,0:T(8,128)S(1)}, f32[64,1536]{1,0:T(8,128)S(1)}, u32[]{:S(2)}, u32[]{:S(2)}) collective-permute-start(f32[64,1536]{1,0:T(8,128)S(1)} %slice.41), channel_id=1, source_target_pairs={{0,8},{1,17},{2,10},{3,19},{4,12},{5,21},{6,14},{7,23},{8,0},{9,25... | collective-permute-start | bytes 1179656 | tf_op jit(solution)/shard_map/ppermute | solution.py:231
  31.8 10.4 %collective-permute-start.13 = (f32[128,1536]{1,0:T(8,128)S(1)}, f32[128,1536]{1,0:T(8,128)S(1)}, u32[]{:S(2)}, u32[]{:S(2)}) collective-permute-start(f32[128,1536]{1,0:T(8,128)S(1)} %collective-permute-done.4.refs_4_), channel_id=1, source_target_pairs={{0,1},{1,0},{2,3},{3,2},{4,5},{5,4},{6,7},{7,6},{8,9},{9,8},{10,11... | collective-permute-start | bytes 2359304 | tf_op jit(solution)/shard_map/ppermute | solution.py:30
  32.8 14.0 %collective-permute-start.8 = (f32[128,1536]{1,0:T(8,128)S(1)}, f32[128,1536]{1,0:T(8,128)S(1)}, u32[]{:S(2)}, u32[]{:S(2)}) collective-permute-start(f32[128,1536]{1,0:T(8,128)S(1)} %collective-permute-done.4.refs_4_), channel_id=1, source_target_pairs={{0,2},{1,33},{2,4},{3,35},{4,6},{5,37},{6,0},{7,39},{8,10},{9,41},... | collective-permute-start | bytes 2359304 | tf_op jit(solution)/shard_map/ppermute | solution.py:231
  34.4 12.4 %collective-permute-start.7 = (f32[128,1536]{1,0:T(8,128)S(1)}, f32[128,1536]{1,0:T(8,128)S(1)}, u32[]{:S(2)}, u32[]{:S(2)}) collective-permute-start(f32[128,1536]{1,0:T(8,128)S(1)} %collective-permute-done.4.refs_4_), channel_id=1, source_target_pairs={{0,6},{1,97},{2,0},{3,99},{4,2},{5,101},{6,4},{7,103},{8,14},{9,10... | collective-permute-start | bytes 2359304 | tf_op jit(solution)/shard_map/ppermute | solution.py:231
  36.9 4.8 %collective-permute-start.14 = (f32[64,1536]{1,0:T(8,128)S(1)}, f32[64,1536]{1,0:T(8,128)S(1)}, u32[]{:S(2)}, u32[]{:S(2)}) collective-permute-start(f32[64,1536]{1,0:T(8,128)S(1)} %collective-permute-done.5.refs_5_), channel_id=1, source_target_pairs={{0,1},{1,0},{2,3},{3,2},{4,5},{5,4},{6,7},{7,6},{8,9},{9,8},{10,11... | collective-permute-start | bytes 1179656 | tf_op jit(solution)/shard_map/ppermute | solution.py:30
  41.7 5.6 %collective-permute-start.12 = (f32[128,1536]{1,0:T(8,128)S(1)}, f32[128,1536]{1,0:T(8,128)S(1)}, u32[]{:S(2)}, u32[]{:S(2)}) collective-permute-start(f32[128,1536]{1,0:T(8,128)S(1)} %collective-permute-done.3.refs_3_), channel_id=1, source_target_pairs={{0,1},{1,0},{2,3},{3,2},{4,5},{5,4},{6,7},{7,6},{8,9},{9,8},{10,11... | collective-permute-start | bytes 2359304 | tf_op jit(solution)/shard_map/ppermute | solution.py:30
  41.7 9.0 %collective-permute-start.10 = (f32[128,1536]{1,0:T(8,128)S(1)}, f32[128,1536]{1,0:T(8,128)S(1)}, u32[]{:S(2)}, u32[]{:S(2)}) collective-permute-start(f32[128,1536]{1,0:T(8,128)S(1)} %collective-permute-done.1.refs_1_), channel_id=1, source_target_pairs={{0,1},{1,0},{2,3},{3,2},{4,5},{5,4},{6,7},{7,6},{8,9},{9,8},{10,11... | collective-permute-start | bytes 2359304 | tf_op jit(solution)/shard_map/ppermute | solution.py:30
  42.2 5.3 %collective-permute-start.11 = (f32[128,1536]{1,0:T(8,128)S(1)}, f32[128,1536]{1,0:T(8,128)S(1)}, u32[]{:S(2)}, u32[]{:S(2)}) collective-permute-start(f32[128,1536]{1,0:T(8,128)S(1)} %collective-permute-done.2.refs_2_), channel_id=1, source_target_pairs={{0,1},{1,0},{2,3},{3,2},{4,5},{5,4},{6,7},{7,6},{8,9},{9,8},{10,11... | collective-permute-start | bytes 2359304 | tf_op jit(solution)/shard_map/ppermute | solution.py:30
  46.8 4.0 %collective-permute-start.17 = (f32[128,1536]{1,0:T(8,128)S(1)}, f32[128,1536]{1,0:T(8,128)S(1)}, u32[]{:S(2)}, u32[]{:S(2)}) collective-permute-start(f32[128,1536]{1,0:T(8,128)S(1)} %collective-permute-done.8.refs_8_), channel_id=1, source_target_pairs={{0,1},{1,0},{2,3},{3,2},{4,5},{5,4},{6,7},{7,6},{8,9},{9,8},{10,11... | collective-permute-start | bytes 2359304 | tf_op jit(solution)/shard_map/ppermute | solution.py:30
  46.8 4.0 %collective-permute-start.16 = (f32[128,1536]{1,0:T(8,128)S(1)}, f32[128,1536]{1,0:T(8,128)S(1)}, u32[]{:S(2)}, u32[]{:S(2)}) collective-permute-start(f32[128,1536]{1,0:T(8,128)S(1)} %collective-permute-done.7.refs_7_), channel_id=1, source_target_pairs={{0,1},{1,0},{2,3},{3,2},{4,5},{5,4},{6,7},{7,6},{8,9},{9,8},{10,11... | collective-permute-start | bytes 2359304 | tf_op jit(solution)/shard_map/ppermute | solution.py:30
  47.3 3.5 %collective-permute-start.15 = (f32[64,1536]{1,0:T(8,128)S(1)}, f32[64,1536]{1,0:T(8,128)S(1)}, u32[]{:S(2)}, u32[]{:S(2)}) collective-permute-start(f32[64,1536]{1,0:T(8,128)S(1)} %collective-permute-done.6.refs_6_), channel_id=1, source_target_pairs={{0,1},{1,0},{2,3},{3,2},{4,5},{5,4},{6,7},{7,6},{8,9},{9,8},{10,11... | collective-permute-start | bytes 1179656 | tf_op jit(solution)/shard_map/ppermute | solution.py:30
  64.7 4.7 %collective-permute-start.18 = (f32[8,64,512]{2,1,0:T(8,128)S(1)}, f32[8,64,512]{2,1,0:T(8,128)S(1)}, u32[]{:S(2)}, u32[]{:S(2)}) collective-permute-start(f32[8,64,512]{2,1,0:T(8,128)S(1)} %get-tuple-element.19), channel_id=1, source_target_pairs={{0,1},{1,0},{2,3},{3,2},{4,5},{5,4},{6,7},{7,6},{8,9},{9,8},{10,11... | collective-permute-start | bytes 3145736 | tf_op jit(solution)/shard_map/ppermute | solution.py:30
  64.8 10.7 %collective-permute-start.23 = (f32[2,64,512]{2,1,0:T(8,128)S(1)}, f32[2,64,512]{2,1,0:T(8,128)S(1)}, u32[]{:S(2)}, u32[]{:S(2)}) collective-permute-start(f32[2,64,512]{2,1,0:T(8,128)S(1)} %get-tuple-element.24), channel_id=1, source_target_pairs={{0,64},{16,80},{32,96},{48,112},{64,0},{80,16},{96,32},{112,48},{1... | collective-permute-start | bytes 786440 | tf_op jit(solution)/shard_map/ppermute | solution.py:34
  66.2 14.3 %collective-permute-start.24 = (f32[2,64,512]{2,1,0:T(8,128)S(1)}, f32[2,64,512]{2,1,0:T(8,128)S(1)}, u32[]{:S(2)}, u32[]{:S(2)}) collective-permute-start(f32[2,64,512]{2,1,0:T(8,128)S(1)} %get-tuple-element.25), channel_id=1, source_target_pairs={{0,32},{16,48},{32,64},{48,80},{64,96},{80,112},{96,0},{112,16},{1... | collective-permute-start | bytes 786440 | tf_op jit(solution)/shard_map/ppermute | solution.py:34
  66.9 13.7 %collective-permute-start.25 = (f32[2,64,512]{2,1,0:T(8,128)S(1)}, f32[2,64,512]{2,1,0:T(8,128)S(1)}, u32[]{:S(2)}, u32[]{:S(2)}) collective-permute-start(f32[2,64,512]{2,1,0:T(8,128)S(1)} %get-tuple-element.26), channel_id=1, source_target_pairs={{0,96},{16,112},{32,0},{48,16},{64,32},{80,48},{96,64},{112,80},{1... | collective-permute-start | bytes 786440 | tf_op jit(solution)/shard_map/ppermute | solution.py:34
  69.6 12.8 %collective-permute-start.19 = (f32[2,64,512]{2,1,0:T(8,128)S(1)}, f32[2,64,512]{2,1,0:T(8,128)S(1)}, u32[]{:S(2)}, u32[]{:S(2)}) collective-permute-start(f32[2,64,512]{2,1,0:T(8,128)S(1)} %get-tuple-element.27), channel_id=1, source_target_pairs={{0,4},{1,5},{2,6},{3,7},{4,0},{5,1},{6,2},{7,3},{8,12},{9,13},{10,... | collective-permute-start | bytes 786440 | tf_op jit(solution)/shard_map/ppermute | solution.py:30
  72.1 11.9 %collective-permute-start.21 = (f32[2,64,512]{2,1,0:T(8,128)S(1)}, f32[2,64,512]{2,1,0:T(8,128)S(1)}, u32[]{:S(2)}, u32[]{:S(2)}) collective-permute-start(f32[2,64,512]{2,1,0:T(8,128)S(1)} %get-tuple-element.28), channel_id=1, source_target_pairs={{0,6},{1,7},{2,0},{3,1},{4,2},{5,3},{6,4},{7,5},{8,14},{9,15},{10,... | collective-permute-start | bytes 786440 | tf_op jit(solution)/shard_map/ppermute | solution.py:30
  75.5 9.0 %collective-permute-start.20 = (f32[2,64,512]{2,1,0:T(8,128)S(1)}, f32[2,64,512]{2,1,0:T(8,128)S(1)}, u32[]{:S(2)}, u32[]{:S(2)}) collective-permute-start(f32[2,64,512]{2,1,0:T(8,128)S(1)} %get-tuple-element.29), channel_id=1, source_target_pairs={{0,2},{1,3},{2,4},{3,5},{4,6},{5,7},{6,0},{7,1},{8,10},{9,11},{10,... | collective-permute-start | bytes 786440 | tf_op jit(solution)/shard_map/ppermute | solution.py:30
  80.7 7.0 %collective-permute-start.26 = (f32[64,512]{1,0:T(8,128)S(1)}, f32[64,512]{1,0:T(8,128)S(1)}, u32[]{:S(2)}, u32[]{:S(2)}) collective-permute-start(f32[64,512]{1,0:T(8,128)S(1)} %slice_bitcast_fusion), channel_id=1, source_target_pairs={{0,16},{16,0},{32,48},{48,32},{64,80},{80,64},{96,112},{112,96},{1... | collective-permute-start | bytes 393224 | tf_op jit(solution)/shard_map/ppermute | solution.py:34
  84.6 5.0 %collective-permute-start.22 = (f32[64,512]{1,0:T(8,128)S(1)}, f32[64,512]{1,0:T(8,128)S(1)}, u32[]{:S(2)}, u32[]{:S(2)}) collective-permute-start(f32[64,512]{1,0:T(8,128)S(1)} %slice_bitcast_fusion.2), channel_id=1, source_target_pairs={{0,8},{1,9},{2,10},{3,11},{4,12},{5,13},{6,14},{7,15},{8,0},{9,1},... | collective-permute-start | bytes 393224 | tf_op jit(solution)/shard_map/ppermute | solution.py:30

commit v4 on v3

--- a/solution.py
+++ b/solution.py
@@ -11,7 +11,7 @@
 B = 64
 F = 512
 K = 1024
-STEPS = 4
+STEPS = 1
 ROWS = 1024
 COLS = 512
 CHUNK = ROWS // STEPS

time: 90.6 us -> 88.6 us (0.978)
  Pallas kernels: 14 us -> 12 us
    pallas_call x1, Pallas kernels: 13.9 us -> 11.9 us  [tile(): pl.pallas_call(tile_kernel, out_shape=[jax.ShapeDtypeStruct((ROWS, COLS),...]
where the time goes in v4:
time: 88.6 us; the launch traced here: 88.4 us
  waiting for transfers between devices  35.4 us (40%)
  starting transfers between devices  34.7 us (39%)
  Pallas kernels  12 us (14%)
  local copies, waits for them, and re-layouts  3.8 us (4%)
  other arithmetic  1.69 us (2%)
    ppermute x8, starting transfers between devices, over_both(): return lax.ppermute(a, ('row', 'col'), both_perm(flip, shift))  19.8 us
    ppermute x8, waiting for transfers between devices, over_both(): return lax.ppermute(a, ('row', 'col'), both_perm(flip, shift))  18.7 us
    pallas_call x1, Pallas kernels, tile(): pl.pallas_call(tile_kernel, out_shape=[jax.ShapeDtypeStruct((ROWS, COLS),...  11.9 us
    ppermute x15, starting transfers between devices, over_col(): return lax.ppermute(a, 'col', col_perm(dy, dz, dc))  8.61 us
    ppermute x15, waiting for transfers between devices, over_col(): return lax.ppermute(a, 'col', col_perm(dy, dz, dc))  8.58 us
    ppermute x4, waiting for transfers between devices, over_row(): return lax.ppermute(a, 'row', row_perm(dx, dh))  8.18 us
    ppermute x4, starting transfers between devices, over_row(): return lax.ppermute(a, 'row', row_perm(dx, dh))  6.31 us
    unnamed x10, local copies, waits for them, and re-layouts  3.7 us
  transfers between devices with their start and end apart: 27, of which 11 were waited for; matrix products, arithmetic and copies ran while one was open for 1% of the time, Pallas kernels for 0%

profile of v4, /device:TPU:0, one launch (start us, length us, event | category | flops | bytes accessed | tf_op | source)
XLA Modules:
  0.0 88.4 jit_solution(16058238244818873147)
XLA Ops:
  0.6 0.9 %copy-done = f32[64,1024]{1,0:T(8,128)S(1)} copy-done((f32[64,1024]{1,0:T(8,128)S(1)}, f32[64,1024]{1,0:T(8,128)}, u32[]{:S(2)}) %copy-start) | copy-done | bytes 262168
  1.6 0.9 %copy-done.1 = f32[64,1024]{1,0:T(8,128)S(1)} copy-done((f32[64,1024]{1,0:T(8,128)S(1)}, f32[64,1024]{1,0:T(8,128)}, u32[]{:S(2)}) %copy-start.1) | copy-done | bytes 262168
  2.5 0.9 %copy-done.2 = f32[64,512]{1,0:T(8,128)S(1)} copy-done((f32[64,512]{1,0:T(8,128)S(1)}, f32[64,512]{1,0:T(8,128)}, u32[]{:S(2)}) %copy-start.2) | copy-done | bytes 131096
  3.4 0.9 %copy-done.3 = f32[64,512]{1,0:T(8,128)S(1)} copy-done((f32[64,512]{1,0:T(8,128)S(1)}, f32[64,512]{1,0:T(8,128)}, u32[]{:S(2)}) %copy-start.3) | copy-done | bytes 131096
  4.3 0.1 pack.1
  4.5 0.1 collective-permute-start
  4.6 1.7 %collective-permute-done = f32[64,1536]{1,0:T(8,128)S(1)} collective-permute-done((f32[64,1536]{1,0:T(8,128)S(1)}, f32[64,1536]{1,0:T(8,128)S(1)}, u32[]{:S(2)}, u32[]{:S(2)}) %collective-permute-start) | collective-permute-done | bytes 393248 | tf_op jit(solution)/shard_map/ppermute | solution.py:30
  6.3 1.7 %collective-permute-start.4 = (f32[128,1536]{1,0:T(8,128)S(1)}, f32[128,1536]{1,0:T(8,128)S(1)}, u32[]{:S(2)}, u32[]{:S(2)}) collective-permute-start(f32[128,1536]{1,0:T(8,128)S(1)} %constant_dynamic-update-slice_fusion.refs_0_), channel_id=1, source_target_pairs={{0,8},{1,17},{2,10},{3,19},{4,12},{5,21},{6,14},{7,23},{8,0},{9,25... | collective-permute-start | bytes 2359304 | tf_op jit(solution)/shard_map/ppermute | solution.py:231
  8.0 3.9 %collective-permute-start.1 = (f32[128,1536]{1,0:T(8,128)S(1)}, f32[128,1536]{1,0:T(8,128)S(1)}, u32[]{:S(2)}, u32[]{:S(2)}) collective-permute-start(f32[128,1536]{1,0:T(8,128)S(1)} %constant_dynamic-update-slice_fusion.refs_0_), channel_id=1, source_target_pairs={{0,4},{1,65},{2,6},{3,67},{4,0},{5,69},{6,2},{7,71},{8,12},{9,73},... | collective-permute-start | bytes 2359304 | tf_op jit(solution)/shard_map/ppermute | solution.py:231
  11.9 0.3 collective-permute-start.9
  12.3 1.9 %collective-permute-start.3 = (f32[128,1536]{1,0:T(8,128)S(1)}, f32[128,1536]{1,0:T(8,128)S(1)}, u32[]{:S(2)}, u32[]{:S(2)}) collective-permute-start(f32[128,1536]{1,0:T(8,128)S(1)} %constant_dynamic-update-slice_fusion.refs_0_), channel_id=1, source_target_pairs={{0,2},{1,33},{2,4},{3,35},{4,6},{5,37},{6,0},{7,39},{8,10},{9,41},... | collective-permute-start | bytes 2359304 | tf_op jit(solution)/shard_map/ppermute | solution.py:231
  14.2 2.1 %collective-permute-start.2 = (f32[128,1536]{1,0:T(8,128)S(1)}, f32[128,1536]{1,0:T(8,128)S(1)}, u32[]{:S(2)}, u32[]{:S(2)}) collective-permute-start(f32[128,1536]{1,0:T(8,128)S(1)} %constant_dynamic-update-slice_fusion.refs_0_), channel_id=1, source_target_pairs={{0,6},{1,97},{2,0},{3,99},{4,2},{5,101},{6,4},{7,103},{8,14},{9,10... | collective-permute-start | bytes 2359304 | tf_op jit(solution)/shard_map/ppermute | solution.py:231
  16.3 9.4 %collective-permute-done.4.refs_4_ = f32[128,1536]{1,0:T(8,128)S(1)} collective-permute-done((f32[128,1536]{1,0:T(8,128)S(1)}, f32[128,1536]{1,0:T(8,128)S(1)}, u32[]{:S(2)}, u32[]{:S(2)}) %collective-permute-start.4) | collective-permute-done | bytes 786464 | tf_op jit(solution)/shard_map/ppermute | solution.py:231
  25.7 4.1 %collective-permute-start.5 = (f32[64,1536]{1,0:T(8,128)S(1)}, f32[64,1536]{1,0:T(8,128)S(1)}, u32[]{:S(2)}, u32[]{:S(2)}) collective-permute-start(f32[64,1536]{1,0:T(8,128)S(1)} %slice.40), channel_id=1, source_target_pairs={{0,4},{1,65},{2,6},{3,67},{4,0},{5,69},{6,2},{7,71},{8,12},{9,73},... | collective-permute-start | bytes 1179656 | tf_op jit(solution)/shard_map/ppermute | solution.py:231
  29.9 0.0 collective-permute-done.1.refs_1_
  29.9 1.9 %collective-permute-start.6 = (f32[64,1536]{1,0:T(8,128)S(1)}, f32[64,1536]{1,0:T(8,128)S(1)}, u32[]{:S(2)}, u32[]{:S(2)}) collective-permute-start(f32[64,1536]{1,0:T(8,128)S(1)} %slice.41), channel_id=1, source_target_pairs={{0,8},{1,17},{2,10},{3,19},{4,12},{5,21},{6,14},{7,23},{8,0},{9,25... | collective-permute-start | bytes 1179656 | tf_op jit(solution)/shard_map/ppermute | solution.py:231
  31.8 0.0 collective-permute-done.9.refs_9_
  31.8 1.0 %collective-permute-start.13 = (f32[128,1536]{1,0:T(8,128)S(1)}, f32[128,1536]{1,0:T(8,128)S(1)}, u32[]{:S(2)}, u32[]{:S(2)}) collective-permute-start(f32[128,1536]{1,0:T(8,128)S(1)} %collective-permute-done.4.refs_4_), channel_id=1, source_target_pairs={{0,1},{1,0},{2,3},{3,2},{4,5},{5,4},{6,7},{7,6},{8,9},{9,8},{10,11... | collective-permute-start | bytes 2359304 | tf_op jit(solution)/shard_map/ppermute | solution.py:30
  32.8 0.0 collective-permute-done.3.refs_3_
  32.8 1.6 %collective-permute-start.8 = (f32[128,1536]{1,0:T(8,128)S(1)}, f32[128,1536]{1,0:T(8,128)S(1)}, u32[]{:S(2)}, u32[]{:S(2)}) collective-permute-start(f32[128,1536]{1,0:T(8,128)S(1)} %collective-permute-done.4.refs_4_), channel_id=1, source_target_pairs={{0,2},{1,33},{2,4},{3,35},{4,6},{5,37},{6,0},{7,39},{8,10},{9,41},... | collective-permute-start | bytes 2359304 | tf_op jit(solution)/shard_map/ppermute | solution.py:231
  34.4 0.0 collective-permute-done.2.refs_2_
  34.4 2.5 %collective-permute-start.7 = (f32[128,1536]{1,0:T(8,128)S(1)}, f32[128,1536]{1,0:T(8,128)S(1)}, u32[]{:S(2)}, u32[]{:S(2)}) collective-permute-start(f32[128,1536]{1,0:T(8,128)S(1)} %collective-permute-done.4.refs_4_), channel_id=1, source_target_pairs={{0,6},{1,97},{2,0},{3,99},{4,2},{5,101},{6,4},{7,103},{8,14},{9,10... | collective-permute-start | bytes 2359304 | tf_op jit(solution)/shard_map/ppermute | solution.py:231
  36.9 0.0 collective-permute-done.5.refs_5_
  36.9 0.0 collective-permute-start.14
  36.9 4.8 %collective-permute-done.6.refs_6_ = f32[64,1536]{1,0:T(8,128)S(1)} collective-permute-done((f32[64,1536]{1,0:T(8,128)S(1)}, f32[64,1536]{1,0:T(8,128)S(1)}, u32[]{:S(2)}, u32[]{:S(2)}) %collective-permute-start.6) | collective-permute-done | bytes 393248 | tf_op jit(solution)/shard_map/ppermute | solution.py:231
  41.7 0.0 collective-permute-start.12
  41.7 0.0 collective-permute-done.14.refs_14_
  41.7 0.5 collective-permute-start.10
  42.2 0.0 collective-permute-done.13.refs_13_
  42.2 0.1 collective-permute-start.11
  42.3 4.5 %collective-permute-done.8.refs_8_ = f32[128,1536]{1,0:T(8,128)S(1)} collective-permute-done((f32[128,1536]{1,0:T(8,128)S(1)}, f32[128,1536]{1,0:T(8,128)S(1)}, u32[]{:S(2)}, u32[]{:S(2)}) %collective-permute-start.8) | collective-permute-done | bytes 786464 | tf_op jit(solution)/shard_map/ppermute | solution.py:231
  46.8 0.0 collective-permute-start.17
  46.8 0.0 collective-permute-done.7.refs_7_
  46.8 0.5 collective-permute-start.16
  47.3 0.0 collective-permute-done.12.refs_12_
  47.3 0.1 collective-permute-start.15
  47.4 0.0 collective-permute-done.11.refs_11_
  47.4 3.4 %collective-permute-done.15.refs_15_ = f32[64,1536]{1,0:T(8,128)S(1)} collective-permute-done((f32[64,1536]{1,0:T(8,128)S(1)}, f32[64,1536]{1,0:T(8,128)S(1)}, u32[]{:S(2)}, u32[]{:S(2)}) %collective-permute-start.15) | collective-permute-done | bytes 393248 | tf_op jit(solution)/shard_map/ppermute | solution.py:30
  50.8 0.0 collective-permute-done.10.refs_10_
  50.8 0.0 collective-permute-done.17.refs_17_
  50.8 0.0 collective-permute-done.16.refs_16_
  50.8 11.9 %tile.1 = (f32[1024,512]{1,0:T(8,128)}, f32[2,64,512]{2,1,0:T(8,128)S(1)}, f32[2,64,512]{2,1,0:T(8,128)S(1)}, f32[2,64,512]{2,1,0:T(8,128)S(1)}, f32[2,64,512]{2...) custom-call(f32[128,1536]{1,0:T(8,128)S(1)} %constant_dynamic-update, ...), custom_call_target="tpu_custom_call" | custom-call | flops 8000000000 | bytes 20000000 | tf_op jit(solution)/shard_map/tile/pallas_call | solution.py:185
  62.7 0.2 collective-permute-start.18
  62.9 1.4 %collective-permute-start.23 = (f32[2,64,512]{2,1,0:T(8,128)S(1)}, f32[2,64,512]{2,1,0:T(8,128)S(1)}, u32[]{:S(2)}, u32[]{:S(2)}) collective-permute-start(f32[2,64,512]{2,1,0:T(8,128)S(1)} %get-tuple-element.24), channel_id=1, source_target_pairs={{0,64},{16,80},{32,96},{48,112},{64,0},{80,16},{96,32},{112,48},{1... | collective-permute-start | bytes 786440 | tf_op jit(solution)/shard_map/ppermute | solution.py:34
  64.2 0.7 collective-permute-start.24
  64.9 2.6 %collective-permute-start.25 = (f32[2,64,512]{2,1,0:T(8,128)S(1)}, f32[2,64,512]{2,1,0:T(8,128)S(1)}, u32[]{:S(2)}, u32[]{:S(2)}) collective-permute-start(f32[2,64,512]{2,1,0:T(8,128)S(1)} %get-tuple-element.26), channel_id=1, source_target_pairs={{0,96},{16,112},{32,0},{48,16},{64,32},{80,48},{96,64},{112,80},{1... | collective-permute-start | bytes 786440 | tf_op jit(solution)/shard_map/ppermute | solution.py:34
  67.5 0.0 collective-permute-done.18
  67.5 0.1 slice_add_fusion.2
  67.6 2.5 %collective-permute-start.19 = (f32[2,64,512]{2,1,0:T(8,128)S(1)}, f32[2,64,512]{2,1,0:T(8,128)S(1)}, u32[]{:S(2)}, u32[]{:S(2)}) collective-permute-start(f32[2,64,512]{2,1,0:T(8,128)S(1)} %get-tuple-element.27), channel_id=1, source_target_pairs={{0,4},{1,5},{2,6},{3,7},{4,0},{5,1},{6,2},{7,3},{8,12},{9,13},{10,... | collective-permute-start | bytes 786440 | tf_op jit(solution)/shard_map/ppermute | solution.py:30
  70.2 1.2 %collective-permute-start.21 = (f32[2,64,512]{2,1,0:T(8,128)S(1)}, f32[2,64,512]{2,1,0:T(8,128)S(1)}, u32[]{:S(2)}, u32[]{:S(2)}) collective-permute-start(f32[2,64,512]{2,1,0:T(8,128)S(1)} %get-tuple-element.28), channel_id=1, source_target_pairs={{0,6},{1,7},{2,0},{3,1},{4,2},{5,3},{6,4},{7,5},{8,14},{9,15},{10,... | collective-permute-start | bytes 786440 | tf_op jit(solution)/shard_map/ppermute | solution.py:30
  71.4 2.2 %collective-permute-done.23 = f32[2,64,512]{2,1,0:T(8,128)S(1)} collective-permute-done((f32[2,64,512]{2,1,0:T(8,128)S(1)}, f32[2,64,512]{2,1,0:T(8,128)S(1)}, u32[]{:S(2)}, u32[]{:S(2)}) %collective-permute-start.23) | collective-permute-done | bytes 262176 | tf_op jit(solution)/shard_map/ppermute | solution.py:34
  73.6 0.4 collective-permute-start.20
  74.0 4.6 %collective-permute-done.24 = f32[2,64,512]{2,1,0:T(8,128)S(1)} collective-permute-done((f32[2,64,512]{2,1,0:T(8,128)S(1)}, f32[2,64,512]{2,1,0:T(8,128)S(1)}, u32[]{:S(2)}, u32[]{:S(2)}) %collective-permute-start.24) | collective-permute-done | bytes 262176 | tf_op jit(solution)/shard_map/ppermute | solution.py:34
  78.6 0.1 add_add_fusion
  78.7 1.7 %collective-permute-start.26 = (f32[64,512]{1,0:T(8,128)S(1)}, f32[64,512]{1,0:T(8,128)S(1)}, u32[]{:S(2)}, u32[]{:S(2)}) collective-permute-start(f32[64,512]{1,0:T(8,128)S(1)} %slice_bitcast_fusion), channel_id=1, source_target_pairs={{0,16},{16,0},{32,48},{48,32},{64,80},{80,64},{96,112},{112,96},{1... | collective-permute-start | bytes 393224 | tf_op jit(solution)/shard_map/ppermute | solution.py:34
  80.4 0.0 collective-permute-done.19
  80.4 1.6 %collective-permute-done.21 = f32[2,64,512]{2,1,0:T(8,128)S(1)} collective-permute-done((f32[2,64,512]{2,1,0:T(8,128)S(1)}, f32[2,64,512]{2,1,0:T(8,128)S(1)}, u32[]{:S(2)}, u32[]{:S(2)}) %collective-permute-start.21) | collective-permute-done | bytes 262176 | tf_op jit(solution)/shard_map/ppermute | solution.py:30
  82.0 0.5 collective-permute-done.20
  82.5 0.1 fusion.2
  82.7 1.7 %collective-permute-start.22 = (f32[64,512]{1,0:T(8,128)S(1)}, f32[64,512]{1,0:T(8,128)S(1)}, u32[]{:S(2)}, u32[]{:S(2)}) collective-permute-start(f32[64,512]{1,0:T(8,128)S(1)} %slice_bitcast_fusion.2), channel_id=1, source_target_pairs={{0,8},{1,9},{2,10},{3,11},{4,12},{5,13},{6,14},{7,15},{8,0},{9,1},... | collective-permute-start | bytes 393224 | tf_op jit(solution)/shard_map/ppermute | solution.py:30
  84.3 1.4 %collective-permute-done.26 = f32[64,512]{1,0:T(8,128)S(1)} collective-permute-done((f32[64,512]{1,0:T(8,128)S(1)}, f32[64,512]{1,0:T(8,128)S(1)}, u32[]{:S(2)}, u32[]{:S(2)}) %collective-permute-start.26) | collective-permute-done | bytes 131104 | tf_op jit(solution)/shard_map/ppermute | solution.py:34
  85.7 0.7 fusion.3
  86.4 1.3 %collective-permute-done.22 = f32[64,512]{1,0:T(8,128)S(1)} collective-permute-done((f32[64,512]{1,0:T(8,128)S(1)}, f32[64,512]{1,0:T(8,128)S(1)}, u32[]{:S(2)}, u32[]{:S(2)}) %collective-permute-start.22) | collective-permute-done | bytes 131104 | tf_op jit(solution)/shard_map/ppermute | solution.py:30
  87.7 0.7 fusion.4
  (12 shorter events, 0.1 us)
Async XLA Ops:
  0.6 1.0 %copy-start = (f32[64,1024]{1,0:T(8,128)S(1)}, f32[64,1024]{1,0:T(8,128)}, u32[]{:S(2)}) copy-start(f32[64,1024]{1,0:T(8,128)} %panel_rows.1) | copy-start | bytes 786436
  1.6 0.9 %copy-start.1 = (f32[64,1024]{1,0:T(8,128)S(1)}, f32[64,1024]{1,0:T(8,128)}, u32[]{:S(2)}) copy-start(f32[64,1024]{1,0:T(8,128)} %panel_cols.1) | copy-start | bytes 786436
  2.5 0.9 %copy-start.2 = (f32[64,512]{1,0:T(8,128)S(1)}, f32[64,512]{1,0:T(8,128)}, u32[]{:S(2)}) copy-start(f32[64,512]{1,0:T(8,128)} %feat_rows.1) | copy-start | bytes 393220
  3.4 0.9 %copy-start.3 = (f32[64,512]{1,0:T(8,128)S(1)}, f32[64,512]{1,0:T(8,128)}, u32[]{:S(2)}) copy-start(f32[64,512]{1,0:T(8,128)} %feat_cols.1) | copy-start | bytes 393220
  4.3 46.4 %copy-start.4 = (f32[1024,512]{1,0:T(8,128)S(1)}, f32[1024,512]{1,0:T(8,128)}, u32[]{:S(2)}) copy-start(f32[1024,512]{1,0:T(8,128)} %refs_18_.1) | copy-start | bytes 6291460
  4.5 1.8 %collective-permute-start = (f32[64,1536]{1,0:T(8,128)S(1)}, f32[64,1536]{1,0:T(8,128)S(1)}, u32[]{:S(2)}, u32[]{:S(2)}) collective-permute-start(f32[64,1536]{1,0:T(8,128)S(1)} %get-tuple-element.16), channel_id=1, source_target_pairs={{0,1},{1,0},{2,3},{3,2},{4,5},{5,4},{6,7},{7,6},{8,9},{9,8},{10,11... | collective-permute-start | bytes 1179656 | tf_op jit(solution)/shard_map/ppermute | solution.py:30
  6.3 19.4 %collective-permute-start.4 = (f32[128,1536]{1,0:T(8,128)S(1)}, f32[128,1536]{1,0:T(8,128)S(1)}, u32[]{:S(2)}, u32[]{:S(2)}) collective-permute-start(f32[128,1536]{1,0:T(8,128)S(1)} %constant_dynamic-update-slice_fusion.refs_0_), channel_id=1, source_target_pairs={{0,8},{1,17},{2,10},{3,19},{4,12},{5,21},{6,14},{7,23},{8,0},{9,25... | collective-permute-start | bytes 2359304 | tf_op jit(solution)/shard_map/ppermute | solution.py:231
  8.0 21.8 %collective-permute-start.1 = (f32[128,1536]{1,0:T(8,128)S(1)}, f32[128,1536]{1,0:T(8,128)S(1)}, u32[]{:S(2)}, u32[]{:S(2)}) collective-permute-start(f32[128,1536]{1,0:T(8,128)S(1)} %constant_dynamic-update-slice_fusion.refs_0_), channel_id=1, source_target_pairs={{0,4},{1,65},{2,6},{3,67},{4,0},{5,69},{6,2},{7,71},{8,12},{9,73},... | collective-permute-start | bytes 2359304 | tf_op jit(solution)/shard_map/ppermute | solution.py:231
  11.9 19.9 %collective-permute-start.9 = (f32[128,1536]{1,0:T(8,128)S(1)}, f32[128,1536]{1,0:T(8,128)S(1)}, u32[]{:S(2)}, u32[]{:S(2)}) collective-permute-start(f32[128,1536]{1,0:T(8,128)S(1)} %constant_dynamic-update-slice_fusion.refs_0_), channel_id=1, source_target_pairs={{0,1},{1,0},{2,3},{3,2},{4,5},{5,4},{6,7},{7,6},{8,9},{9,8},{10,11... | collective-permute-start | bytes 2359304 | tf_op jit(solution)/shard_map/ppermute | solution.py:30
  12.3 20.5 %collective-permute-start.3 = (f32[128,1536]{1,0:T(8,128)S(1)}, f32[128,1536]{1,0:T(8,128)S(1)}, u32[]{:S(2)}, u32[]{:S(2)}) collective-permute-start(f32[128,1536]{1,0:T(8,128)S(1)} %constant_dynamic-update-slice_fusion.refs_0_), channel_id=1, source_target_pairs={{0,2},{1,33},{2,4},{3,35},{4,6},{5,37},{6,0},{7,39},{8,10},{9,41},... | collective-permute-start | bytes 2359304 | tf_op jit(solution)/shard_map/ppermute | solution.py:231
  14.2 20.2 %collective-permute-start.2 = (f32[128,1536]{1,0:T(8,128)S(1)}, f32[128,1536]{1,0:T(8,128)S(1)}, u32[]{:S(2)}, u32[]{:S(2)}) collective-permute-start(f32[128,1536]{1,0:T(8,128)S(1)} %constant_dynamic-update-slice_fusion.refs_0_), channel_id=1, source_target_pairs={{0,6},{1,97},{2,0},{3,99},{4,2},{5,101},{6,4},{7,103},{8,14},{9,10... | collective-permute-start | bytes 2359304 | tf_op jit(solution)/shard_map/ppermute | solution.py:231
  25.7 11.2 %collective-permute-start.5 = (f32[64,1536]{1,0:T(8,128)S(1)}, f32[64,1536]{1,0:T(8,128)S(1)}, u32[]{:S(2)}, u32[]{:S(2)}) collective-permute-start(f32[64,1536]{1,0:T(8,128)S(1)} %slice.40), channel_id=1, source_target_pairs={{0,4},{1,65},{2,6},{3,67},{4,0},{5,69},{6,2},{7,71},{8,12},{9,73},... | collective-permute-start | bytes 1179656 | tf_op jit(solution)/shard_map/ppermute | solution.py:231
  29.9 11.8 %collective-permute-start.6 = (f32[64,1536]{1,0:T(8,128)S(1)}, f32[64,1536]{1,0:T(8,128)S(1)}, u32[]{:S(2)}, u32[]{:S(2)}) collective-permute-start(f32[64,1536]{1,0:T(8,128)S(1)} %slice.41), channel_id=1, source_target_pairs={{0,8},{1,17},{2,10},{3,19},{4,12},{5,21},{6,14},{7,23},{8,0},{9,25... | collective-permute-start | bytes 1179656 | tf_op jit(solution)/shard_map/ppermute | solution.py:231
  31.8 10.4 %collective-permute-start.13 = (f32[128,1536]{1,0:T(8,128)S(1)}, f32[128,1536]{1,0:T(8,128)S(1)}, u32[]{:S(2)}, u32[]{:S(2)}) collective-permute-start(f32[128,1536]{1,0:T(8,128)S(1)} %collective-permute-done.4.refs_4_), channel_id=1, source_target_pairs={{0,1},{1,0},{2,3},{3,2},{4,5},{5,4},{6,7},{7,6},{8,9},{9,8},{10,11... | collective-permute-start | bytes 2359304 | tf_op jit(solution)/shard_map/ppermute | solution.py:30
  32.8 14.0 %collective-permute-start.8 = (f32[128,1536]{1,0:T(8,128)S(1)}, f32[128,1536]{1,0:T(8,128)S(1)}, u32[]{:S(2)}, u32[]{:S(2)}) collective-permute-start(f32[128,1536]{1,0:T(8,128)S(1)} %collective-permute-done.4.refs_4_), channel_id=1, source_target_pairs={{0,2},{1,33},{2,4},{3,35},{4,6},{5,37},{6,0},{7,39},{8,10},{9,41},... | collective-permute-start | bytes 2359304 | tf_op jit(solution)/shard_map/ppermute | solution.py:231
  34.4 12.4 %collective-permute-start.7 = (f32[128,1536]{1,0:T(8,128)S(1)}, f32[128,1536]{1,0:T(8,128)S(1)}, u32[]{:S(2)}, u32[]{:S(2)}) collective-permute-start(f32[128,1536]{1,0:T(8,128)S(1)} %collective-permute-done.4.refs_4_), channel_id=1, source_target_pairs={{0,6},{1,97},{2,0},{3,99},{4,2},{5,101},{6,4},{7,103},{8,14},{9,10... | collective-permute-start | bytes 2359304 | tf_op jit(solution)/shard_map/ppermute | solution.py:231
  36.9 4.8 %collective-permute-start.14 = (f32[64,1536]{1,0:T(8,128)S(1)}, f32[64,1536]{1,0:T(8,128)S(1)}, u32[]{:S(2)}, u32[]{:S(2)}) collective-permute-start(f32[64,1536]{1,0:T(8,128)S(1)} %collective-permute-done.5.refs_5_), channel_id=1, source_target_pairs={{0,1},{1,0},{2,3},{3,2},{4,5},{5,4},{6,7},{7,6},{8,9},{9,8},{10,11... | collective-permute-start | bytes 1179656 | tf_op jit(solution)/shard_map/ppermute | solution.py:30
  41.7 5.6 %collective-permute-start.12 = (f32[128,1536]{1,0:T(8,128)S(1)}, f32[128,1536]{1,0:T(8,128)S(1)}, u32[]{:S(2)}, u32[]{:S(2)}) collective-permute-start(f32[128,1536]{1,0:T(8,128)S(1)} %collective-permute-done.3.refs_3_), channel_id=1, source_target_pairs={{0,1},{1,0},{2,3},{3,2},{4,5},{5,4},{6,7},{7,6},{8,9},{9,8},{10,11... | collective-permute-start | bytes 2359304 | tf_op jit(solution)/shard_map/ppermute | solution.py:30
  41.7 9.0 %collective-permute-start.10 = (f32[128,1536]{1,0:T(8,128)S(1)}, f32[128,1536]{1,0:T(8,128)S(1)}, u32[]{:S(2)}, u32[]{:S(2)}) collective-permute-start(f32[128,1536]{1,0:T(8,128)S(1)} %collective-permute-done.1.refs_1_), channel_id=1, source_target_pairs={{0,1},{1,0},{2,3},{3,2},{4,5},{5,4},{6,7},{7,6},{8,9},{9,8},{10,11... | collective-permute-start | bytes 2359304 | tf_op jit(solution)/shard_map/ppermute | solution.py:30
  42.2 5.1 %collective-permute-start.11 = (f32[128,1536]{1,0:T(8,128)S(1)}, f32[128,1536]{1,0:T(8,128)S(1)}, u32[]{:S(2)}, u32[]{:S(2)}) collective-permute-start(f32[128,1536]{1,0:T(8,128)S(1)} %collective-permute-done.2.refs_2_), channel_id=1, source_target_pairs={{0,1},{1,0},{2,3},{3,2},{4,5},{5,4},{6,7},{7,6},{8,9},{9,8},{10,11... | collective-permute-start | bytes 2359304 | tf_op jit(solution)/shard_map/ppermute | solution.py:30
  46.8 4.0 %collective-permute-start.17 = (f32[128,1536]{1,0:T(8,128)S(1)}, f32[128,1536]{1,0:T(8,128)S(1)}, u32[]{:S(2)}, u32[]{:S(2)}) collective-permute-start(f32[128,1536]{1,0:T(8,128)S(1)} %collective-permute-done.8.refs_8_), channel_id=1, source_target_pairs={{0,1},{1,0},{2,3},{3,2},{4,5},{5,4},{6,7},{7,6},{8,9},{9,8},{10,11... | collective-permute-start | bytes 2359304 | tf_op jit(solution)/shard_map/ppermute | solution.py:30
  46.8 4.0 %collective-permute-start.16 = (f32[128,1536]{1,0:T(8,128)S(1)}, f32[128,1536]{1,0:T(8,128)S(1)}, u32[]{:S(2)}, u32[]{:S(2)}) collective-permute-start(f32[128,1536]{1,0:T(8,128)S(1)} %collective-permute-done.7.refs_7_), channel_id=1, source_target_pairs={{0,1},{1,0},{2,3},{3,2},{4,5},{5,4},{6,7},{7,6},{8,9},{9,8},{10,11... | collective-permute-start | bytes 2359304 | tf_op jit(solution)/shard_map/ppermute | solution.py:30
  47.3 3.5 %collective-permute-start.15 = (f32[64,1536]{1,0:T(8,128)S(1)}, f32[64,1536]{1,0:T(8,128)S(1)}, u32[]{:S(2)}, u32[]{:S(2)}) collective-permute-start(f32[64,1536]{1,0:T(8,128)S(1)} %collective-permute-done.6.refs_6_), channel_id=1, source_target_pairs={{0,1},{1,0},{2,3},{3,2},{4,5},{5,4},{6,7},{7,6},{8,9},{9,8},{10,11... | collective-permute-start | bytes 1179656 | tf_op jit(solution)/shard_map/ppermute | solution.py:30
  62.7 4.8 %collective-permute-start.18 = (f32[8,64,512]{2,1,0:T(8,128)S(1)}, f32[8,64,512]{2,1,0:T(8,128)S(1)}, u32[]{:S(2)}, u32[]{:S(2)}) collective-permute-start(f32[8,64,512]{2,1,0:T(8,128)S(1)} %get-tuple-element.19), channel_id=1, source_target_pairs={{0,1},{1,0},{2,3},{3,2},{4,5},{5,4},{6,7},{7,6},{8,9},{9,8},{10,11... | collective-permute-start | bytes 3145736 | tf_op jit(solution)/shard_map/ppermute | solution.py:30
  62.9 10.7 %collective-permute-start.23 = (f32[2,64,512]{2,1,0:T(8,128)S(1)}, f32[2,64,512]{2,1,0:T(8,128)S(1)}, u32[]{:S(2)}, u32[]{:S(2)}) collective-permute-start(f32[2,64,512]{2,1,0:T(8,128)S(1)} %get-tuple-element.24), channel_id=1, source_target_pairs={{0,64},{16,80},{32,96},{48,112},{64,0},{80,16},{96,32},{112,48},{1... | collective-permute-start | bytes 786440 | tf_op jit(solution)/shard_map/ppermute | solution.py:34
  64.2 14.4 %collective-permute-start.24 = (f32[2,64,512]{2,1,0:T(8,128)S(1)}, f32[2,64,512]{2,1,0:T(8,128)S(1)}, u32[]{:S(2)}, u32[]{:S(2)}) collective-permute-start(f32[2,64,512]{2,1,0:T(8,128)S(1)} %get-tuple-element.25), channel_id=1, source_target_pairs={{0,32},{16,48},{32,64},{48,80},{64,96},{80,112},{96,0},{112,16},{1... | collective-permute-start | bytes 786440 | tf_op jit(solution)/shard_map/ppermute | solution.py:34
  64.9 13.7 %collective-permute-start.25 = (f32[2,64,512]{2,1,0:T(8,128)S(1)}, f32[2,64,512]{2,1,0:T(8,128)S(1)}, u32[]{:S(2)}, u32[]{:S(2)}) collective-permute-start(f32[2,64,512]{2,1,0:T(8,128)S(1)} %get-tuple-element.26), channel_id=1, source_target_pairs={{0,96},{16,112},{32,0},{48,16},{64,32},{80,48},{96,64},{112,80},{1... | collective-permute-start | bytes 786440 | tf_op jit(solution)/shard_map/ppermute | solution.py:34
  67.6 12.8 %collective-permute-start.19 = (f32[2,64,512]{2,1,0:T(8,128)S(1)}, f32[2,64,512]{2,1,0:T(8,128)S(1)}, u32[]{:S(2)}, u32[]{:S(2)}) collective-permute-start(f32[2,64,512]{2,1,0:T(8,128)S(1)} %get-tuple-element.27), channel_id=1, source_target_pairs={{0,4},{1,5},{2,6},{3,7},{4,0},{5,1},{6,2},{7,3},{8,12},{9,13},{10,... | collective-permute-start | bytes 786440 | tf_op jit(solution)/shard_map/ppermute | solution.py:30
  70.2 11.9 %collective-permute-start.21 = (f32[2,64,512]{2,1,0:T(8,128)S(1)}, f32[2,64,512]{2,1,0:T(8,128)S(1)}, u32[]{:S(2)}, u32[]{:S(2)}) collective-permute-start(f32[2,64,512]{2,1,0:T(8,128)S(1)} %get-tuple-element.28), channel_id=1, source_target_pairs={{0,6},{1,7},{2,0},{3,1},{4,2},{5,3},{6,4},{7,5},{8,14},{9,15},{10,... | collective-permute-start | bytes 786440 | tf_op jit(solution)/shard_map/ppermute | solution.py:30
  73.6 9.0 %collective-permute-start.20 = (f32[2,64,512]{2,1,0:T(8,128)S(1)}, f32[2,64,512]{2,1,0:T(8,128)S(1)}, u32[]{:S(2)}, u32[]{:S(2)}) collective-permute-start(f32[2,64,512]{2,1,0:T(8,128)S(1)} %get-tuple-element.29), channel_id=1, source_target_pairs={{0,2},{1,3},{2,4},{3,5},{4,6},{5,7},{6,0},{7,1},{8,10},{9,11},{10,... | collective-permute-start | bytes 786440 | tf_op jit(solution)/shard_map/ppermute | solution.py:30
  78.7 7.0 %collective-permute-start.26 = (f32[64,512]{1,0:T(8,128)S(1)}, f32[64,512]{1,0:T(8,128)S(1)}, u32[]{:S(2)}, u32[]{:S(2)}) collective-permute-start(f32[64,512]{1,0:T(8,128)S(1)} %slice_bitcast_fusion), channel_id=1, source_target_pairs={{0,16},{16,0},{32,48},{48,32},{64,80},{80,64},{96,112},{112,96},{1... | collective-permute-start | bytes 393224 | tf_op jit(solution)/shard_map/ppermute | solution.py:34
  82.7 5.0 %collective-permute-start.22 = (f32[64,512]{1,0:T(8,128)S(1)}, f32[64,512]{1,0:T(8,128)S(1)}, u32[]{:S(2)}, u32[]{:S(2)}) collective-permute-start(f32[64,512]{1,0:T(8,128)S(1)} %slice_bitcast_fusion.2), channel_id=1, source_target_pairs={{0,8},{1,9},{2,10},{3,11},{4,12},{5,13},{6,14},{7,15},{8,0},{9,1},... | collective-permute-start | bytes 393224 | tf_op jit(solution)/shard_map/ppermute | solution.py:30

commit v5 on v4

--- a/solution.py
+++ b/solution.py
@@ -11,10 +11,8 @@
 B = 64
 F = 512
 K = 1024
-STEPS = 1
 ROWS = 1024
 COLS = 512
-CHUNK = ROWS // STEPS
 SHIFTS = (0, 2, 1, 3)
 
 
@@ -53,7 +51,6 @@
 
 f32, bf16 = jnp.float32, jnp.bfloat16
 whole = pl.BlockSpec(memory_space=pltpu.VMEM)
-block = pl.BlockSpec((CHUNK, COLS), lambda i: (i, 0))
 W = F + K
 
 
@@ -86,8 +83,8 @@
         return [
             pltpu.make_async_copy(other[0], give.at[:, :F], sems.at[0]),
             pltpu.make_async_copy(other[1], give.at[:, F:], sems.at[1]),
-            pltpu.make_async_copy(mine[0], keep.at[:B, :F], sems.at[2]),
-            pltpu.make_async_copy(mine[1], keep.at[:B, F:], sems.at[3]),
+            pltpu.make_async_copy(mine[0], keep.at[:, :F], sems.at[2]),
+            pltpu.make_async_copy(mine[1], keep.at[:, F:], sems.at[3]),
         ]
 
     rows, cols = (feat_rows, panel_rows), (feat_cols, panel_cols)
@@ -106,7 +103,7 @@
 def pack(*shards):
     return pl.pallas_call(
         pack_kernel,
-        out_shape=[jax.ShapeDtypeStruct((2 * B, W), f32), jax.ShapeDtypeStruct((B, W), f32)],
+        out_shape=[jax.ShapeDtypeStruct((B, W), f32)] * 2,
         in_specs=[anywhere] * 4,
         out_specs=[whole] * 2,
         scratch_shapes=[pltpu.SemaphoreType.DMA((4,))],
@@ -116,68 +113,60 @@
     )(*shards)
 
 
-PACK_VMEM = 4
+PACK_VMEM = 60
+
+
+def put(a, at, hi, lo, norm):
+    hi[at, :], lo[at, :] = split(a)
+    a = a[:, :F]
+    norm[at, :] = jnp.broadcast_to(jnp.sum(a * a, axis=1, keepdims=True), (a.shape[0], 128))
 
 
 def tile_kernel(*refs):
-    place = places()
     native, swapped, acc, acc_new = refs[:9], refs[9:18], refs[18], refs[19]
     own_out, sib_out, col_out = refs[20:24], refs[24], refs[25:29]
-    rh, rl, rf, ch, cl, cf, nr, nc, row_term, col_term, tsum = refs[29:]
-    step = pl.program_id(0)
-
-    def put(a, at, hi, lo, feat, norm):
-        hi[at, :], lo[at, :] = split(a)
-        a = a[:, :F]
-        feat[at, :] = a
-        norm[at, :] = jnp.broadcast_to(jnp.sum(a * a, axis=1, keepdims=True), (a.shape[0], 128))
-
-    @pl.when(step == 0)
-    def _():
-        def prepare(row_source, col_source, start):
-            for n in range(8):
-                at = place[1 + n] * B
-                col_at = pl.ds(pl.multiple_of(place[9 + n] * B, B), B)
-                if n == HALVED:
-                    for half in range(2):
-                        put(row_source[n + half][...], pl.ds(pl.multiple_of(at + half * B, B), B), rh, rl, rf, nr)
-                    put(col_source[n + start // B][...], col_at, ch, cl, cf, nc)
-                    continue
-                k = n + (n > HALVED)
-                put(row_source[k][...], pl.ds(pl.multiple_of(at, 2 * B), 2 * B), rh, rl, rf, nr)
-                put(col_source[k][start : start + B, :], col_at, ch, cl, cf, nc)
-
-        pl.when(place[0] == 0)(lambda: prepare(native, swapped, B))
-        pl.when(place[0] == 1)(lambda: prepare(swapped, native, 0))
-        col_term[...] = jnp.zeros_like(col_term)
-        tsum[...] = jnp.zeros_like(tsum)
-
-    at = pl.ds(pl.multiple_of(step * CHUNK, CHUNK), CHUNK)
-    grams = acc[...] + dot3(rh[at, F:], rl[at, F:], ch[:, F:], cl[:, F:], NT)
+    rh, rl, nr, ch, cl, nc, row_term, col_term = refs[29:]
+    place = places()
+    def prepare(row_source, col_source, start):
+        for n in range(8):
+            k = n + (n > HALVED)
+            at = place[1 + n] * B
+            col_at = pl.ds(pl.multiple_of(place[9 + n] * B, B), B)
+            if n == HALVED:
+                for half in range(2):
+                    put(row_source[k + half][...], pl.ds(pl.multiple_of(at + half * B, B), B), rh, rl, nr)
+                put(col_source[k + start // B][...], col_at, ch, cl, nc)
+                continue
+            put(row_source[k][...], pl.ds(pl.multiple_of(at, 2 * B), 2 * B), rh, rl, nr)
+            put(col_source[k][start : start + B, :], col_at, ch, cl, nc)
+
+    pl.when(place[0] == 0)(lambda: prepare(native, swapped, B))
+    pl.when(place[0] == 1)(lambda: prepare(swapped, native, 0))
+
+    def feat(hi, lo):
+        return hi[:, :F].astype(f32) + lo[:, :F].astype(f32)
+
+    grams = acc[...] + dot3(rh[:, F:], rl[:, F:], ch[:, F:], cl[:, F:], NT)
     acc_new[...] = grams
-    cross = dot3(rh[at, :F], rl[at, :F], ch[:, :F], cl[:, :F], NT)
+    cross = dot3(rh[:, :F], rl[:, :F], ch[:, :F], cl[:, :F], NT)
     nc_row = nc[...].T[0:1, :]
-    dist_sq = nr[at, :][:, 0:1] + nc_row - 2.0 * cross
+    dist_sq = nr[:, 0:1] + nc_row - 2.0 * cross
     weights = grams * jnp.exp(-decay_rate * dist_sq)
     wh, wl = split(weights)
     s = jnp.sum(weights, axis=1, keepdims=True)
-    row_term[at, :] = grad_scale * (dot3(wh, wl, ch[:, :F], cl[:, :F], NN) - s * rf[at, :])
-    col_term[...] += dot3(wh, wl, rh[at, :F], rl[at, :F], TN)
-    tsum[...] += jnp.broadcast_to(jnp.sum(weights, axis=0, keepdims=True), (8, COLS))
-
-    @pl.when(step == STEPS - 1)
-    def _():
-        def take(k, src):
-            return src[pl.ds(pl.multiple_of(place[17 + k] * B, B), B), :]
-
-        t = jnp.broadcast_to(tsum[0:1, :], (128, COLS)).T[:, 0:1]
-        col_term[...] = grad_scale * (col_term[...] - t * cf[...])
-        for n in range(4):
-            for d in range(2):
-                k = n * 2 + d
-                own_out[n][d] = take(k, row_term)
-                sib_out[k] = take(8 + k, row_term)
-                col_out[n][d] = take(16 + k, col_term)
+    row_term[...] = grad_scale * (dot3(wh, wl, ch[:, :F], cl[:, :F], NN) - s * feat(rh, rl))
+    t = jnp.broadcast_to(jnp.sum(weights, axis=0, keepdims=True), (128, COLS)).T[:, 0:1]
+    col_term[...] = grad_scale * (dot3(wh, wl, rh[:, :F], rl[:, :F], TN) - t * feat(ch, cl))
+
+    def take(k, src):
+        return src[pl.ds(pl.multiple_of(place[17 + k] * B, B), B), :]
+
+    for n in range(4):
+        for d in range(2):
+            k = n * 2 + d
+            own_out[n][d] = take(k, row_term)
+            sib_out[k] = take(8 + k, row_term)
+            col_out[n][d] = take(16 + k, col_term)
 
 
 def tile(native, swapped, accumulator):
@@ -188,24 +177,18 @@
         + [pair] * 4
         + [jax.ShapeDtypeStruct((8, B, F), f32)]
         + [pair] * 4,
-        grid_spec=pl.GridSpec(
-            grid=(STEPS,),
-            in_specs=[whole] * 18 + [block],
-            out_specs=[block] + [whole] * 9,
-            scratch_shapes=[
-                pltpu.VMEM((ROWS, W), bf16),
-                pltpu.VMEM((ROWS, W), bf16),
-                pltpu.VMEM((ROWS, F), f32),
-                pltpu.VMEM((COLS, W), bf16),
-                pltpu.VMEM((COLS, W), bf16),
-                pltpu.VMEM((COLS, F), f32),
-                pltpu.VMEM((ROWS, 128), f32),
-                pltpu.VMEM((COLS, 128), f32),
-                pltpu.VMEM((ROWS, F), f32),
-                pltpu.VMEM((COLS, F), f32),
-                pltpu.VMEM((8, COLS), f32),
-            ],
-        ),
+        in_specs=[whole] * 19,
+        out_specs=[whole] * 10,
+        scratch_shapes=[
+            pltpu.VMEM((ROWS, W), bf16),
+            pltpu.VMEM((ROWS, W), bf16),
+            pltpu.VMEM((ROWS, 128), f32),
+            pltpu.VMEM((COLS, W), bf16),
+            pltpu.VMEM((COLS, W), bf16),
+            pltpu.VMEM((COLS, 128), f32),
+            pltpu.VMEM((ROWS, F), f32),
+            pltpu.VMEM((COLS, F), f32),
+        ],
         compiler_params=pltpu.CompilerParams(vmem_limit_bytes=TILE_VMEM * 1024 * 1024),
         cost_estimate=pl.CostEstimate(flops=8_000_000_000, bytes_accessed=20_000_000, transcendentals=524288),
         name="tile",
@@ -236,7 +219,7 @@
 
 def gather(shards):
     keep, give = pack(*shards)
-    own = lax.dynamic_update_slice(keep, over_col(give, dc=1), (B, 0))
+    own = jnp.concatenate([keep, over_col(give, dc=1)], axis=0)
     far = over_both(own, flip=1)
     near = [own] + [over_both(own, shift=-d) for d in SHIFTS[1:]]
     other = [far] + [over_both(far, shift=-d) for d in SHIFTS[2:]]

time: 88.6 us -> 87.1 us (0.983)
  local copies, waits for them, and re-layouts: 3.8 us -> 1.13 us
  Pallas kernels: 12 us -> 14 us
    unnamed x10 -> x3, local copies, waits for them, and re-layouts: 3.7 us -> 1.03 us
    pallas_call x1, Pallas kernels: 0.12 us -> 2.23 us  [pack(): pl.pallas_call(pack_kernel, out_shape=[jax.ShapeDtypeStruct((B, W), f32)]...]
  transfers between devices with their start and end apart: 27 -> 27, of which waited for: 11 -> 11; matrix products, arithmetic and copies ran while one was open for 1% -> 2% of each run, Pallas kernels for 0% -> 0%
where the time goes in v5:
time: 87.1 us; the launch traced here: 86.9 us
  starting transfers between devices  34.7 us (40%)
  waiting for transfers between devices  34.6 us (40%)
  Pallas kernels  14 us (16%)
  other arithmetic  1.69 us (2%)
  local copies, waits for them, and re-layouts  1.13 us (1%)
    ppermute x8, starting transfers between devices, over_both(): return lax.ppermute(a, ('row', 'col'), both_perm(flip, shift))  19.8 us
    ppermute x8, waiting for transfers between devices, over_both(): return lax.ppermute(a, ('row', 'col'), both_perm(flip, shift))  18.7 us
    pallas_call x1, Pallas kernels, tile(): pl.pallas_call(tile_kernel, out_shape=[jax.ShapeDtypeStruct((ROWS, COLS),...  11.7 us
    ppermute x15, starting transfers between devices, over_col(): return lax.ppermute(a, 'col', col_perm(dy, dz, dc))  8.6 us
    ppermute x4, waiting for transfers between devices, over_row(): return lax.ppermute(a, 'row', row_perm(dx, dh))  8.18 us
    ppermute x15, waiting for transfers between devices, over_col(): return lax.ppermute(a, 'col', col_perm(dy, dz, dc))  7.76 us
    ppermute x4, starting transfers between devices, over_row(): return lax.ppermute(a, 'row', row_perm(dx, dh))  6.31 us
    pallas_call x1, Pallas kernels, pack(): pl.pallas_call(pack_kernel, out_shape=[jax.ShapeDtypeStruct((B, W), f32)]...  2.23 us
  transfers between devices with their start and end apart: 27, of which 11 were waited for; matrix products, arithmetic and copies ran while one was open for 2% of the time, Pallas kernels for 0%

profile of v5, /device:TPU:0, one launch (start us, length us, event | category | flops | bytes accessed | tf_op | source)
XLA Modules:
  0.0 86.9 jit_solution(6084599312914162445)
XLA Ops:
  0.6 0.0 copy-start
  0.6 2.2 %pack.1 = (f32[64,1536]{1,0:T(8,128)}, f32[64,1536]{1,0:T(8,128)}) custom-call(f32[64,512]{1,0:T(8,128)} %feat_rows.1, f32[64,512]{1,0:T(8,128)} %feat_cols.1, f32[64,1024]{1,0:T(8,128)} %panel_rows.1, f32[64,1024]{1,0:T(8,128)} %panel_cols.1), custom_call_target="tpu_custom_call" | custom-call | bytes 1600000 | tf_op jit(solution)/shard_map/pack/pallas_call | solution.py:104
  2.9 0.1 collective-permute-start
  3.0 1.0 %constant_dynamic-update-slice_fusion.1 = f32[128,1536]{1,0:T(8,128)S(1)} fusion(f32[64,1536]{1,0:T(8,128)} %get-tuple-element.15), kind=kLoop, calls=%fused_computation.15 | loop fusion | bytes 786432
  4.0 0.9 %collective-permute-done = f32[64,1536]{1,0:T(8,128)S(1)} collective-permute-done((f32[64,1536]{1,0:T(8,128)}, f32[64,1536]{1,0:T(8,128)S(1)}, u32[]{:S(2)}, u32[]{:S(2)}) %collective-permute-start) | collective-permute-done | bytes 393248 | tf_op jit(solution)/shard_map/ppermute | solution.py:28
  4.9 1.7 %collective-permute-start.4 = (f32[128,1536]{1,0:T(8,128)S(1)}, f32[128,1536]{1,0:T(8,128)S(1)}, u32[]{:S(2)}, u32[]{:S(2)}) collective-permute-start(f32[128,1536]{1,0:T(8,128)S(1)} %constant_dynamic-update-slice_fusion.refs_0_), channel_id=1, source_target_pairs={{0,8},{1,17},{2,10},{3,19},{4,12},{5,21},{6,14},{7,23},{8,0},{9,25... | collective-permute-start | bytes 2359304 | tf_op jit(solution)/shard_map/ppermute | solution.py:214
  6.7 3.9 %collective-permute-start.1 = (f32[128,1536]{1,0:T(8,128)S(1)}, f32[128,1536]{1,0:T(8,128)S(1)}, u32[]{:S(2)}, u32[]{:S(2)}) collective-permute-start(f32[128,1536]{1,0:T(8,128)S(1)} %constant_dynamic-update-slice_fusion.refs_0_), channel_id=1, source_target_pairs={{0,4},{1,65},{2,6},{3,67},{4,0},{5,69},{6,2},{7,71},{8,12},{9,73},... | collective-permute-start | bytes 2359304 | tf_op jit(solution)/shard_map/ppermute | solution.py:214
  10.5 0.3 collective-permute-start.9
  10.9 1.9 %collective-permute-start.3 = (f32[128,1536]{1,0:T(8,128)S(1)}, f32[128,1536]{1,0:T(8,128)S(1)}, u32[]{:S(2)}, u32[]{:S(2)}) collective-permute-start(f32[128,1536]{1,0:T(8,128)S(1)} %constant_dynamic-update-slice_fusion.refs_0_), channel_id=1, source_target_pairs={{0,2},{1,33},{2,4},{3,35},{4,6},{5,37},{6,0},{7,39},{8,10},{9,41},... | collective-permute-start | bytes 2359304 | tf_op jit(solution)/shard_map/ppermute | solution.py:214
  12.8 2.1 %collective-permute-start.2 = (f32[128,1536]{1,0:T(8,128)S(1)}, f32[128,1536]{1,0:T(8,128)S(1)}, u32[]{:S(2)}, u32[]{:S(2)}) collective-permute-start(f32[128,1536]{1,0:T(8,128)S(1)} %constant_dynamic-update-slice_fusion.refs_0_), channel_id=1, source_target_pairs={{0,6},{1,97},{2,0},{3,99},{4,2},{5,101},{6,4},{7,103},{8,14},{9,10... | collective-permute-start | bytes 2359304 | tf_op jit(solution)/shard_map/ppermute | solution.py:214
  14.9 9.4 %collective-permute-done.4.refs_4_ = f32[128,1536]{1,0:T(8,128)S(1)} collective-permute-done((f32[128,1536]{1,0:T(8,128)S(1)}, f32[128,1536]{1,0:T(8,128)S(1)}, u32[]{:S(2)}, u32[]{:S(2)}) %collective-permute-start.4) | collective-permute-done | bytes 786464 | tf_op jit(solution)/shard_map/ppermute | solution.py:214
  24.3 4.1 %collective-permute-start.5 = (f32[64,1536]{1,0:T(8,128)S(1)}, f32[64,1536]{1,0:T(8,128)S(1)}, u32[]{:S(2)}, u32[]{:S(2)}) collective-permute-start(f32[64,1536]{1,0:T(8,128)S(1)} %slice.40), channel_id=1, source_target_pairs={{0,4},{1,65},{2,6},{3,67},{4,0},{5,69},{6,2},{7,71},{8,12},{9,73},... | collective-permute-start | bytes 1179656 | tf_op jit(solution)/shard_map/ppermute | solution.py:214
  28.5 0.0 collective-permute-done.1.refs_1_
  28.5 1.9 %collective-permute-start.6 = (f32[64,1536]{1,0:T(8,128)S(1)}, f32[64,1536]{1,0:T(8,128)S(1)}, u32[]{:S(2)}, u32[]{:S(2)}) collective-permute-start(f32[64,1536]{1,0:T(8,128)S(1)} %slice.41), channel_id=1, source_target_pairs={{0,8},{1,17},{2,10},{3,19},{4,12},{5,21},{6,14},{7,23},{8,0},{9,25... | collective-permute-start | bytes 1179656 | tf_op jit(solution)/shard_map/ppermute | solution.py:214
  30.4 0.0 collective-permute-done.9.refs_9_
  30.4 1.0 %collective-permute-start.13 = (f32[128,1536]{1,0:T(8,128)S(1)}, f32[128,1536]{1,0:T(8,128)S(1)}, u32[]{:S(2)}, u32[]{:S(2)}) collective-permute-start(f32[128,1536]{1,0:T(8,128)S(1)} %collective-permute-done.4.refs_4_), channel_id=1, source_target_pairs={{0,1},{1,0},{2,3},{3,2},{4,5},{5,4},{6,7},{7,6},{8,9},{9,8},{10,11... | collective-permute-start | bytes 2359304 | tf_op jit(solution)/shard_map/ppermute | solution.py:28
  31.4 0.0 collective-permute-done.3.refs_3_
  31.4 1.6 %collective-permute-start.8 = (f32[128,1536]{1,0:T(8,128)S(1)}, f32[128,1536]{1,0:T(8,128)S(1)}, u32[]{:S(2)}, u32[]{:S(2)}) collective-permute-start(f32[128,1536]{1,0:T(8,128)S(1)} %collective-permute-done.4.refs_4_), channel_id=1, source_target_pairs={{0,2},{1,33},{2,4},{3,35},{4,6},{5,37},{6,0},{7,39},{8,10},{9,41},... | collective-permute-start | bytes 2359304 | tf_op jit(solution)/shard_map/ppermute | solution.py:214
  33.0 0.0 collective-permute-done.2.refs_2_
  33.0 2.5 %collective-permute-start.7 = (f32[128,1536]{1,0:T(8,128)S(1)}, f32[128,1536]{1,0:T(8,128)S(1)}, u32[]{:S(2)}, u32[]{:S(2)}) collective-permute-start(f32[128,1536]{1,0:T(8,128)S(1)} %collective-permute-done.4.refs_4_), channel_id=1, source_target_pairs={{0,6},{1,97},{2,0},{3,99},{4,2},{5,101},{6,4},{7,103},{8,14},{9,10... | collective-permute-start | bytes 2359304 | tf_op jit(solution)/shard_map/ppermute | solution.py:214
  35.5 0.0 collective-permute-done.5.refs_5_
  35.5 0.0 collective-permute-start.14
  35.5 4.8 %collective-permute-done.6.refs_6_ = f32[64,1536]{1,0:T(8,128)S(1)} collective-permute-done((f32[64,1536]{1,0:T(8,128)S(1)}, f32[64,1536]{1,0:T(8,128)S(1)}, u32[]{:S(2)}, u32[]{:S(2)}) %collective-permute-start.6) | collective-permute-done | bytes 393248 | tf_op jit(solution)/shard_map/ppermute | solution.py:214
  40.3 0.0 collective-permute-start.12
  40.3 0.0 collective-permute-done.14.refs_14_
  40.3 0.5 collective-permute-start.10
  40.9 0.0 collective-permute-done.13.refs_13_
  40.9 0.1 collective-permute-start.11
  40.9 4.5 %collective-permute-done.8.refs_8_ = f32[128,1536]{1,0:T(8,128)S(1)} collective-permute-done((f32[128,1536]{1,0:T(8,128)S(1)}, f32[128,1536]{1,0:T(8,128)S(1)}, u32[]{:S(2)}, u32[]{:S(2)}) %collective-permute-start.8) | collective-permute-done | bytes 786464 | tf_op jit(solution)/shard_map/ppermute | solution.py:214
  45.4 0.0 collective-permute-start.17
  45.4 0.0 collective-permute-done.7.refs_7_
  45.4 0.5 collective-permute-start.16
  45.9 0.0 collective-permute-done.12.refs_12_
  45.9 0.1 collective-permute-start.15
  46.0 0.0 collective-permute-done.11.refs_11_
  46.0 3.4 %collective-permute-done.15.refs_15_ = f32[64,1536]{1,0:T(8,128)S(1)} collective-permute-done((f32[64,1536]{1,0:T(8,128)S(1)}, f32[64,1536]{1,0:T(8,128)S(1)}, u32[]{:S(2)}, u32[]{:S(2)}) %collective-permute-start.15) | collective-permute-done | bytes 393248 | tf_op jit(solution)/shard_map/ppermute | solution.py:28
  49.4 0.0 collective-permute-done.10.refs_10_
  49.4 0.0 collective-permute-done.17.refs_17_
  49.4 0.0 collective-permute-done.16.refs_16_
  49.4 0.0 copy-done
  49.4 11.7 %tile.1 = (f32[1024,512]{1,0:T(8,128)}, f32[2,64,512]{2,1,0:T(8,128)S(1)}, f32[2,64,512]{2,1,0:T(8,128)S(1)}, f32[2,64,512]{2,1,0:T(8,128)S(1)}, f32[2,64,512]{2...) custom-call(f32[128,1536]{1,0:T(8,128)S(1)} %constant_dynamic-update, ...), custom_call_target="tpu_custom_call" | custom-call | flops 8000000000 | bytes 20000000 | tf_op jit(solution)/shard_map/tile/pallas_call | solution.py:174
  61.1 0.2 collective-permute-start.18
  61.4 1.4 %collective-permute-start.23 = (f32[2,64,512]{2,1,0:T(8,128)S(1)}, f32[2,64,512]{2,1,0:T(8,128)S(1)}, u32[]{:S(2)}, u32[]{:S(2)}) collective-permute-start(f32[2,64,512]{2,1,0:T(8,128)S(1)} %get-tuple-element.24), channel_id=1, source_target_pairs={{0,64},{16,80},{32,96},{48,112},{64,0},{80,16},{96,32},{112,48},{1... | collective-permute-start | bytes 786440 | tf_op jit(solution)/shard_map/ppermute | solution.py:32
  62.7 0.7 collective-permute-start.24
  63.4 2.6 %collective-permute-start.25 = (f32[2,64,512]{2,1,0:T(8,128)S(1)}, f32[2,64,512]{2,1,0:T(8,128)S(1)}, u32[]{:S(2)}, u32[]{:S(2)}) collective-permute-start(f32[2,64,512]{2,1,0:T(8,128)S(1)} %get-tuple-element.26), channel_id=1, source_target_pairs={{0,96},{16,112},{32,0},{48,16},{64,32},{80,48},{96,64},{112,80},{1... | collective-permute-start | bytes 786440 | tf_op jit(solution)/shard_map/ppermute | solution.py:32
  66.0 0.0 collective-permute-done.18
  66.0 0.1 slice_add_fusion.2
  66.1 2.5 %collective-permute-start.19 = (f32[2,64,512]{2,1,0:T(8,128)S(1)}, f32[2,64,512]{2,1,0:T(8,128)S(1)}, u32[]{:S(2)}, u32[]{:S(2)}) collective-permute-start(f32[2,64,512]{2,1,0:T(8,128)S(1)} %get-tuple-element.27), channel_id=1, source_target_pairs={{0,4},{1,5},{2,6},{3,7},{4,0},{5,1},{6,2},{7,3},{8,12},{9,13},{10,... | collective-permute-start | bytes 786440 | tf_op jit(solution)/shard_map/ppermute | solution.py:28
  68.6 1.2 %collective-permute-start.21 = (f32[2,64,512]{2,1,0:T(8,128)S(1)}, f32[2,64,512]{2,1,0:T(8,128)S(1)}, u32[]{:S(2)}, u32[]{:S(2)}) collective-permute-start(f32[2,64,512]{2,1,0:T(8,128)S(1)} %get-tuple-element.28), channel_id=1, source_target_pairs={{0,6},{1,7},{2,0},{3,1},{4,2},{5,3},{6,4},{7,5},{8,14},{9,15},{10,... | collective-permute-start | bytes 786440 | tf_op jit(solution)/shard_map/ppermute | solution.py:28
  69.8 2.2 %collective-permute-done.23 = f32[2,64,512]{2,1,0:T(8,128)S(1)} collective-permute-done((f32[2,64,512]{2,1,0:T(8,128)S(1)}, f32[2,64,512]{2,1,0:T(8,128)S(1)}, u32[]{:S(2)}, u32[]{:S(2)}) %collective-permute-start.23) | collective-permute-done | bytes 262176 | tf_op jit(solution)/shard_map/ppermute | solution.py:32
  72.0 0.4 collective-permute-start.20
  72.5 4.6 %collective-permute-done.24 = f32[2,64,512]{2,1,0:T(8,128)S(1)} collective-permute-done((f32[2,64,512]{2,1,0:T(8,128)S(1)}, f32[2,64,512]{2,1,0:T(8,128)S(1)}, u32[]{:S(2)}, u32[]{:S(2)}) %collective-permute-start.24) | collective-permute-done | bytes 262176 | tf_op jit(solution)/shard_map/ppermute | solution.py:32
  77.1 0.0 collective-permute-done.25
  77.1 0.1 add_add_fusion
  77.2 1.7 %collective-permute-start.26 = (f32[64,512]{1,0:T(8,128)S(1)}, f32[64,512]{1,0:T(8,128)S(1)}, u32[]{:S(2)}, u32[]{:S(2)}) collective-permute-start(f32[64,512]{1,0:T(8,128)S(1)} %slice_bitcast_fusion), channel_id=1, source_target_pairs={{0,16},{16,0},{32,48},{48,32},{64,80},{80,64},{96,112},{112,96},{1... | collective-permute-start | bytes 393224 | tf_op jit(solution)/shard_map/ppermute | solution.py:32
  78.9 0.0 collective-permute-done.19
  78.9 1.6 %collective-permute-done.21 = f32[2,64,512]{2,1,0:T(8,128)S(1)} collective-permute-done((f32[2,64,512]{2,1,0:T(8,128)S(1)}, f32[2,64,512]{2,1,0:T(8,128)S(1)}, u32[]{:S(2)}, u32[]{:S(2)}) %collective-permute-start.21) | collective-permute-done | bytes 262176 | tf_op jit(solution)/shard_map/ppermute | solution.py:28
  80.5 0.5 collective-permute-done.20
  81.0 0.1 fusion.2
  81.2 1.7 %collective-permute-start.22 = (f32[64,512]{1,0:T(8,128)S(1)}, f32[64,512]{1,0:T(8,128)S(1)}, u32[]{:S(2)}, u32[]{:S(2)}) collective-permute-start(f32[64,512]{1,0:T(8,128)S(1)} %slice_bitcast_fusion.2), channel_id=1, source_target_pairs={{0,8},{1,9},{2,10},{3,11},{4,12},{5,13},{6,14},{7,15},{8,0},{9,1},... | collective-permute-start | bytes 393224 | tf_op jit(solution)/shard_map/ppermute | solution.py:28
  82.8 1.4 %collective-permute-done.26 = f32[64,512]{1,0:T(8,128)S(1)} collective-permute-done((f32[64,512]{1,0:T(8,128)S(1)}, f32[64,512]{1,0:T(8,128)S(1)}, u32[]{:S(2)}, u32[]{:S(2)}) %collective-permute-start.26) | collective-permute-done | bytes 131104 | tf_op jit(solution)/shard_map/ppermute | solution.py:32
  84.2 0.7 fusion.3
  84.9 1.3 %collective-permute-done.22 = f32[64,512]{1,0:T(8,128)S(1)} collective-permute-done((f32[64,512]{1,0:T(8,128)S(1)}, f32[64,512]{1,0:T(8,128)S(1)}, u32[]{:S(2)}, u32[]{:S(2)}) %collective-permute-start.22) | collective-permute-done | bytes 131104 | tf_op jit(solution)/shard_map/ppermute | solution.py:28
  86.2 0.7 fusion.4
  (5 shorter events, 0.1 us)
Async XLA Ops:
  0.6 48.8 %copy-start = (f32[1024,512]{1,0:T(8,128)S(1)}, f32[1024,512]{1,0:T(8,128)}, u32[]{:S(2)}) copy-start(f32[1024,512]{1,0:T(8,128)} %refs_18_.1) | copy-start | bytes 6291460
  2.9 2.0 %collective-permute-start = (f32[64,1536]{1,0:T(8,128)}, f32[64,1536]{1,0:T(8,128)S(1)}, u32[]{:S(2)}, u32[]{:S(2)}) collective-permute-start(f32[64,1536]{1,0:T(8,128)} %get-tuple-element.16), channel_id=1, source_target_pairs={{0,1},{1,0},{2,3},{3,2},{4,5},{5,4},{6,7},{7,6},{8,9},{9,8},{10,11... | collective-permute-start | bytes 1179656 | tf_op jit(solution)/shard_map/ppermute | solution.py:28
  4.9 19.4 %collective-permute-start.4 = (f32[128,1536]{1,0:T(8,128)S(1)}, f32[128,1536]{1,0:T(8,128)S(1)}, u32[]{:S(2)}, u32[]{:S(2)}) collective-permute-start(f32[128,1536]{1,0:T(8,128)S(1)} %constant_dynamic-update-slice_fusion.refs_0_), channel_id=1, source_target_pairs={{0,8},{1,17},{2,10},{3,19},{4,12},{5,21},{6,14},{7,23},{8,0},{9,25... | collective-permute-start | bytes 2359304 | tf_op jit(solution)/shard_map/ppermute | solution.py:214
  6.7 21.8 %collective-permute-start.1 = (f32[128,1536]{1,0:T(8,128)S(1)}, f32[128,1536]{1,0:T(8,128)S(1)}, u32[]{:S(2)}, u32[]{:S(2)}) collective-permute-start(f32[128,1536]{1,0:T(8,128)S(1)} %constant_dynamic-update-slice_fusion.refs_0_), channel_id=1, source_target_pairs={{0,4},{1,65},{2,6},{3,67},{4,0},{5,69},{6,2},{7,71},{8,12},{9,73},... | collective-permute-start | bytes 2359304 | tf_op jit(solution)/shard_map/ppermute | solution.py:214
  10.5 19.9 %collective-permute-start.9 = (f32[128,1536]{1,0:T(8,128)S(1)}, f32[128,1536]{1,0:T(8,128)S(1)}, u32[]{:S(2)}, u32[]{:S(2)}) collective-permute-start(f32[128,1536]{1,0:T(8,128)S(1)} %constant_dynamic-update-slice_fusion.refs_0_), channel_id=1, source_target_pairs={{0,1},{1,0},{2,3},{3,2},{4,5},{5,4},{6,7},{7,6},{8,9},{9,8},{10,11... | collective-permute-start | bytes 2359304 | tf_op jit(solution)/shard_map/ppermute | solution.py:28
  10.9 20.5 %collective-permute-start.3 = (f32[128,1536]{1,0:T(8,128)S(1)}, f32[128,1536]{1,0:T(8,128)S(1)}, u32[]{:S(2)}, u32[]{:S(2)}) collective-permute-start(f32[128,1536]{1,0:T(8,128)S(1)} %constant_dynamic-update-slice_fusion.refs_0_), channel_id=1, source_target_pairs={{0,2},{1,33},{2,4},{3,35},{4,6},{5,37},{6,0},{7,39},{8,10},{9,41},... | collective-permute-start | bytes 2359304 | tf_op jit(solution)/shard_map/ppermute | solution.py:214
  12.8 20.2 %collective-permute-start.2 = (f32[128,1536]{1,0:T(8,128)S(1)}, f32[128,1536]{1,0:T(8,128)S(1)}, u32[]{:S(2)}, u32[]{:S(2)}) collective-permute-start(f32[128,1536]{1,0:T(8,128)S(1)} %constant_dynamic-update-slice_fusion.refs_0_), channel_id=1, source_target_pairs={{0,6},{1,97},{2,0},{3,99},{4,2},{5,101},{6,4},{7,103},{8,14},{9,10... | collective-permute-start | bytes 2359304 | tf_op jit(solution)/shard_map/ppermute | solution.py:214
  24.3 11.2 %collective-permute-start.5 = (f32[64,1536]{1,0:T(8,128)S(1)}, f32[64,1536]{1,0:T(8,128)S(1)}, u32[]{:S(2)}, u32[]{:S(2)}) collective-permute-start(f32[64,1536]{1,0:T(8,128)S(1)} %slice.40), channel_id=1, source_target_pairs={{0,4},{1,65},{2,6},{3,67},{4,0},{5,69},{6,2},{7,71},{8,12},{9,73},... | collective-permute-start | bytes 1179656 | tf_op jit(solution)/shard_map/ppermute | solution.py:214
  28.5 11.8 %collective-permute-start.6 = (f32[64,1536]{1,0:T(8,128)S(1)}, f32[64,1536]{1,0:T(8,128)S(1)}, u32[]{:S(2)}, u32[]{:S(2)}) collective-permute-start(f32[64,1536]{1,0:T(8,128)S(1)} %slice.41), channel_id=1, source_target_pairs={{0,8},{1,17},{2,10},{3,19},{4,12},{5,21},{6,14},{7,23},{8,0},{9,25... | collective-permute-start | bytes 1179656 | tf_op jit(solution)/shard_map/ppermute | solution.py:214
  30.4 10.4 %collective-permute-start.13 = (f32[128,1536]{1,0:T(8,128)S(1)}, f32[128,1536]{1,0:T(8,128)S(1)}, u32[]{:S(2)}, u32[]{:S(2)}) collective-permute-start(f32[128,1536]{1,0:T(8,128)S(1)} %collective-permute-done.4.refs_4_), channel_id=1, source_target_pairs={{0,1},{1,0},{2,3},{3,2},{4,5},{5,4},{6,7},{7,6},{8,9},{9,8},{10,11... | collective-permute-start | bytes 2359304 | tf_op jit(solution)/shard_map/ppermute | solution.py:28
  31.4 14.0 %collective-permute-start.8 = (f32[128,1536]{1,0:T(8,128)S(1)}, f32[128,1536]{1,0:T(8,128)S(1)}, u32[]{:S(2)}, u32[]{:S(2)}) collective-permute-start(f32[128,1536]{1,0:T(8,128)S(1)} %collective-permute-done.4.refs_4_), channel_id=1, source_target_pairs={{0,2},{1,33},{2,4},{3,35},{4,6},{5,37},{6,0},{7,39},{8,10},{9,41},... | collective-permute-start | bytes 2359304 | tf_op jit(solution)/shard_map/ppermute | solution.py:214
  33.0 12.4 %collective-permute-start.7 = (f32[128,1536]{1,0:T(8,128)S(1)}, f32[128,1536]{1,0:T(8,128)S(1)}, u32[]{:S(2)}, u32[]{:S(2)}) collective-permute-start(f32[128,1536]{1,0:T(8,128)S(1)} %collective-permute-done.4.refs_4_), channel_id=1, source_target_pairs={{0,6},{1,97},{2,0},{3,99},{4,2},{5,101},{6,4},{7,103},{8,14},{9,10... | collective-permute-start | bytes 2359304 | tf_op jit(solution)/shard_map/ppermute | solution.py:214
  35.5 4.8 %collective-permute-start.14 = (f32[64,1536]{1,0:T(8,128)S(1)}, f32[64,1536]{1,0:T(8,128)S(1)}, u32[]{:S(2)}, u32[]{:S(2)}) collective-permute-start(f32[64,1536]{1,0:T(8,128)S(1)} %collective-permute-done.5.refs_5_), channel_id=1, source_target_pairs={{0,1},{1,0},{2,3},{3,2},{4,5},{5,4},{6,7},{7,6},{8,9},{9,8},{10,11... | collective-permute-start | bytes 1179656 | tf_op jit(solution)/shard_map/ppermute | solution.py:28
  40.3 5.6 %collective-permute-start.12 = (f32[128,1536]{1,0:T(8,128)S(1)}, f32[128,1536]{1,0:T(8,128)S(1)}, u32[]{:S(2)}, u32[]{:S(2)}) collective-permute-start(f32[128,1536]{1,0:T(8,128)S(1)} %collective-permute-done.3.refs_3_), channel_id=1, source_target_pairs={{0,1},{1,0},{2,3},{3,2},{4,5},{5,4},{6,7},{7,6},{8,9},{9,8},{10,11... | collective-permute-start | bytes 2359304 | tf_op jit(solution)/shard_map/ppermute | solution.py:28
  40.3 9.0 %collective-permute-start.10 = (f32[128,1536]{1,0:T(8,128)S(1)}, f32[128,1536]{1,0:T(8,128)S(1)}, u32[]{:S(2)}, u32[]{:S(2)}) collective-permute-start(f32[128,1536]{1,0:T(8,128)S(1)} %collective-permute-done.1.refs_1_), channel_id=1, source_target_pairs={{0,1},{1,0},{2,3},{3,2},{4,5},{5,4},{6,7},{7,6},{8,9},{9,8},{10,11... | collective-permute-start | bytes 2359304 | tf_op jit(solution)/shard_map/ppermute | solution.py:28
  40.9 5.1 %collective-permute-start.11 = (f32[128,1536]{1,0:T(8,128)S(1)}, f32[128,1536]{1,0:T(8,128)S(1)}, u32[]{:S(2)}, u32[]{:S(2)}) collective-permute-start(f32[128,1536]{1,0:T(8,128)S(1)} %collective-permute-done.2.refs_2_), channel_id=1, source_target_pairs={{0,1},{1,0},{2,3},{3,2},{4,5},{5,4},{6,7},{7,6},{8,9},{9,8},{10,11... | collective-permute-start | bytes 2359304 | tf_op jit(solution)/shard_map/ppermute | solution.py:28
  45.4 4.0 %collective-permute-start.17 = (f32[128,1536]{1,0:T(8,128)S(1)}, f32[128,1536]{1,0:T(8,128)S(1)}, u32[]{:S(2)}, u32[]{:S(2)}) collective-permute-start(f32[128,1536]{1,0:T(8,128)S(1)} %collective-permute-done.8.refs_8_), channel_id=1, source_target_pairs={{0,1},{1,0},{2,3},{3,2},{4,5},{5,4},{6,7},{7,6},{8,9},{9,8},{10,11... | collective-permute-start | bytes 2359304 | tf_op jit(solution)/shard_map/ppermute | solution.py:28
  45.4 4.0 %collective-permute-start.16 = (f32[128,1536]{1,0:T(8,128)S(1)}, f32[128,1536]{1,0:T(8,128)S(1)}, u32[]{:S(2)}, u32[]{:S(2)}) collective-permute-start(f32[128,1536]{1,0:T(8,128)S(1)} %collective-permute-done.7.refs_7_), channel_id=1, source_target_pairs={{0,1},{1,0},{2,3},{3,2},{4,5},{5,4},{6,7},{7,6},{8,9},{9,8},{10,11... | collective-permute-start | bytes 2359304 | tf_op jit(solution)/shard_map/ppermute | solution.py:28
  45.9 3.5 %collective-permute-start.15 = (f32[64,1536]{1,0:T(8,128)S(1)}, f32[64,1536]{1,0:T(8,128)S(1)}, u32[]{:S(2)}, u32[]{:S(2)}) collective-permute-start(f32[64,1536]{1,0:T(8,128)S(1)} %collective-permute-done.6.refs_6_), channel_id=1, source_target_pairs={{0,1},{1,0},{2,3},{3,2},{4,5},{5,4},{6,7},{7,6},{8,9},{9,8},{10,11... | collective-permute-start | bytes 1179656 | tf_op jit(solution)/shard_map/ppermute | solution.py:28
  61.1 4.8 %collective-permute-start.18 = (f32[8,64,512]{2,1,0:T(8,128)S(1)}, f32[8,64,512]{2,1,0:T(8,128)S(1)}, u32[]{:S(2)}, u32[]{:S(2)}) collective-permute-start(f32[8,64,512]{2,1,0:T(8,128)S(1)} %get-tuple-element.19), channel_id=1, source_target_pairs={{0,1},{1,0},{2,3},{3,2},{4,5},{5,4},{6,7},{7,6},{8,9},{9,8},{10,11... | collective-permute-start | bytes 3145736 | tf_op jit(solution)/shard_map/ppermute | solution.py:28
  61.4 10.7 %collective-permute-start.23 = (f32[2,64,512]{2,1,0:T(8,128)S(1)}, f32[2,64,512]{2,1,0:T(8,128)S(1)}, u32[]{:S(2)}, u32[]{:S(2)}) collective-permute-start(f32[2,64,512]{2,1,0:T(8,128)S(1)} %get-tuple-element.24), channel_id=1, source_target_pairs={{0,64},{16,80},{32,96},{48,112},{64,0},{80,16},{96,32},{112,48},{1... | collective-permute-start | bytes 786440 | tf_op jit(solution)/shard_map/ppermute | solution.py:32
  62.7 14.4 %collective-permute-start.24 = (f32[2,64,512]{2,1,0:T(8,128)S(1)}, f32[2,64,512]{2,1,0:T(8,128)S(1)}, u32[]{:S(2)}, u32[]{:S(2)}) collective-permute-start(f32[2,64,512]{2,1,0:T(8,128)S(1)} %get-tuple-element.25), channel_id=1, source_target_pairs={{0,32},{16,48},{32,64},{48,80},{64,96},{80,112},{96,0},{112,16},{1... | collective-permute-start | bytes 786440 | tf_op jit(solution)/shard_map/ppermute | solution.py:32
  63.4 13.7 %collective-permute-start.25 = (f32[2,64,512]{2,1,0:T(8,128)S(1)}, f32[2,64,512]{2,1,0:T(8,128)S(1)}, u32[]{:S(2)}, u32[]{:S(2)}) collective-permute-start(f32[2,64,512]{2,1,0:T(8,128)S(1)} %get-tuple-element.26), channel_id=1, source_target_pairs={{0,96},{16,112},{32,0},{48,16},{64,32},{80,48},{96,64},{112,80},{1... | collective-permute-start | bytes 786440 | tf_op jit(solution)/shard_map/ppermute | solution.py:32
  66.1 12.8 %collective-permute-start.19 = (f32[2,64,512]{2,1,0:T(8,128)S(1)}, f32[2,64,512]{2,1,0:T(8,128)S(1)}, u32[]{:S(2)}, u32[]{:S(2)}) collective-permute-start(f32[2,64,512]{2,1,0:T(8,128)S(1)} %get-tuple-element.27), channel_id=1, source_target_pairs={{0,4},{1,5},{2,6},{3,7},{4,0},{5,1},{6,2},{7,3},{8,12},{9,13},{10,... | collective-permute-start | bytes 786440 | tf_op jit(solution)/shard_map/ppermute | solution.py:28
  68.6 11.9 %collective-permute-start.21 = (f32[2,64,512]{2,1,0:T(8,128)S(1)}, f32[2,64,512]{2,1,0:T(8,128)S(1)}, u32[]{:S(2)}, u32[]{:S(2)}) collective-permute-start(f32[2,64,512]{2,1,0:T(8,128)S(1)} %get-tuple-element.28), channel_id=1, source_target_pairs={{0,6},{1,7},{2,0},{3,1},{4,2},{5,3},{6,4},{7,5},{8,14},{9,15},{10,... | collective-permute-start | bytes 786440 | tf_op jit(solution)/shard_map/ppermute | solution.py:28
  72.0 9.0 %collective-permute-start.20 = (f32[2,64,512]{2,1,0:T(8,128)S(1)}, f32[2,64,512]{2,1,0:T(8,128)S(1)}, u32[]{:S(2)}, u32[]{:S(2)}) collective-permute-start(f32[2,64,512]{2,1,0:T(8,128)S(1)} %get-tuple-element.29), channel_id=1, source_target_pairs={{0,2},{1,3},{2,4},{3,5},{4,6},{5,7},{6,0},{7,1},{8,10},{9,11},{10,... | collective-permute-start | bytes 786440 | tf_op jit(solution)/shard_map/ppermute | solution.py:28
  77.2 7.0 %collective-permute-start.26 = (f32[64,512]{1,0:T(8,128)S(1)}, f32[64,512]{1,0:T(8,128)S(1)}, u32[]{:S(2)}, u32[]{:S(2)}) collective-permute-start(f32[64,512]{1,0:T(8,128)S(1)} %slice_bitcast_fusion), channel_id=1, source_target_pairs={{0,16},{16,0},{32,48},{48,32},{64,80},{80,64},{96,112},{112,96},{1... | collective-permute-start | bytes 393224 | tf_op jit(solution)/shard_map/ppermute | solution.py:32
  81.2 5.0 %collective-permute-start.22 = (f32[64,512]{1,0:T(8,128)S(1)}, f32[64,512]{1,0:T(8,128)S(1)}, u32[]{:S(2)}, u32[]{:S(2)}) collective-permute-start(f32[64,512]{1,0:T(8,128)S(1)} %slice_bitcast_fusion.2), channel_id=1, source_target_pairs={{0,8},{1,9},{2,10},{3,11},{4,12},{5,13},{6,14},{7,15},{8,0},{9,1},... | collective-permute-start | bytes 393224 | tf_op jit(solution)/shard_map/ppermute | solution.py:28

commit v6 on v5

--- a/solution.py
+++ b/solution.py
@@ -235,7 +235,7 @@
     sib = over_col(sib, dc=1)
     own = [a + sib[2 * n : 2 * n + 2] for n, a in enumerate(own)]
     row_sum, col_sum = own[0], col[0]
-    for n in range(1, 4):
+    for n in (1, 3, 2):
         row_sum = row_sum + over_col(own[n], dz=SHIFTS[n])
         col_sum = col_sum + over_row(col[n], dx=SHIFTS[n])
     grad_rows = row_sum[0] + over_col(row_sum[1], dy=1)

time: 87.1 us -> 86.9 us (level)
    ppermute x15, waiting for transfers between devices: 7.76 us -> 6.35 us  [over_col(): return lax.ppermute(a, 'col', col_perm(dy, dz, dc))]
    ppermute x4, waiting for transfers between devices: 8.18 us -> 9.41 us  [over_row(): return lax.ppermute(a, 'row', row_perm(dx, dh))]
    ppermute x4, starting transfers between devices: 6.31 us -> 5.1 us  [over_row(): return lax.ppermute(a, 'row', row_perm(dx, dh))]
    ppermute x15, starting transfers between devices: 8.6 us -> 9.59 us  [over_col(): return lax.ppermute(a, 'col', col_perm(dy, dz, dc))]
where the time goes in v6:
time: 86.9 us; the launch traced here: 86.5 us
  starting transfers between devices  34.5 us (40%)
  waiting for transfers between devices  34.4 us (40%)
  Pallas kernels  14 us (16%)
  other arithmetic  1.69 us (2%)
  local copies, waits for them, and re-layouts  1.13 us (1%)
    ppermute x8, starting transfers between devices, over_both(): return lax.ppermute(a, ('row', 'col'), both_perm(flip, shift))  19.8 us
    ppermute x8, waiting for transfers between devices, over_both(): return lax.ppermute(a, ('row', 'col'), both_perm(flip, shift))  18.7 us
    pallas_call x1, Pallas kernels, tile(): pl.pallas_call(tile_kernel, out_shape=[jax.ShapeDtypeStruct((ROWS, COLS),...  11.7 us
    ppermute x15, starting transfers between devices, over_col(): return lax.ppermute(a, 'col', col_perm(dy, dz, dc))  9.59 us
    ppermute x4, waiting for transfers between devices, over_row(): return lax.ppermute(a, 'row', row_perm(dx, dh))  9.41 us
    ppermute x15, waiting for transfers between devices, over_col(): return lax.ppermute(a, 'col', col_perm(dy, dz, dc))  6.35 us
    ppermute x4, starting transfers between devices, over_row(): return lax.ppermute(a, 'row', row_perm(dx, dh))  5.1 us
    pallas_call x1, Pallas kernels, pack(): pl.pallas_call(pack_kernel, out_shape=[jax.ShapeDtypeStruct((B, W), f32)]...  2.23 us
  transfers between devices with their start and end apart: 27, of which 11 were waited for; matrix products, arithmetic and copies ran while one was open for 2% of the time, Pallas kernels for 0%

profile of v6, /device:TPU:0, one launch (start us, length us, event | category | flops | bytes accessed | tf_op | source)
XLA Modules:
  0.0 86.5 jit_solution(2730929677614731071)
XLA Ops:
  0.6 0.0 copy-start
  0.6 2.2 %pack.1 = (f32[64,1536]{1,0:T(8,128)}, f32[64,1536]{1,0:T(8,128)}) custom-call(f32[64,512]{1,0:T(8,128)} %feat_rows.1, f32[64,512]{1,0:T(8,128)} %feat_cols.1, f32[64,1024]{1,0:T(8,128)} %panel_rows.1, f32[64,1024]{1,0:T(8,128)} %panel_cols.1), custom_call_target="tpu_custom_call" | custom-call | bytes 1600000 | tf_op jit(solution)/shard_map/pack/pallas_call | solution.py:104
  2.9 0.1 collective-permute-start
  3.0 1.0 %constant_dynamic-update-slice_fusion.1 = f32[128,1536]{1,0:T(8,128)S(1)} fusion(f32[64,1536]{1,0:T(8,128)} %get-tuple-element.15), kind=kLoop, calls=%fused_computation.15 | loop fusion | bytes 786432
  4.0 0.9 %collective-permute-done = f32[64,1536]{1,0:T(8,128)S(1)} collective-permute-done((f32[64,1536]{1,0:T(8,128)}, f32[64,1536]{1,0:T(8,128)S(1)}, u32[]{:S(2)}, u32[]{:S(2)}) %collective-permute-start) | collective-permute-done | bytes 393248 | tf_op jit(solution)/shard_map/ppermute | solution.py:28
  4.9 1.7 %collective-permute-start.4 = (f32[128,1536]{1,0:T(8,128)S(1)}, f32[128,1536]{1,0:T(8,128)S(1)}, u32[]{:S(2)}, u32[]{:S(2)}) collective-permute-start(f32[128,1536]{1,0:T(8,128)S(1)} %constant_dynamic-update-slice_fusion.refs_0_), channel_id=1, source_target_pairs={{0,8},{1,17},{2,10},{3,19},{4,12},{5,21},{6,14},{7,23},{8,0},{9,25... | collective-permute-start | bytes 2359304 | tf_op jit(solution)/shard_map/ppermute | solution.py:214
  6.7 3.9 %collective-permute-start.1 = (f32[128,1536]{1,0:T(8,128)S(1)}, f32[128,1536]{1,0:T(8,128)S(1)}, u32[]{:S(2)}, u32[]{:S(2)}) collective-permute-start(f32[128,1536]{1,0:T(8,128)S(1)} %constant_dynamic-update-slice_fusion.refs_0_), channel_id=1, source_target_pairs={{0,4},{1,65},{2,6},{3,67},{4,0},{5,69},{6,2},{7,71},{8,12},{9,73},... | collective-permute-start | bytes 2359304 | tf_op jit(solution)/shard_map/ppermute | solution.py:214
  10.5 0.3 collective-permute-start.9
  10.9 1.9 %collective-permute-start.3 = (f32[128,1536]{1,0:T(8,128)S(1)}, f32[128,1536]{1,0:T(8,128)S(1)}, u32[]{:S(2)}, u32[]{:S(2)}) collective-permute-start(f32[128,1536]{1,0:T(8,128)S(1)} %constant_dynamic-update-slice_fusion.refs_0_), channel_id=1, source_target_pairs={{0,2},{1,33},{2,4},{3,35},{4,6},{5,37},{6,0},{7,39},{8,10},{9,41},... | collective-permute-start | bytes 2359304 | tf_op jit(solution)/shard_map/ppermute | solution.py:214
  12.8 2.1 %collective-permute-start.2 = (f32[128,1536]{1,0:T(8,128)S(1)}, f32[128,1536]{1,0:T(8,128)S(1)}, u32[]{:S(2)}, u32[]{:S(2)}) collective-permute-start(f32[128,1536]{1,0:T(8,128)S(1)} %constant_dynamic-update-slice_fusion.refs_0_), channel_id=1, source_target_pairs={{0,6},{1,97},{2,0},{3,99},{4,2},{5,101},{6,4},{7,103},{8,14},{9,10... | collective-permute-start | bytes 2359304 | tf_op jit(solution)/shard_map/ppermute | solution.py:214
  14.9 9.4 %collective-permute-done.4.refs_4_ = f32[128,1536]{1,0:T(8,128)S(1)} collective-permute-done((f32[128,1536]{1,0:T(8,128)S(1)}, f32[128,1536]{1,0:T(8,128)S(1)}, u32[]{:S(2)}, u32[]{:S(2)}) %collective-permute-start.4) | collective-permute-done | bytes 786464 | tf_op jit(solution)/shard_map/ppermute | solution.py:214
  24.3 4.1 %collective-permute-start.5 = (f32[64,1536]{1,0:T(8,128)S(1)}, f32[64,1536]{1,0:T(8,128)S(1)}, u32[]{:S(2)}, u32[]{:S(2)}) collective-permute-start(f32[64,1536]{1,0:T(8,128)S(1)} %slice.40), channel_id=1, source_target_pairs={{0,4},{1,65},{2,6},{3,67},{4,0},{5,69},{6,2},{7,71},{8,12},{9,73},... | collective-permute-start | bytes 1179656 | tf_op jit(solution)/shard_map/ppermute | solution.py:214
  28.5 0.0 collective-permute-done.1.refs_1_
  28.5 1.9 %collective-permute-start.6 = (f32[64,1536]{1,0:T(8,128)S(1)}, f32[64,1536]{1,0:T(8,128)S(1)}, u32[]{:S(2)}, u32[]{:S(2)}) collective-permute-start(f32[64,1536]{1,0:T(8,128)S(1)} %slice.41), channel_id=1, source_target_pairs={{0,8},{1,17},{2,10},{3,19},{4,12},{5,21},{6,14},{7,23},{8,0},{9,25... | collective-permute-start | bytes 1179656 | tf_op jit(solution)/shard_map/ppermute | solution.py:214
  30.4 0.0 collective-permute-done.9.refs_9_
  30.4 1.0 %collective-permute-start.13 = (f32[128,1536]{1,0:T(8,128)S(1)}, f32[128,1536]{1,0:T(8,128)S(1)}, u32[]{:S(2)}, u32[]{:S(2)}) collective-permute-start(f32[128,1536]{1,0:T(8,128)S(1)} %collective-permute-done.4.refs_4_), channel_id=1, source_target_pairs={{0,1},{1,0},{2,3},{3,2},{4,5},{5,4},{6,7},{7,6},{8,9},{9,8},{10,11... | collective-permute-start | bytes 2359304 | tf_op jit(solution)/shard_map/ppermute | solution.py:28
  31.4 0.0 collective-permute-done.3.refs_3_
  31.4 1.6 %collective-permute-start.8 = (f32[128,1536]{1,0:T(8,128)S(1)}, f32[128,1536]{1,0:T(8,128)S(1)}, u32[]{:S(2)}, u32[]{:S(2)}) collective-permute-start(f32[128,1536]{1,0:T(8,128)S(1)} %collective-permute-done.4.refs_4_), channel_id=1, source_target_pairs={{0,2},{1,33},{2,4},{3,35},{4,6},{5,37},{6,0},{7,39},{8,10},{9,41},... | collective-permute-start | bytes 2359304 | tf_op jit(solution)/shard_map/ppermute | solution.py:214
  33.0 0.0 collective-permute-done.2.refs_2_
  33.0 2.5 %collective-permute-start.7 = (f32[128,1536]{1,0:T(8,128)S(1)}, f32[128,1536]{1,0:T(8,128)S(1)}, u32[]{:S(2)}, u32[]{:S(2)}) collective-permute-start(f32[128,1536]{1,0:T(8,128)S(1)} %collective-permute-done.4.refs_4_), channel_id=1, source_target_pairs={{0,6},{1,97},{2,0},{3,99},{4,2},{5,101},{6,4},{7,103},{8,14},{9,10... | collective-permute-start | bytes 2359304 | tf_op jit(solution)/shard_map/ppermute | solution.py:214
  35.5 0.0 collective-permute-done.5.refs_5_
  35.5 0.0 collective-permute-start.14
  35.5 4.8 %collective-permute-done.6.refs_6_ = f32[64,1536]{1,0:T(8,128)S(1)} collective-permute-done((f32[64,1536]{1,0:T(8,128)S(1)}, f32[64,1536]{1,0:T(8,128)S(1)}, u32[]{:S(2)}, u32[]{:S(2)}) %collective-permute-start.6) | collective-permute-done | bytes 393248 | tf_op jit(solution)/shard_map/ppermute | solution.py:214
  40.3 0.0 collective-permute-start.12
  40.3 0.0 collective-permute-done.14.refs_14_
  40.3 0.5 collective-permute-start.10
  40.9 0.0 collective-permute-done.13.refs_13_
  40.9 0.1 collective-permute-start.11
  40.9 4.5 %collective-permute-done.8.refs_8_ = f32[128,1536]{1,0:T(8,128)S(1)} collective-permute-done((f32[128,1536]{1,0:T(8,128)S(1)}, f32[128,1536]{1,0:T(8,128)S(1)}, u32[]{:S(2)}, u32[]{:S(2)}) %collective-permute-start.8) | collective-permute-done | bytes 786464 | tf_op jit(solution)/shard_map/ppermute | solution.py:214
  45.4 0.0 collective-permute-start.17
  45.4 0.0 collective-permute-done.7.refs_7_
  45.4 0.5 collective-permute-start.16
  45.9 0.0 collective-permute-done.12.refs_12_
  45.9 0.1 collective-permute-start.15
  46.0 0.0 collective-permute-done.11.refs_11_
  46.0 3.4 %collective-permute-done.15.refs_15_ = f32[64,1536]{1,0:T(8,128)S(1)} collective-permute-done((f32[64,1536]{1,0:T(8,128)S(1)}, f32[64,1536]{1,0:T(8,128)S(1)}, u32[]{:S(2)}, u32[]{:S(2)}) %collective-permute-start.15) | collective-permute-done | bytes 393248 | tf_op jit(solution)/shard_map/ppermute | solution.py:28
  49.4 0.0 collective-permute-done.10.refs_10_
  49.4 0.0 collective-permute-done.17.refs_17_
  49.4 0.0 collective-permute-done.16.refs_16_
  49.4 0.0 copy-done
  49.4 11.7 %tile.1 = (f32[1024,512]{1,0:T(8,128)}, f32[2,64,512]{2,1,0:T(8,128)S(1)}, f32[2,64,512]{2,1,0:T(8,128)S(1)}, f32[2,64,512]{2,1,0:T(8,128)S(1)}, f32[2,64,512]{2...) custom-call(f32[128,1536]{1,0:T(8,128)S(1)} %constant_dynamic-update, ...), custom_call_target="tpu_custom_call" | custom-call | flops 8000000000 | bytes 20000000 | tf_op jit(solution)/shard_map/tile/pallas_call | solution.py:174
  61.1 0.2 collective-permute-start.18
  61.4 1.4 %collective-permute-start.23 = (f32[2,64,512]{2,1,0:T(8,128)S(1)}, f32[2,64,512]{2,1,0:T(8,128)S(1)}, u32[]{:S(2)}, u32[]{:S(2)}) collective-permute-start(f32[2,64,512]{2,1,0:T(8,128)S(1)} %get-tuple-element.24), channel_id=1, source_target_pairs={{0,64},{16,80},{32,96},{48,112},{64,0},{80,16},{96,32},{112,48},{1... | collective-permute-start | bytes 786440 | tf_op jit(solution)/shard_map/ppermute | solution.py:32
  62.7 1.9 %collective-permute-start.24 = (f32[2,64,512]{2,1,0:T(8,128)S(1)}, f32[2,64,512]{2,1,0:T(8,128)S(1)}, u32[]{:S(2)}, u32[]{:S(2)}) collective-permute-start(f32[2,64,512]{2,1,0:T(8,128)S(1)} %get-tuple-element.25), channel_id=1, source_target_pairs={{0,96},{16,112},{32,0},{48,16},{64,32},{80,48},{96,64},{112,80},{1... | collective-permute-start | bytes 786440 | tf_op jit(solution)/shard_map/ppermute | solution.py:32
  64.6 0.1 collective-permute-start.25
  64.7 0.0 collective-permute-done.18
  64.7 0.1 slice_add_fusion.2
  64.9 2.5 %collective-permute-start.19 = (f32[2,64,512]{2,1,0:T(8,128)S(1)}, f32[2,64,512]{2,1,0:T(8,128)S(1)}, u32[]{:S(2)}, u32[]{:S(2)}) collective-permute-start(f32[2,64,512]{2,1,0:T(8,128)S(1)} %get-tuple-element.27), channel_id=1, source_target_pairs={{0,4},{1,5},{2,6},{3,7},{4,0},{5,1},{6,2},{7,3},{8,12},{9,13},{10,... | collective-permute-start | bytes 786440 | tf_op jit(solution)/shard_map/ppermute | solution.py:28
  67.4 0.5 collective-permute-start.21
  67.9 4.1 %collective-permute-done.23 = f32[2,64,512]{2,1,0:T(8,128)S(1)} collective-permute-done((f32[2,64,512]{2,1,0:T(8,128)S(1)}, f32[2,64,512]{2,1,0:T(8,128)S(1)}, u32[]{:S(2)}, u32[]{:S(2)}) %collective-permute-start.23) | collective-permute-done | bytes 262176 | tf_op jit(solution)/shard_map/ppermute | solution.py:32
  72.0 2.3 %collective-permute-start.20 = (f32[2,64,512]{2,1,0:T(8,128)S(1)}, f32[2,64,512]{2,1,0:T(8,128)S(1)}, u32[]{:S(2)}, u32[]{:S(2)}) collective-permute-start(f32[2,64,512]{2,1,0:T(8,128)S(1)} %get-tuple-element.29), channel_id=1, source_target_pairs={{0,6},{1,7},{2,0},{3,1},{4,2},{5,3},{6,4},{7,5},{8,14},{9,15},{10,... | collective-permute-start | bytes 786440 | tf_op jit(solution)/shard_map/ppermute | solution.py:28
  74.4 1.2 %collective-permute-done.24 = f32[2,64,512]{2,1,0:T(8,128)S(1)} collective-permute-done((f32[2,64,512]{2,1,0:T(8,128)S(1)}, f32[2,64,512]{2,1,0:T(8,128)S(1)}, u32[]{:S(2)}, u32[]{:S(2)}) %collective-permute-start.24) | collective-permute-done | bytes 262176 | tf_op jit(solution)/shard_map/ppermute | solution.py:32
  75.6 1.5 %collective-permute-done.25 = f32[2,64,512]{2,1,0:T(8,128)S(1)} collective-permute-done((f32[2,64,512]{2,1,0:T(8,128)S(1)}, f32[2,64,512]{2,1,0:T(8,128)S(1)}, u32[]{:S(2)}, u32[]{:S(2)}) %collective-permute-start.25) | collective-permute-done | bytes 262176 | tf_op jit(solution)/shard_map/ppermute | solution.py:32
  77.1 0.1 add_add_fusion
  77.2 1.7 %collective-permute-start.26 = (f32[64,512]{1,0:T(8,128)S(1)}, f32[64,512]{1,0:T(8,128)S(1)}, u32[]{:S(2)}, u32[]{:S(2)}) collective-permute-start(f32[64,512]{1,0:T(8,128)S(1)} %slice_bitcast_fusion), channel_id=1, source_target_pairs={{0,16},{16,0},{32,48},{48,32},{64,80},{80,64},{96,112},{112,96},{1... | collective-permute-start | bytes 393224 | tf_op jit(solution)/shard_map/ppermute | solution.py:32
  78.9 0.0 collective-permute-done.19
  78.9 1.1 %collective-permute-done.21 = f32[2,64,512]{2,1,0:T(8,128)S(1)} collective-permute-done((f32[2,64,512]{2,1,0:T(8,128)S(1)}, f32[2,64,512]{2,1,0:T(8,128)S(1)}, u32[]{:S(2)}, u32[]{:S(2)}) %collective-permute-start.21) | collective-permute-done | bytes 262176 | tf_op jit(solution)/shard_map/ppermute | solution.py:28
  80.0 0.0 collective-permute-done.20
  80.0 0.1 fusion.2
  80.1 1.4 %collective-permute-start.22 = (f32[64,512]{1,0:T(8,128)S(1)}, f32[64,512]{1,0:T(8,128)S(1)}, u32[]{:S(2)}, u32[]{:S(2)}) collective-permute-start(f32[64,512]{1,0:T(8,128)S(1)} %slice_bitcast_fusion.2), channel_id=1, source_target_pairs={{0,8},{1,9},{2,10},{3,11},{4,12},{5,13},{6,14},{7,15},{8,0},{9,1},... | collective-permute-start | bytes 393224 | tf_op jit(solution)/shard_map/ppermute | solution.py:28
  81.6 2.6 %collective-permute-done.26 = f32[64,512]{1,0:T(8,128)S(1)} collective-permute-done((f32[64,512]{1,0:T(8,128)S(1)}, f32[64,512]{1,0:T(8,128)S(1)}, u32[]{:S(2)}, u32[]{:S(2)}) %collective-permute-start.26) | collective-permute-done | bytes 131104 | tf_op jit(solution)/shard_map/ppermute | solution.py:32
  84.2 0.7 fusion.3
  84.9 1.0 %collective-permute-done.22 = f32[64,512]{1,0:T(8,128)S(1)} collective-permute-done((f32[64,512]{1,0:T(8,128)S(1)}, f32[64,512]{1,0:T(8,128)S(1)}, u32[]{:S(2)}, u32[]{:S(2)}) %collective-permute-start.22) | collective-permute-done | bytes 131104 | tf_op jit(solution)/shard_map/ppermute | solution.py:28
  85.8 0.7 fusion.4
  (5 shorter events, 0.1 us)
Async XLA Ops:
  0.6 48.8 %copy-start = (f32[1024,512]{1,0:T(8,128)S(1)}, f32[1024,512]{1,0:T(8,128)}, u32[]{:S(2)}) copy-start(f32[1024,512]{1,0:T(8,128)} %refs_18_.1) | copy-start | bytes 6291460
  2.9 2.0 %collective-permute-start = (f32[64,1536]{1,0:T(8,128)}, f32[64,1536]{1,0:T(8,128)S(1)}, u32[]{:S(2)}, u32[]{:S(2)}) collective-permute-start(f32[64,1536]{1,0:T(8,128)} %get-tuple-element.16), channel_id=1, source_target_pairs={{0,1},{1,0},{2,3},{3,2},{4,5},{5,4},{6,7},{7,6},{8,9},{9,8},{10,11... | collective-permute-start | bytes 1179656 | tf_op jit(solution)/shard_map/ppermute | solution.py:28
  4.9 19.4 %collective-permute-start.4 = (f32[128,1536]{1,0:T(8,128)S(1)}, f32[128,1536]{1,0:T(8,128)S(1)}, u32[]{:S(2)}, u32[]{:S(2)}) collective-permute-start(f32[128,1536]{1,0:T(8,128)S(1)} %constant_dynamic-update-slice_fusion.refs_0_), channel_id=1, source_target_pairs={{0,8},{1,17},{2,10},{3,19},{4,12},{5,21},{6,14},{7,23},{8,0},{9,25... | collective-permute-start | bytes 2359304 | tf_op jit(solution)/shard_map/ppermute | solution.py:214
  6.7 21.8 %collective-permute-start.1 = (f32[128,1536]{1,0:T(8,128)S(1)}, f32[128,1536]{1,0:T(8,128)S(1)}, u32[]{:S(2)}, u32[]{:S(2)}) collective-permute-start(f32[128,1536]{1,0:T(8,128)S(1)} %constant_dynamic-update-slice_fusion.refs_0_), channel_id=1, source_target_pairs={{0,4},{1,65},{2,6},{3,67},{4,0},{5,69},{6,2},{7,71},{8,12},{9,73},... | collective-permute-start | bytes 2359304 | tf_op jit(solution)/shard_map/ppermute | solution.py:214
  10.5 19.9 %collective-permute-start.9 = (f32[128,1536]{1,0:T(8,128)S(1)}, f32[128,1536]{1,0:T(8,128)S(1)}, u32[]{:S(2)}, u32[]{:S(2)}) collective-permute-start(f32[128,1536]{1,0:T(8,128)S(1)} %constant_dynamic-update-slice_fusion.refs_0_), channel_id=1, source_target_pairs={{0,1},{1,0},{2,3},{3,2},{4,5},{5,4},{6,7},{7,6},{8,9},{9,8},{10,11... | collective-permute-start | bytes 2359304 | tf_op jit(solution)/shard_map/ppermute | solution.py:28
  10.9 20.5 %collective-permute-start.3 = (f32[128,1536]{1,0:T(8,128)S(1)}, f32[128,1536]{1,0:T(8,128)S(1)}, u32[]{:S(2)}, u32[]{:S(2)}) collective-permute-start(f32[128,1536]{1,0:T(8,128)S(1)} %constant_dynamic-update-slice_fusion.refs_0_), channel_id=1, source_target_pairs={{0,2},{1,33},{2,4},{3,35},{4,6},{5,37},{6,0},{7,39},{8,10},{9,41},... | collective-permute-start | bytes 2359304 | tf_op jit(solution)/shard_map/ppermute | solution.py:214
  12.8 20.2 %collective-permute-start.2 = (f32[128,1536]{1,0:T(8,128)S(1)}, f32[128,1536]{1,0:T(8,128)S(1)}, u32[]{:S(2)}, u32[]{:S(2)}) collective-permute-start(f32[128,1536]{1,0:T(8,128)S(1)} %constant_dynamic-update-slice_fusion.refs_0_), channel_id=1, source_target_pairs={{0,6},{1,97},{2,0},{3,99},{4,2},{5,101},{6,4},{7,103},{8,14},{9,10... | collective-permute-start | bytes 2359304 | tf_op jit(solution)/shard_map/ppermute | solution.py:214
  24.3 11.2 %collective-permute-start.5 = (f32[64,1536]{1,0:T(8,128)S(1)}, f32[64,1536]{1,0:T(8,128)S(1)}, u32[]{:S(2)}, u32[]{:S(2)}) collective-permute-start(f32[64,1536]{1,0:T(8,128)S(1)} %slice.40), channel_id=1, source_target_pairs={{0,4},{1,65},{2,6},{3,67},{4,0},{5,69},{6,2},{7,71},{8,12},{9,73},... | collective-permute-start | bytes 1179656 | tf_op jit(solution)/shard_map/ppermute | solution.py:214
  28.5 11.8 %collective-permute-start.6 = (f32[64,1536]{1,0:T(8,128)S(1)}, f32[64,1536]{1,0:T(8,128)S(1)}, u32[]{:S(2)}, u32[]{:S(2)}) collective-permute-start(f32[64,1536]{1,0:T(8,128)S(1)} %slice.41), channel_id=1, source_target_pairs={{0,8},{1,17},{2,10},{3,19},{4,12},{5,21},{6,14},{7,23},{8,0},{9,25... | collective-permute-start | bytes 1179656 | tf_op jit(solution)/shard_map/ppermute | solution.py:214
  30.4 10.4 %collective-permute-start.13 = (f32[128,1536]{1,0:T(8,128)S(1)}, f32[128,1536]{1,0:T(8,128)S(1)}, u32[]{:S(2)}, u32[]{:S(2)}) collective-permute-start(f32[128,1536]{1,0:T(8,128)S(1)} %collective-permute-done.4.refs_4_), channel_id=1, source_target_pairs={{0,1},{1,0},{2,3},{3,2},{4,5},{5,4},{6,7},{7,6},{8,9},{9,8},{10,11... | collective-permute-start | bytes 2359304 | tf_op jit(solution)/shard_map/ppermute | solution.py:28
  31.4 14.0 %collective-permute-start.8 = (f32[128,1536]{1,0:T(8,128)S(1)}, f32[128,1536]{1,0:T(8,128)S(1)}, u32[]{:S(2)}, u32[]{:S(2)}) collective-permute-start(f32[128,1536]{1,0:T(8,128)S(1)} %collective-permute-done.4.refs_4_), channel_id=1, source_target_pairs={{0,2},{1,33},{2,4},{3,35},{4,6},{5,37},{6,0},{7,39},{8,10},{9,41},... | collective-permute-start | bytes 2359304 | tf_op jit(solution)/shard_map/ppermute | solution.py:214
  33.0 12.4 %collective-permute-start.7 = (f32[128,1536]{1,0:T(8,128)S(1)}, f32[128,1536]{1,0:T(8,128)S(1)}, u32[]{:S(2)}, u32[]{:S(2)}) collective-permute-start(f32[128,1536]{1,0:T(8,128)S(1)} %collective-permute-done.4.refs_4_), channel_id=1, source_target_pairs={{0,6},{1,97},{2,0},{3,99},{4,2},{5,101},{6,4},{7,103},{8,14},{9,10... | collective-permute-start | bytes 2359304 | tf_op jit(solution)/shard_map/ppermute | solution.py:214
  35.5 4.8 %collective-permute-start.14 = (f32[64,1536]{1,0:T(8,128)S(1)}, f32[64,1536]{1,0:T(8,128)S(1)}, u32[]{:S(2)}, u32[]{:S(2)}) collective-permute-start(f32[64,1536]{1,0:T(8,128)S(1)} %collective-permute-done.5.refs_5_), channel_id=1, source_target_pairs={{0,1},{1,0},{2,3},{3,2},{4,5},{5,4},{6,7},{7,6},{8,9},{9,8},{10,11... | collective-permute-start | bytes 1179656 | tf_op jit(solution)/shard_map/ppermute | solution.py:28
  40.3 5.6 %collective-permute-start.12 = (f32[128,1536]{1,0:T(8,128)S(1)}, f32[128,1536]{1,0:T(8,128)S(1)}, u32[]{:S(2)}, u32[]{:S(2)}) collective-permute-start(f32[128,1536]{1,0:T(8,128)S(1)} %collective-permute-done.3.refs_3_), channel_id=1, source_target_pairs={{0,1},{1,0},{2,3},{3,2},{4,5},{5,4},{6,7},{7,6},{8,9},{9,8},{10,11... | collective-permute-start | bytes 2359304 | tf_op jit(solution)/shard_map/ppermute | solution.py:28
  40.3 9.0 %collective-permute-start.10 = (f32[128,1536]{1,0:T(8,128)S(1)}, f32[128,1536]{1,0:T(8,128)S(1)}, u32[]{:S(2)}, u32[]{:S(2)}) collective-permute-start(f32[128,1536]{1,0:T(8,128)S(1)} %collective-permute-done.1.refs_1_), channel_id=1, source_target_pairs={{0,1},{1,0},{2,3},{3,2},{4,5},{5,4},{6,7},{7,6},{8,9},{9,8},{10,11... | collective-permute-start | bytes 2359304 | tf_op jit(solution)/shard_map/ppermute | solution.py:28
  40.9 5.1 %collective-permute-start.11 = (f32[128,1536]{1,0:T(8,128)S(1)}, f32[128,1536]{1,0:T(8,128)S(1)}, u32[]{:S(2)}, u32[]{:S(2)}) collective-permute-start(f32[128,1536]{1,0:T(8,128)S(1)} %collective-permute-done.2.refs_2_), channel_id=1, source_target_pairs={{0,1},{1,0},{2,3},{3,2},{4,5},{5,4},{6,7},{7,6},{8,9},{9,8},{10,11... | collective-permute-start | bytes 2359304 | tf_op jit(solution)/shard_map/ppermute | solution.py:28
  45.4 4.0 %collective-permute-start.17 = (f32[128,1536]{1,0:T(8,128)S(1)}, f32[128,1536]{1,0:T(8,128)S(1)}, u32[]{:S(2)}, u32[]{:S(2)}) collective-permute-start(f32[128,1536]{1,0:T(8,128)S(1)} %collective-permute-done.8.refs_8_), channel_id=1, source_target_pairs={{0,1},{1,0},{2,3},{3,2},{4,5},{5,4},{6,7},{7,6},{8,9},{9,8},{10,11... | collective-permute-start | bytes 2359304 | tf_op jit(solution)/shard_map/ppermute | solution.py:28
  45.4 4.0 %collective-permute-start.16 = (f32[128,1536]{1,0:T(8,128)S(1)}, f32[128,1536]{1,0:T(8,128)S(1)}, u32[]{:S(2)}, u32[]{:S(2)}) collective-permute-start(f32[128,1536]{1,0:T(8,128)S(1)} %collective-permute-done.7.refs_7_), channel_id=1, source_target_pairs={{0,1},{1,0},{2,3},{3,2},{4,5},{5,4},{6,7},{7,6},{8,9},{9,8},{10,11... | collective-permute-start | bytes 2359304 | tf_op jit(solution)/shard_map/ppermute | solution.py:28
  45.9 3.5 %collective-permute-start.15 = (f32[64,1536]{1,0:T(8,128)S(1)}, f32[64,1536]{1,0:T(8,128)S(1)}, u32[]{:S(2)}, u32[]{:S(2)}) collective-permute-start(f32[64,1536]{1,0:T(8,128)S(1)} %collective-permute-done.6.refs_6_), channel_id=1, source_target_pairs={{0,1},{1,0},{2,3},{3,2},{4,5},{5,4},{6,7},{7,6},{8,9},{9,8},{10,11... | collective-permute-start | bytes 1179656 | tf_op jit(solution)/shard_map/ppermute | solution.py:28
  61.1 3.6 %collective-permute-start.18 = (f32[8,64,512]{2,1,0:T(8,128)S(1)}, f32[8,64,512]{2,1,0:T(8,128)S(1)}, u32[]{:S(2)}, u32[]{:S(2)}) collective-permute-start(f32[8,64,512]{2,1,0:T(8,128)S(1)} %get-tuple-element.19), channel_id=1, source_target_pairs={{0,1},{1,0},{2,3},{3,2},{4,5},{5,4},{6,7},{7,6},{8,9},{9,8},{10,11... | collective-permute-start | bytes 3145736 | tf_op jit(solution)/shard_map/ppermute | solution.py:28
  61.4 10.7 %collective-permute-start.23 = (f32[2,64,512]{2,1,0:T(8,128)S(1)}, f32[2,64,512]{2,1,0:T(8,128)S(1)}, u32[]{:S(2)}, u32[]{:S(2)}) collective-permute-start(f32[2,64,512]{2,1,0:T(8,128)S(1)} %get-tuple-element.24), channel_id=1, source_target_pairs={{0,64},{16,80},{32,96},{48,112},{64,0},{80,16},{96,32},{112,48},{1... | collective-permute-start | bytes 786440 | tf_op jit(solution)/shard_map/ppermute | solution.py:32
  62.7 12.9 %collective-permute-start.24 = (f32[2,64,512]{2,1,0:T(8,128)S(1)}, f32[2,64,512]{2,1,0:T(8,128)S(1)}, u32[]{:S(2)}, u32[]{:S(2)}) collective-permute-start(f32[2,64,512]{2,1,0:T(8,128)S(1)} %get-tuple-element.25), channel_id=1, source_target_pairs={{0,96},{16,112},{32,0},{48,16},{64,32},{80,48},{96,64},{112,80},{1... | collective-permute-start | bytes 786440 | tf_op jit(solution)/shard_map/ppermute | solution.py:32
  64.6 12.4 %collective-permute-start.25 = (f32[2,64,512]{2,1,0:T(8,128)S(1)}, f32[2,64,512]{2,1,0:T(8,128)S(1)}, u32[]{:S(2)}, u32[]{:S(2)}) collective-permute-start(f32[2,64,512]{2,1,0:T(8,128)S(1)} %get-tuple-element.26), channel_id=1, source_target_pairs={{0,32},{16,48},{32,64},{48,80},{64,96},{80,112},{96,0},{112,16},{1... | collective-permute-start | bytes 786440 | tf_op jit(solution)/shard_map/ppermute | solution.py:32
  64.9 14.0 %collective-permute-start.19 = (f32[2,64,512]{2,1,0:T(8,128)S(1)}, f32[2,64,512]{2,1,0:T(8,128)S(1)}, u32[]{:S(2)}, u32[]{:S(2)}) collective-permute-start(f32[2,64,512]{2,1,0:T(8,128)S(1)} %get-tuple-element.27), channel_id=1, source_target_pairs={{0,4},{1,5},{2,6},{3,7},{4,0},{5,1},{6,2},{7,3},{8,12},{9,13},{10,... | collective-permute-start | bytes 786440 | tf_op jit(solution)/shard_map/ppermute | solution.py:28
  67.4 12.6 %collective-permute-start.21 = (f32[2,64,512]{2,1,0:T(8,128)S(1)}, f32[2,64,512]{2,1,0:T(8,128)S(1)}, u32[]{:S(2)}, u32[]{:S(2)}) collective-permute-start(f32[2,64,512]{2,1,0:T(8,128)S(1)} %get-tuple-element.28), channel_id=1, source_target_pairs={{0,2},{1,3},{2,4},{3,5},{4,6},{5,7},{6,0},{7,1},{8,10},{9,11},{10,... | collective-permute-start | bytes 786440 | tf_op jit(solution)/shard_map/ppermute | solution.py:28
  72.0 8.0 %collective-permute-start.20 = (f32[2,64,512]{2,1,0:T(8,128)S(1)}, f32[2,64,512]{2,1,0:T(8,128)S(1)}, u32[]{:S(2)}, u32[]{:S(2)}) collective-permute-start(f32[2,64,512]{2,1,0:T(8,128)S(1)} %get-tuple-element.29), channel_id=1, source_target_pairs={{0,6},{1,7},{2,0},{3,1},{4,2},{5,3},{6,4},{7,5},{8,14},{9,15},{10,... | collective-permute-start | bytes 786440 | tf_op jit(solution)/shard_map/ppermute | solution.py:28
  77.2 7.0 %collective-permute-start.26 = (f32[64,512]{1,0:T(8,128)S(1)}, f32[64,512]{1,0:T(8,128)S(1)}, u32[]{:S(2)}, u32[]{:S(2)}) collective-permute-start(f32[64,512]{1,0:T(8,128)S(1)} %slice_bitcast_fusion), channel_id=1, source_target_pairs={{0,16},{16,0},{32,48},{48,32},{64,80},{80,64},{96,112},{112,96},{1... | collective-permute-start | bytes 393224 | tf_op jit(solution)/shard_map/ppermute | solution.py:32
  80.1 5.7 %collective-permute-start.22 = (f32[64,512]{1,0:T(8,128)S(1)}, f32[64,512]{1,0:T(8,128)S(1)}, u32[]{:S(2)}, u32[]{:S(2)}) collective-permute-start(f32[64,512]{1,0:T(8,128)S(1)} %slice_bitcast_fusion.2), channel_id=1, source_target_pairs={{0,8},{1,9},{2,10},{3,11},{4,12},{5,13},{6,14},{7,15},{8,0},{9,1},... | collective-permute-start | bytes 393224 | tf_op jit(solution)/shard_map/ppermute | solution.py:28
